TPU v7x, 32 devices: a whole 2x2x4 slice. The times are simulated.
32 devices in a mesh: section: 2 (over y), tensor: 4 (over x, core), ctx: 4 (over z).
Axes of the slice: x: 2, y: 2, z: 4, core: 2. Of those that a mesh axis runs over, the one named last changes fastest.
Arguments:
- inputs: bfloat16 [4, 4, 256, 4, 2048], P(None, 'ctx', 'tensor'), may hold values from -6 to 6
- out_grads: bfloat16 [4, 4, 256, 4, 2048], P(None, 'ctx', 'tensor'), may hold values from -6 to 6
- norm1_gain: float32 [2, 2048], P('section'), may hold values from 0.5 to 1.5
- norm1_bias: float32 [2, 2048], P('section'), may hold values from -1.8 to 1.8
- norm2_gain: float32 [2, 2048], P('section'), may hold values from 0.5 to 1.5
- norm2_bias: float32 [2, 2048], P('section'), may hold values from -1.8 to 1.8
- w_qkv: bfloat16 [2, 2048, 8, 768], P('section', None, 'tensor'), may hold values from -0.125 to 0.125
- b_qkv: float32 [2, 8, 768], P('section', 'tensor'), may hold values from -3 to 3
- w_out: bfloat16 [2, 8, 256, 2048], P('section', 'tensor'), may hold values from -0.5 to 0.5
- b_out: float32 [2, 2048], P('section'), may hold values from -1.8 to 1.8
- input_projection: bfloat16 [2, 2048, 8192], P('section', None, 'tensor'), may hold values from -0.125 to 0.125
- input_bias_vector: float32 [2, 8192], P('section', 'tensor'), may hold values from -3 to 3
- down_projection: bfloat16 [2, 8192, 2048], P('section', 'tensor'), may hold values from -0.0625 to 0.0625
- b_down: float32 [2, 2048], P('section'), may hold values from -1.8 to 1.8
Outputs:
- states: bfloat16 [2, 4, 4, 256, 4, 2048], P('section', None, 'ctx', 'tensor')
- input_grads: float32 [2, 4, 4, 256, 4, 2048], P('section', None, 'ctx', 'tensor')
- grad_norm1_gain: float32 [2, 2048], P('section')
- grad_norm1_bias: float32 [2, 2048], P('section')
- grad_norm2_gain: float32 [2, 2048], P('section')
- grad_norm2_bias: float32 [2, 2048], P('section')
- grad_w_qkv: float32 [2, 2048, 8, 768], P('section', None, 'tensor')
- grad_b_qkv: float32 [2, 8, 768], P('section', 'tensor')
- grad_w_out: float32 [2, 8, 256, 2048], P('section', 'tensor')
- grad_b_out: float32 [2, 2048], P('section')
- grad_w_in: float32 [2, 2048, 8192], P('section', None, 'tensor')
- grad_b_in: float32 [2, 8192], P('section', 'tensor')
- grad_w_down: float32 [2, 8192, 2048], P('section', 'tensor')
- grad_b_down: float32 [2, 2048], P('section')
All inputs are finite; a program needn't handle non-finite values.
Results may differ from a plain program's by a relative error of at most 0.013.
Values may be sent and summed in bfloat16 or wider, within the bound.
A program may use at most 768 MiB of HBM per device.

v0:
```python
from functools import partial

import jax
import jax.numpy as jnp
from jax import lax
from jax.sharding import PartitionSpec as P

ROT = 64


epsilon = 1e-05
masked_score = -1e30


def from_behind(value, axis, steps):
    count = lax.axis_size(axis)
    initial, last = (max(0, -steps), min(count, count - steps))
    return lax.ppermute(value, axis, [(source, source + steps) for source in range(initial, last)])


def shortened(x):
    return jax.tree.map(lambda a: a.astype(jnp.bfloat16) if a.dtype == jnp.float32 else a, x)


def standardize(values):
    average = jnp.mean(values, axis=-1, keepdims=True)
    centred = values - average
    inverse = lax.rsqrt(jnp.mean(centred * centred, axis=-1, keepdims=True) + epsilon)
    return (centred * inverse, inverse)


def norm_back(grad_out, standard, inverse, gain):
    scaled = grad_out * gain
    spread = jnp.mean(scaled * standard, axis=-1, keepdims=True)
    return inverse * (scaled - jnp.mean(scaled, axis=-1, keepdims=True) - standard * spread)


def angle_tables(offset, row_total):
    frequency = 1.0 / 10000.0 ** (jnp.arange(0, ROT, 2, dtype=jnp.float32) / ROT)
    places = (offset + jnp.arange(row_total, dtype=jnp.int32)).astype(jnp.float32)
    angles = places[:, None] * frequency[None, :]
    angles = jnp.concatenate([angles, angles], axis=-1)[:, None, None, :]
    return (jnp.cos(angles), jnp.sin(angles))


def rotate(values, cosine, sine_table):
    half_rot = ROT // 2
    leading = values[..., :ROT]
    turned = jnp.concatenate([-leading[..., half_rot:], leading[..., :half_rot]], axis=-1)
    return jnp.concatenate([leading * cosine + turned * sine_table, values[..., ROT:]], axis=-1)


def rotate_back(grad_in, cosine, sine_table):
    half_rot = ROT // 2
    leading = grad_in[..., :ROT]
    lifted = leading * sine_table
    turned = jnp.concatenate([lifted[..., half_rot:], -lifted[..., :half_rot]], axis=-1)
    return jnp.concatenate([leading * cosine + turned, grad_in[..., ROT:]], axis=-1)


def block_forward(row_block, weights, cosine, sine_table, offset):
    (
        gain_one,
        bias_one,
        gain_two,
        bias_two,
        w_qkv,
        b_qkv,
        w_out,
        b_out,
        input_projection,
        input_bias_vector,
        down_projection,
        b_down,
    ) = weights
    standard, inverse = standardize(row_block.astype(jnp.float32))
    local_one = (standard * gain_one + bias_one).astype(jnp.bfloat16)
    local_two = (standard * gain_two + bias_two).astype(jnp.bfloat16)
    normed_one, second_normed = (
        lax.all_gather(local_one, "tensor", axis=0, tiled=True),
        lax.all_gather(local_two, "tensor", axis=0, tiled=True),
    )
    head_size = w_qkv.shape[-1] // 3
    projected = (
        jnp.einsum("csd,dhe->cshe", normed_one, w_qkv, preferred_element_type=jnp.float32) + b_qkv
    )
    query_low = rotate(projected[..., :head_size], cosine, sine_table).astype(jnp.bfloat16)
    key_low = rotate(projected[..., head_size : 2 * head_size], cosine, sine_table).astype(
        jnp.bfloat16
    )
    value_low = projected[..., 2 * head_size :].astype(jnp.bfloat16)
    keys_whole, values_whole = (
        lax.all_gather(key_low, "ctx", axis=0, tiled=True),
        lax.all_gather(value_low, "ctx", axis=0, tiled=True),
    )
    scores = jnp.einsum(
        "cshe,kshe->shck", query_low, keys_whole, preferred_element_type=jnp.float32
    ) * head_size ** (-0.5)
    query_place = offset + jnp.arange(query_low.shape[0], dtype=jnp.int32)
    key_place = jnp.arange(keys_whole.shape[0], dtype=jnp.int32)
    allowed = key_place[None, :] <= query_place[:, None]
    scores = jnp.where(allowed, scores, masked_score)
    row_peak = jnp.max(scores, axis=-1, keepdims=True)
    logsum = row_peak + jnp.log(jnp.sum(jnp.exp(scores - row_peak), axis=-1, keepdims=True))
    chance = jnp.exp(scores - logsum)
    chance_low = chance.astype(jnp.bfloat16)
    context = jnp.einsum(
        "shck,kshe->cshe", chance_low, values_whole, preferred_element_type=jnp.float32
    ).astype(jnp.bfloat16)
    hidden_state = (
        jnp.einsum(
            "csd,df->csf", second_normed, input_projection, preferred_element_type=jnp.float32
        )
        + input_bias_vector
    )
    active_units = jax.nn.gelu(hidden_state, approximate=False).astype(jnp.bfloat16)
    return (
        standard,
        inverse,
        normed_one,
        second_normed,
        query_low,
        keys_whole,
        values_whole,
        chance,
        chance_low,
        context,
        hidden_state,
        active_units,
    )


def make_branch(context, active_units, w_out, down_projection):

    def branch_rows(first_row, row_total):
        attention = jnp.einsum("cshe,hed->csd", context, w_out, preferred_element_type=jnp.float32)
        return attention + jnp.einsum(
            "csf,fd->csd", active_units, down_projection, preferred_element_type=jnp.float32
        )

    return branch_rows


def body(
    inputs,
    out_grads,
    norm1_gain,
    norm1_bias,
    norm2_gain,
    norm2_bias,
    w_qkv,
    b_qkv,
    w_out,
    b_out,
    input_projection,
    input_bias_vector,
    down_projection,
    b_down,
):
    weights = tuple(
        (
            argument[0]
            for argument in (
                norm1_gain,
                norm1_bias,
                norm2_gain,
                norm2_bias,
                w_qkv,
                b_qkv,
                w_out,
                b_out,
                input_projection,
                input_bias_vector,
                down_projection,
                b_down,
            )
        )
    )
    (
        gain_one,
        bias_one,
        gain_two,
        bias_two,
        qkv_weight,
        qkv_bias,
        out_weight,
        out_bias,
        in_weight,
        in_bias,
        down_weight,
        down_bias,
    ) = weights
    micro_count = inputs.shape[0]
    row_count = inputs.shape[2]
    group_rows = row_count * lax.axis_size("tensor")
    offset = lax.axis_index("ctx") * group_rows
    cosine, sine_table = angle_tables(offset, group_rows)
    first_section = lax.axis_index("section") == 0
    head_size = qkv_weight.shape[-1] // 3
    scale = head_size ** (-0.5)
    arrived = jnp.zeros(inputs.shape[2:], jnp.bfloat16)
    kept_inputs = []
    produced = []
    for moment in range(micro_count + 1):
        row_block = jnp.where(first_section, inputs[min(moment, micro_count - 1), 0], arrived)
        kept_inputs.append(row_block)
        forward_parts = block_forward(row_block, weights, cosine, sine_table, offset)
        branch_rows = make_branch(forward_parts[9], forward_parts[11], out_weight, down_weight)
        summed = lax.psum_scatter(
            branch_rows(jnp.int32(0), row_count * lax.axis_size("tensor")),
            "tensor",
            scatter_dimension=0,
            tiled=True,
        )
        result = (row_block.astype(jnp.float32) + summed + out_bias + down_bias).astype(
            jnp.bfloat16
        )
        produced.append(result)
        if moment < micro_count:
            arrived = from_behind(result, "section", 1)
    big_totals = [
        jnp.zeros(qkv_weight.shape, jnp.float32),
        jnp.zeros(qkv_bias.shape, jnp.float32),
        jnp.zeros(out_weight.shape, jnp.float32),
        jnp.zeros(in_weight.shape, jnp.float32),
        jnp.zeros(in_bias.shape, jnp.float32),
        jnp.zeros(down_weight.shape, jnp.float32),
    ]
    small_totals = [jnp.zeros(gain_one.shape, jnp.float32) for counter in range(5)]
    arrived = jnp.zeros(inputs.shape[2:], jnp.bfloat16)
    back_list = []
    gelu_exact = partial(jax.nn.gelu, approximate=False)
    for moment in range(micro_count + 1):
        row_block = jnp.where(
            first_section,
            kept_inputs[max(moment - 1, 0)],
            kept_inputs[min(moment + 1, micro_count)],
        )
        cotangent = jnp.where(first_section, arrived, out_grads[min(moment, micro_count - 1), 0])
        weight_valid = jnp.where(
            first_section, 1.0 if moment >= 1 else 0.0, 1.0 if moment < micro_count else 0.0
        )
        (
            standard,
            inverse,
            normed_one,
            second_normed,
            query_low,
            keys_whole,
            values_whole,
            chance,
            chance_low,
            context,
            hidden_state,
            active_units,
        ) = block_forward(row_block, weights, cosine, sine_table, offset)
        grads_whole = lax.all_gather(cotangent, "tensor", axis=0, tiled=True)
        d_w_down = jnp.einsum(
            "csf,csd->fd", active_units, grads_whole, preferred_element_type=jnp.float32
        )
        d_active = jnp.einsum(
            "csd,fd->csf", grads_whole, down_weight, preferred_element_type=jnp.float32
        )
        gelu_value, gelu_pull = jax.vjp(gelu_exact, hidden_state)
        d_hidden = gelu_pull(d_active)[0].astype(jnp.bfloat16)
        d_w_in = jnp.einsum(
            "csd,csf->df", second_normed, d_hidden, preferred_element_type=jnp.float32
        )
        d_b_in = jnp.sum(d_hidden, axis=(0, 1), dtype=jnp.float32)
        d_two = jnp.einsum("csf,df->csd", d_hidden, in_weight, preferred_element_type=jnp.float32)
        d_w_out = jnp.einsum(
            "cshe,csd->hed", context, grads_whole, preferred_element_type=jnp.float32
        )
        d_context = jnp.einsum(
            "csd,hed->cshe", grads_whole, out_weight, preferred_element_type=jnp.float32
        ).astype(jnp.bfloat16)
        d_chance = jnp.einsum(
            "cshe,kshe->shck", d_context, values_whole, preferred_element_type=jnp.float32
        )
        d_value = jnp.einsum(
            "shck,cshe->kshe", chance_low, d_context, preferred_element_type=jnp.float32
        )
        d_scores = (
            chance * (d_chance - jnp.sum(d_chance * chance, axis=-1, keepdims=True))
        ).astype(jnp.bfloat16)
        d_query = (
            jnp.einsum("shck,kshe->cshe", d_scores, keys_whole, preferred_element_type=jnp.float32)
            * scale
        )
        d_key = (
            jnp.einsum("shck,cshe->kshe", d_scores, query_low, preferred_element_type=jnp.float32)
            * scale
        )
        key_own, value_own = (
            lax.psum_scatter(d_key, "ctx", scatter_dimension=0, tiled=True),
            lax.psum_scatter(d_value, "ctx", scatter_dimension=0, tiled=True),
        )
        d_projected = jnp.concatenate(
            [
                rotate_back(d_query, cosine, sine_table),
                rotate_back(key_own, cosine, sine_table),
                value_own,
            ],
            axis=-1,
        ).astype(jnp.bfloat16)
        d_w_qkv = jnp.einsum(
            "csd,cshe->dhe", normed_one, d_projected, preferred_element_type=jnp.float32
        )
        d_b_qkv = jnp.sum(d_projected, axis=(0, 1), dtype=jnp.float32)
        d_one = jnp.einsum(
            "cshe,dhe->csd", d_projected, qkv_weight, preferred_element_type=jnp.float32
        )
        own_one, own_two = (
            lax.psum_scatter(d_one, "tensor", scatter_dimension=0, tiled=True),
            lax.psum_scatter(d_two, "tensor", scatter_dimension=0, tiled=True),
        )
        vector_terms = [
            jnp.sum(own_one * standard, axis=(0, 1)),
            jnp.sum(own_one, axis=(0, 1)),
            jnp.sum(own_two * standard, axis=(0, 1)),
            jnp.sum(own_two, axis=(0, 1)),
        ]
        d_input = (
            cotangent.astype(jnp.float32)
            + norm_back(own_one, standard, inverse, gain_one)
            + norm_back(own_two, standard, inverse, gain_two)
        )
        vector_terms.append(jnp.sum(cotangent, axis=(0, 1), dtype=jnp.float32))
        new_terms = [d_w_qkv, d_b_qkv, d_w_out, d_w_in, d_b_in, d_w_down]
        big_totals = [total + weight_valid * term for total, term in zip(big_totals, new_terms)]
        small_totals = [
            total + weight_valid * term for total, term in zip(small_totals, vector_terms)
        ]
        back_list.append(d_input)
        if moment < micro_count:
            arrived = from_behind(d_input.astype(jnp.bfloat16), "section", -1)
    big_sums = jax.tree.map(
        lambda part: part.astype(jnp.float32), lax.psum(shortened(tuple(big_totals)), "ctx")
    )
    vector_sums = lax.psum(tuple(small_totals), ("tensor", "ctx"))
    states = jnp.stack(
        [
            jnp.where(first_section, produced[batch_index], produced[batch_index + 1])
            for batch_index in range(micro_count)
        ]
    )[None, :, None]
    input_grads = jnp.stack(
        [
            jnp.where(first_section, back_list[batch_index + 1], back_list[batch_index])
            for batch_index in range(micro_count)
        ]
    )[None, :, None]
    return (
        states,
        input_grads,
        vector_sums[0][None],
        vector_sums[1][None],
        vector_sums[2][None],
        vector_sums[3][None],
        big_sums[0][None],
        big_sums[1][None],
        big_sums[2][None],
        vector_sums[4][None],
        big_sums[3][None],
        big_sums[4][None],
        big_sums[5][None],
        vector_sums[4][None],
    )


def solution(mesh):
    return jax.shard_map(
        body,
        mesh=mesh,
        in_specs=(
            P(None, "ctx", "tensor", None, None),
            P(None, "ctx", "tensor", None, None),
            P("section", None),
            P("section", None),
            P("section", None),
            P("section", None),
            P("section", None, "tensor", None),
            P("section", "tensor", None),
            P("section", "tensor", None, None),
            P("section", None),
            P("section", None, "tensor"),
            P("section", "tensor"),
            P("section", "tensor", None),
            P("section", None),
        ),
        out_specs=(
            P("section", None, "ctx", "tensor", None, None),
            P("section", None, "ctx", "tensor", None, None),
            P("section", None),
            P("section", None),
            P("section", None),
            P("section", None),
            P("section", None, "tensor", None),
            P("section", "tensor", None),
            P("section", "tensor", None, None),
            P("section", None),
            P("section", None, "tensor"),
            P("section", "tensor"),
            P("section", "tensor", None),
            P("section", None),
        ),
        check_vma=False,
    )
```

profile of v0, /device:TPU:0, one launch (start us, length us, event | category | flops | bytes accessed | tf_op | source)
XLA Modules:
  0.0 6508.5 jit_solution(14030166036694617952)
XLA Ops:
  17.4 35.8 all-gather.47.cloned.1.call-done
  107.5 64.7 all-gather.51.cloned.1.call-done
  181.5 71.5 %all-gather.49.cloned.1.call-done = bf16[1024,4,2,256]{3,0,2,1:T(8,128)(2,1)} async-done(((bf16[256,4,2,256]{3,0,2,1:T(8,128)(2,1)}), bf16[1024,4,2,256]{3,0,2,1:T(8,128)(2,1)}) %all-gather.49.cloned.1.call-update) | async-done | bytes 4194320 | tf_op jit(solution)/shard_map/all_gather | solution.py:94
  262.5 33.7 bitcast_add_fusion.13
  296.4 70.3 %reduce-scatter.26.cloned.1.call-done = f32[64,4,2048]{2,0,1:T(8,128)} async-done(((f32[256,4,2048]{2,0,1:T(8,128)}), f32[64,4,2048]{2,0,1:T(8,128)}) %reduce-scatter.26.cloned.1.call-update) | async-done | bytes 2097168 | tf_op jit(solution)/shard_map/reduce_scatter | solution.py:209
  404.3 34.9 all-gather.55.cloned.1.call-done
  494.0 64.3 all-gather.59.cloned.1.call-done
  567.6 72.3 %all-gather.57.cloned.1.call-done = bf16[1024,4,2,256]{3,0,2,1:T(8,128)(2,1)} async-done(((bf16[256,4,2,256]{3,0,2,1:T(8,128)(2,1)}), bf16[1024,4,2,256]{3,0,2,1:T(8,128)(2,1)}) %all-gather.57.cloned.1.call-update) | async-done | bytes 4194320 | tf_op jit(solution)/shard_map/all_gather | solution.py:94
  649.4 33.7 bitcast_add_fusion.12
  683.3 70.3 %reduce-scatter.28.cloned.1.call-done = f32[64,4,2048]{2,0,1:T(8,128)} async-done(((f32[256,4,2048]{2,0,1:T(8,128)}), f32[64,4,2048]{2,0,1:T(8,128)}) %reduce-scatter.28.cloned.1.call-update) | async-done | bytes 2097168 | tf_op jit(solution)/shard_map/reduce_scatter | solution.py:209
  792.5 34.3 all-gather.63.cloned.1.call-done
  917.8 64.9 all-gather.67.cloned.1.call-done
  992.0 72.0 %all-gather.65.cloned.1.call-done = bf16[1024,4,2,256]{3,0,2,1:T(8,128)(2,1)} async-done(((bf16[256,4,2,256]{3,0,2,1:T(8,128)(2,1)}), bf16[1024,4,2,256]{3,0,2,1:T(8,128)(2,1)}) %all-gather.65.cloned.1.call-update) | async-done | bytes 4194320 | tf_op jit(solution)/shard_map/all_gather | solution.py:94
  1073.6 33.7 bitcast_add_fusion.11
  1107.5 70.3 %reduce-scatter.30.cloned.1.call-done = f32[64,4,2048]{2,0,1:T(8,128)} async-done(((f32[256,4,2048]{2,0,1:T(8,128)}), f32[64,4,2048]{2,0,1:T(8,128)}) %reduce-scatter.30.cloned.1.call-update) | async-done | bytes 2097168 | tf_op jit(solution)/shard_map/reduce_scatter | solution.py:209
  1215.3 34.0 all-gather.71.cloned.1.call-done
  1340.7 64.8 all-gather.75.cloned.1.call-done
  1414.7 72.3 %all-gather.73.cloned.1.call-done = bf16[1024,4,2,256]{3,0,2,1:T(8,128)(2,1)} async-done(((bf16[256,4,2,256]{3,0,2,1:T(8,128)(2,1)}), bf16[1024,4,2,256]{3,0,2,1:T(8,128)(2,1)}) %all-gather.73.cloned.1.call-update) | async-done | bytes 4194320 | tf_op jit(solution)/shard_map/all_gather | solution.py:94
  1496.5 33.5 bitcast_add_fusion.10
  1530.2 70.3 %reduce-scatter.32.cloned.1.call-done = f32[64,4,2048]{2,0,1:T(8,128)} async-done(((f32[256,4,2048]{2,0,1:T(8,128)}), f32[64,4,2048]{2,0,1:T(8,128)}) %reduce-scatter.32.cloned.1.call-update) | async-done | bytes 2097168 | tf_op jit(solution)/shard_map/reduce_scatter | solution.py:209
  1827.4 76.9 %all-gather.97.cloned.1.call-done = bf16[1024,4,2,256]{3,0,2,1:T(8,128)(2,1)} async-done(((bf16[256,4,2,256]{3,0,2,1:T(8,128)(2,1)}), bf16[1024,4,2,256]{3,0,2,1:T(8,128)(2,1)}) %all-gather.97.cloned.1.call-update) | async-done | bytes 4194320 | tf_op jit(solution)/shard_map/all_gather | solution.py:93
  1911.7 73.5 %all-gather.107.cloned.1.call-done = bf16[1024,4,2,256]{3,0,2,1:T(8,128)(2,1)} async-done(((bf16[256,4,2,256]{3,0,2,1:T(8,128)(2,1)}), bf16[1024,4,2,256]{3,0,2,1:T(8,128)(2,1)}) %all-gather.107.cloned.1.call-update) | async-done | bytes 4194320 | tf_op jit(solution)/shard_map/all_gather | solution.py:93
  1992.7 73.8 %all-gather.127.cloned.1.call-done = bf16[1024,4,2,256]{3,0,2,1:T(8,128)(2,1)} async-done(((bf16[256,4,2,256]{3,0,2,1:T(8,128)(2,1)}), bf16[1024,4,2,256]{3,0,2,1:T(8,128)(2,1)}) %all-gather.127.cloned.1.call-update) | async-done | bytes 4194320 | tf_op jit(solution)/shard_map/all_gather | solution.py:93
  2074.3 73.7 %all-gather.117.cloned.1.call-done = bf16[1024,4,2,256]{3,0,2,1:T(8,128)(2,1)} async-done(((bf16[256,4,2,256]{3,0,2,1:T(8,128)(2,1)}), bf16[1024,4,2,256]{3,0,2,1:T(8,128)(2,1)}) %all-gather.117.cloned.1.call-update) | async-done | bytes 4194320 | tf_op jit(solution)/shard_map/all_gather | solution.py:93
  2155.1 73.8 %all-gather.89.cloned.1.call-done = bf16[1024,4,2,256]{3,0,2,1:T(8,128)(2,1)} async-done(((bf16[256,4,2,256]{3,0,2,1:T(8,128)(2,1)}), bf16[1024,4,2,256]{3,0,2,1:T(8,128)(2,1)}) %all-gather.89.cloned.1.call-update) | async-done | bytes 4194320 | tf_op jit(solution)/shard_map/all_gather | solution.py:93
  2255.7 54.0 all-gather.91.cloned.1.call-done
  2524.2 47.1 fusion.738
  2579.5 78.7 %fusion.24 = (f32[256,4,2048]{2,0,1:T(8,128)}, f32[256,4,2048]{2,0,1:T(8,128)}, f32[256,4,2048]{2,0,1:T(8,128)}, f32[256,4,2048]{2,0,1:T(8,128)}) fusion(f32[256,4,2048]{2,0,1:T(8,128)} %fusion.52, f32[2048]{0:T(1024)S(1)} %bitcast.949, u8[256,2048]{1,0:T(8,128)(4,1)S(1)} %copy-done.141, u8[256,2048]{1,0:T(8,128)(4,1)S(1)} %copy-done.142, ...), kind=kLoop, calls=%fused_computation.49 | loop fusion | flops 564133888 | bytes 71311360 | tf_op jit(solution)/shard_map/jvp()/erfc | solution.py:264
  2717.6 101.0 %reduce-scatter.38.cloned.1.call-done = f32[256,4,2,256]{0,3,2,1:T(8,128)} async-done(((f32[1024,4,2,256]{0,3,2,1:T(8,128)}), f32[256,4,2,256]{0,3,2,1:T(8,128)}) %reduce-scatter.38.cloned.1.call-update) | async-done | bytes 2097168 | tf_op jit(solution)/shard_map/reduce_scatter | solution.py:296
  2834.0 59.7 reduce-scatter.42.cloned.1.call-done
  2893.7 74.3 %reduce-scatter.40.cloned.1.call-done = f32[64,4,2048]{2,0,1:T(8,128)} async-done(((f32[256,4,2048]{2,0,1:T(8,128)}), f32[64,4,2048]{2,0,1:T(8,128)}) %reduce-scatter.40.cloned.1.call-update) | async-done | bytes 2097168 | tf_op jit(solution)/shard_map/reduce_scatter | solution.py:314
  2979.5 25.1 collective-permute-done.4
  3009.4 31.3 all-gather.99.cloned.1.call-done
  3046.2 77.3 %all-gather.101.cloned.1.call-done = bf16[1024,4,2,256]{3,0,2,1:T(8,128)(2,1)} async-done(((bf16[256,4,2,256]{3,0,2,1:T(8,128)(2,1)}), bf16[1024,4,2,256]{3,0,2,1:T(8,128)(2,1)}) %all-gather.101.cloned.1.call-update) | async-done | bytes 4194320 | tf_op jit(solution)/shard_map/all_gather | solution.py:94
  3196.7 90.4 %reduce-scatter.44.cloned.1.call-done = f32[256,4,2,256]{3,0,2,1:T(8,128)} async-done(((f32[1024,4,2,256]{3,0,2,1:T(8,128)}), f32[256,4,2,256]{3,0,2,1:T(8,128)}) %reduce-scatter.44.cloned.1.call-update) | async-done | bytes 2097168 | tf_op jit(solution)/shard_map/reduce_scatter | solution.py:295
  3306.7 127.8 %reduce-scatter.46.cloned.1.call-done = f32[256,4,2,256]{0,3,2,1:T(8,128)} async-done(((f32[1024,4,2,256]{0,3,2,1:T(8,128)}), f32[256,4,2,256]{0,3,2,1:T(8,128)}) %reduce-scatter.46.cloned.1.call-update) | async-done | bytes 2097168 | tf_op jit(solution)/shard_map/reduce_scatter | solution.py:296
  3449.8 59.7 reduce-scatter.50.cloned.1.call-done
  3509.5 75.0 %reduce-scatter.48.cloned.1.call-done = f32[64,4,2048]{2,0,1:T(8,128)} async-done(((f32[256,4,2048]{2,0,1:T(8,128)}), f32[64,4,2048]{2,0,1:T(8,128)}) %reduce-scatter.48.cloned.1.call-update) | async-done | bytes 2097168 | tf_op jit(solution)/shard_map/reduce_scatter | solution.py:314
  3597.5 25.1 collective-permute-done.5
  3628.7 30.0 all-gather.109.cloned.1.call-done
  3663.3 78.2 %all-gather.111.cloned.1.call-done = bf16[1024,4,2,256]{3,0,2,1:T(8,128)(2,1)} async-done(((bf16[256,4,2,256]{3,0,2,1:T(8,128)(2,1)}), bf16[1024,4,2,256]{3,0,2,1:T(8,128)(2,1)}) %all-gather.111.cloned.1.call-update) | async-done | bytes 4194320 | tf_op jit(solution)/shard_map/all_gather | solution.py:94
  3814.9 89.3 %reduce-scatter.52.cloned.1.call-done = f32[256,4,2,256]{3,0,2,1:T(8,128)} async-done(((f32[1024,4,2,256]{3,0,2,1:T(8,128)}), f32[256,4,2,256]{3,0,2,1:T(8,128)}) %reduce-scatter.52.cloned.1.call-update) | async-done | bytes 2097168 | tf_op jit(solution)/shard_map/reduce_scatter | solution.py:295
  3923.6 128.6 %reduce-scatter.54.cloned.1.call-done = f32[256,4,2,256]{0,3,2,1:T(8,128)} async-done(((f32[1024,4,2,256]{0,3,2,1:T(8,128)}), f32[256,4,2,256]{0,3,2,1:T(8,128)}) %reduce-scatter.54.cloned.1.call-update) | async-done | bytes 2097168 | tf_op jit(solution)/shard_map/reduce_scatter | solution.py:296
  4067.5 59.8 reduce-scatter.58.cloned.1.call-done
  4127.3 75.1 %reduce-scatter.56.cloned.1.call-done = f32[64,4,2048]{2,0,1:T(8,128)} async-done(((f32[256,4,2048]{2,0,1:T(8,128)}), f32[64,4,2048]{2,0,1:T(8,128)}) %reduce-scatter.56.cloned.1.call-update) | async-done | bytes 2097168 | tf_op jit(solution)/shard_map/reduce_scatter | solution.py:314
  4215.2 25.1 collective-permute-done.6
  4246.4 30.0 all-gather.119.cloned.1.call-done
  4281.0 78.4 %all-gather.121.cloned.1.call-done = bf16[1024,4,2,256]{3,0,2,1:T(8,128)(2,1)} async-done(((bf16[256,4,2,256]{3,0,2,1:T(8,128)(2,1)}), bf16[1024,4,2,256]{3,0,2,1:T(8,128)(2,1)}) %all-gather.121.cloned.1.call-update) | async-done | bytes 4194320 | tf_op jit(solution)/shard_map/all_gather | solution.py:94
  4432.5 89.4 %reduce-scatter.60.cloned.1.call-done = f32[256,4,2,256]{3,0,2,1:T(8,128)} async-done(((f32[1024,4,2,256]{3,0,2,1:T(8,128)}), f32[256,4,2,256]{3,0,2,1:T(8,128)}) %reduce-scatter.60.cloned.1.call-update) | async-done | bytes 2097168 | tf_op jit(solution)/shard_map/reduce_scatter | solution.py:295
  4541.4 128.6 %reduce-scatter.62.cloned.1.call-done = f32[256,4,2,256]{0,3,2,1:T(8,128)} async-done(((f32[1024,4,2,256]{0,3,2,1:T(8,128)}), f32[256,4,2,256]{0,3,2,1:T(8,128)}) %reduce-scatter.62.cloned.1.call-update) | async-done | bytes 2097168 | tf_op jit(solution)/shard_map/reduce_scatter | solution.py:296
  4692.7 52.9 reduce-scatter.66.cloned.1.call-done
  4745.6 75.1 %reduce-scatter.64.cloned.1.call-done = f32[64,4,2048]{2,0,1:T(8,128)} async-done(((f32[256,4,2048]{2,0,1:T(8,128)}), f32[64,4,2048]{2,0,1:T(8,128)}) %reduce-scatter.64.cloned.1.call-update) | async-done | bytes 2097168 | tf_op jit(solution)/shard_map/reduce_scatter | solution.py:314
  4833.3 25.5 collective-permute-done.7
  4866.3 36.8 all-gather.83.cloned.1.call-done
  4910.2 27.3 all-gather.129.cloned.1.call-done
  4942.1 77.7 %all-gather.131.cloned.1.call-done = bf16[1024,4,2,256]{3,0,2,1:T(8,128)(2,1)} async-done(((bf16[256,4,2,256]{3,0,2,1:T(8,128)(2,1)}), bf16[1024,4,2,256]{3,0,2,1:T(8,128)(2,1)}) %all-gather.131.cloned.1.call-update) | async-done | bytes 4194320 | tf_op jit(solution)/shard_map/all_gather | solution.py:94
  5120.9 33.8 bitcast_add_fusion.9
  5227.0 32.9 convert_reduce_fusion
  5413.1 33.1 fusion.131
  5446.2 42.5 fusion.132
  5488.7 25.2 fusion.153
  5555.0 63.2 reduce-scatter.72.cloned.1.call-done
  5643.0 84.5 %all-reduce = (f32[1,2048]{1,0:T(1,128)}, f32[1,2048]{1,0:T(1,128)}, f32[1,2048]{1,0:T(1,128)}, f32[1,2048]{1,0:T(1,128)}, f32[1,2048]{1,0:T(1,128)S(1)}) all-reduce(f32[1,2048]{1,0:T(1,128)S(1)} %bitcast.926, f32[1,2048]{1,0:T(1,128)S(1)} %bitcast.927, ...), channel_id=1, replica_groups=mesh['section'=2,'tensor'=4,'ctx'=4] {'tensor','ctx'}, use_global_device_ids=true, to_apply=%region_95.96 | all-reduce | flops 10240 | bytes 81920 | tf_op jit(solution)/shard_map/psum | solution.py:340
  5727.5 733.8 %all-reduce.5.cloned.1.call-done = (bf16[1,2048,2,768]{3,1,2,0:T(8,128)(2,1)}, bf16[1,2,256,2048]{3,2,1,0:T(8,128)(2,1)}, bf16[1,2048,2048]{2,1,0:T(8,128)(2,1)}, bf16[1,2048,2048]{2,1,0:T(8,128)(2,1)}) async-done(((bf16[1,2048,2,768]{3,1,2,0:T(8,128)(2,1)}, bf16[1,2,256,2048]{3,2,1,0:T(8,128)(2,1)}, bf16[1,2048,2048]{2,1,0:T(8,128)(2,1)}, bf16[1,2048,2048]{2,1,0:T(8,128)(2,1)}), ...) | async-done | bytes 25165840 | tf_op jit(solution)/shard_map/psum | solution.py:338
  (1042 shorter events, 1933.8 us)
Async XLA Ops:
  16.6 155.6 %all-gather.51.cloned.1.call-start = ((), (), s32[]{:S(2)}) async-start(), calls=%async_computation.27 | async-start | bytes 5242880 | tf_op jit(solution)/shard_map/all_gather | solution.py:93
  68.6 184.4 %all-gather.49.cloned.1.call-start = ((), (), s32[]{:S(2)}) async-start(), calls=%async_computation.26 | async-start | bytes 5242880 | tf_op jit(solution)/shard_map/all_gather | solution.py:94
  70.9 295.8 %reduce-scatter.26.cloned.1.call-start = ((), (), s32[]{:S(2)}) async-start(), calls=%async_computation.29 | async-start | bytes 10485760 | tf_op jit(solution)/shard_map/reduce_scatter | solution.py:209
  296.4 142.8 %all-gather.55.cloned.1.call-start = ((), (), s32[]{:S(2)}) async-start(), calls=%async_computation.30 | async-start | bytes 5242880 | tf_op jit(solution)/shard_map/all_gather | solution.py:80
  404.2 154.1 %all-gather.59.cloned.1.call-start = ((), (), s32[]{:S(2)}) async-start(), calls=%async_computation.32 | async-start | bytes 5242880 | tf_op jit(solution)/shard_map/all_gather | solution.py:93
  455.0 184.8 %all-gather.57.cloned.1.call-start = ((), (), s32[]{:S(2)}) async-start(), calls=%async_computation.31 | async-start | bytes 5242880 | tf_op jit(solution)/shard_map/all_gather | solution.py:94
  457.4 296.2 %reduce-scatter.28.cloned.1.call-start = ((), (), s32[]{:S(2)}) async-start(), calls=%async_computation.34 | async-start | bytes 10485760 | tf_op jit(solution)/shard_map/reduce_scatter | solution.py:209
  683.2 143.5 %all-gather.63.cloned.1.call-start = ((), (), s32[]{:S(2)}) async-start(), calls=%async_computation.35 | async-start | bytes 5242880 | tf_op jit(solution)/shard_map/all_gather | solution.py:80
  791.7 108.2 %all-gather.69.cloned.1.call-start = ((), (), s32[]{:S(2)}) async-start(), calls=%async_computation.38 | async-start | bytes 5242880 | tf_op jit(solution)/shard_map/all_gather | solution.py:81
  792.4 190.3 %all-gather.67.cloned.1.call-start = ((), (), s32[]{:S(2)}) async-start(), calls=%async_computation.37 | async-start | bytes 5242880 | tf_op jit(solution)/shard_map/all_gather | solution.py:93
  882.3 181.7 %all-gather.65.cloned.1.call-start = ((), (), s32[]{:S(2)}) async-start(), calls=%async_computation.36 | async-start | bytes 5242880 | tf_op jit(solution)/shard_map/all_gather | solution.py:94
  884.7 293.1 %reduce-scatter.30.cloned.1.call-start = ((), (), s32[]{:S(2)}) async-start(), calls=%async_computation.39 | async-start | bytes 10485760 | tf_op jit(solution)/shard_map/reduce_scatter | solution.py:209
  1107.4 141.8 %all-gather.71.cloned.1.call-start = ((), (), s32[]{:S(2)}) async-start(), calls=%async_computation.40 | async-start | bytes 5242880 | tf_op jit(solution)/shard_map/all_gather | solution.py:80
  1215.2 190.2 %all-gather.75.cloned.1.call-start = ((), (), s32[]{:S(2)}) async-start(), calls=%async_computation.42 | async-start | bytes 5242880 | tf_op jit(solution)/shard_map/all_gather | solution.py:93
  1304.8 182.1 %all-gather.73.cloned.1.call-start = ((), (), s32[]{:S(2)}) async-start(), calls=%async_computation.41 | async-start | bytes 5242880 | tf_op jit(solution)/shard_map/all_gather | solution.py:94
  1307.2 293.3 %reduce-scatter.32.cloned.1.call-start = ((), (), s32[]{:S(2)}) async-start(), calls=%async_computation.44 | async-start | bytes 10485760 | tf_op jit(solution)/shard_map/reduce_scatter | solution.py:209
  1530.2 146.1 %all-gather.125.cloned.1.call-start = ((), (), s32[]{:S(2)}) async-start(), calls=%async_computation.85 | async-start | bytes 5242880 | tf_op jit(solution)/shard_map/all_gather | solution.py:80
  1641.2 108.2 %all-gather.115.cloned.1.call-start = ((), (), s32[]{:S(2)}) async-start(), calls=%async_computation.76 | async-start | bytes 5242880 | tf_op jit(solution)/shard_map/all_gather | solution.py:80
  1642.0 144.0 %all-gather.87.cloned.1.call-start = ((), (), s32[]{:S(2)}) async-start(), calls=%async_computation.50 | async-start | bytes 5242880 | tf_op jit(solution)/shard_map/all_gather | solution.py:80
  1642.6 179.4 %all-gather.135.cloned.1.call-start = ((), (), s32[]{:S(2)}) async-start(), calls=%async_computation.94 | async-start | bytes 5242880 | tf_op jit(solution)/shard_map/all_gather | solution.py:257
  1649.3 255.0 %all-gather.97.cloned.1.call-start = ((), (), s32[]{:S(2)}) async-start(), calls=%async_computation.59 | async-start | bytes 5242880 | tf_op jit(solution)/shard_map/all_gather | solution.py:93
  1655.4 329.8 %all-gather.107.cloned.1.call-start = ((), (), s32[]{:S(2)}) async-start(), calls=%async_computation.68 | async-start | bytes 5242880 | tf_op jit(solution)/shard_map/all_gather | solution.py:93
  1660.9 405.6 %all-gather.127.cloned.1.call-start = ((), (), s32[]{:S(2)}) async-start(), calls=%async_computation.86 | async-start | bytes 5242880 | tf_op jit(solution)/shard_map/all_gather | solution.py:93
  1731.7 416.3 %all-gather.117.cloned.1.call-start = ((), (), s32[]{:S(2)}) async-start(), calls=%async_computation.77 | async-start | bytes 5242880 | tf_op jit(solution)/shard_map/all_gather | solution.py:93
  1805.0 423.9 %all-gather.89.cloned.1.call-start = ((), (), s32[]{:S(2)}) async-start(), calls=%async_computation.51 | async-start | bytes 5242880 | tf_op jit(solution)/shard_map/all_gather | solution.py:93
  1811.7 498.0 %all-gather.91.cloned.1.call-start = ((), (), s32[]{:S(2)}) async-start(), calls=%async_computation.52 | async-start | bytes 5242880 | tf_op jit(solution)/shard_map/all_gather | solution.py:94
  1814.0 531.4 %all-gather.103.cloned.1.call-start = ((), (), s32[]{:S(2)}) async-start(), calls=%async_computation.65 | async-start | bytes 5242880 | tf_op jit(solution)/shard_map/all_gather | solution.py:81
  1814.7 565.6 %all-gather.113.cloned.1.call-start = ((), (), s32[]{:S(2)}) async-start(), calls=%async_computation.74 | async-start | bytes 5242880 | tf_op jit(solution)/shard_map/all_gather | solution.py:81
  1815.5 600.8 %all-gather.123.cloned.1.call-start = ((), (), s32[]{:S(2)}) async-start(), calls=%async_computation.83 | async-start | bytes 5242880 | tf_op jit(solution)/shard_map/all_gather | solution.py:81
  1816.1 636.1 %all-gather.85.cloned.1.call-start = ((), (), s32[]{:S(2)}) async-start(), calls=%async_computation.48 | async-start | bytes 5242880 | tf_op jit(solution)/shard_map/all_gather | solution.py:81
  1816.7 671.6 %all-gather.93.cloned.1.call-start = ((), (), s32[]{:S(2)}) async-start(), calls=%async_computation.56 | async-start | bytes 5242880 | tf_op jit(solution)/shard_map/all_gather | solution.py:81
  1817.4 706.8 %all-gather.133.cloned.1.call-start = ((), (), s32[]{:S(2)}) async-start(), calls=%async_computation.92 | async-start | bytes 5242880 | tf_op jit(solution)/shard_map/all_gather | solution.py:81
  1992.7 708.9 %reduce-scatter.36.cloned.1.call-start = ((), (), s32[]{:S(2)}) async-start(), calls=%async_computation.53 | async-start | bytes 10485760 | tf_op jit(solution)/shard_map/reduce_scatter | solution.py:295
  2345.3 473.3 %reduce-scatter.38.cloned.1.call-start = ((), (), s32[]{:S(2)}) async-start(), calls=%async_computation.54 | async-start | bytes 10485760 | tf_op jit(solution)/shard_map/reduce_scatter | solution.py:296
  2578.3 315.5 %reduce-scatter.42.cloned.1.call-start = ((), (), s32[]{:S(2)}) async-start(), calls=%async_computation.57 | async-start | bytes 10485760 | tf_op jit(solution)/shard_map/reduce_scatter | solution.py:315
  2693.4 274.6 %reduce-scatter.40.cloned.1.call-start = ((), (), s32[]{:S(2)}) async-start(), calls=%async_computation.55 | async-start | bytes 10485760 | tf_op jit(solution)/shard_map/reduce_scatter | solution.py:314
  2833.9 206.8 %all-gather.99.cloned.1.call-start = ((), (), s32[]{:S(2)}) async-start(), calls=%async_computation.60 | async-start | bytes 5242880 | tf_op jit(solution)/shard_map/all_gather | solution.py:257
  3007.0 116.5 %all-gather.101.cloned.1.call-start = ((), (), s32[]{:S(2)}) async-start(), calls=%async_computation.61 | async-start | bytes 5242880 | tf_op jit(solution)/shard_map/all_gather | solution.py:94
  3009.3 277.8 %reduce-scatter.44.cloned.1.call-start = ((), (), s32[]{:S(2)}) async-start(), calls=%async_computation.62 | async-start | bytes 10485760 | tf_op jit(solution)/shard_map/reduce_scatter | solution.py:295
  3144.0 290.6 %reduce-scatter.46.cloned.1.call-start = ((), (), s32[]{:S(2)}) async-start(), calls=%async_computation.63 | async-start | bytes 10485760 | tf_op jit(solution)/shard_map/reduce_scatter | solution.py:296
  3151.4 358.1 %reduce-scatter.50.cloned.1.call-start = ((), (), s32[]{:S(2)}) async-start(), calls=%async_computation.66 | async-start | bytes 10485760 | tf_op jit(solution)/shard_map/reduce_scatter | solution.py:315
  3186.5 398.0 %reduce-scatter.48.cloned.1.call-start = ((), (), s32[]{:S(2)}) async-start(), calls=%async_computation.64 | async-start | bytes 10485760 | tf_op jit(solution)/shard_map/reduce_scatter | solution.py:314
  3449.8 208.9 %all-gather.109.cloned.1.call-start = ((), (), s32[]{:S(2)}) async-start(), calls=%async_computation.69 | async-start | bytes 5242880 | tf_op jit(solution)/shard_map/all_gather | solution.py:257
  3624.9 116.6 %all-gather.111.cloned.1.call-start = ((), (), s32[]{:S(2)}) async-start(), calls=%async_computation.70 | async-start | bytes 5242880 | tf_op jit(solution)/shard_map/all_gather | solution.py:94
  3627.3 276.9 %reduce-scatter.52.cloned.1.call-start = ((), (), s32[]{:S(2)}) async-start(), calls=%async_computation.71 | async-start | bytes 10485760 | tf_op jit(solution)/shard_map/reduce_scatter | solution.py:295
  3761.0 291.2 %reduce-scatter.54.cloned.1.call-start = ((), (), s32[]{:S(2)}) async-start(), calls=%async_computation.72 | async-start | bytes 10485760 | tf_op jit(solution)/shard_map/reduce_scatter | solution.py:296
  3769.1 358.1 %reduce-scatter.58.cloned.1.call-start = ((), (), s32[]{:S(2)}) async-start(), calls=%async_computation.75 | async-start | bytes 10485760 | tf_op jit(solution)/shard_map/reduce_scatter | solution.py:315
  3804.7 397.6 %reduce-scatter.56.cloned.1.call-start = ((), (), s32[]{:S(2)}) async-start(), calls=%async_computation.73 | async-start | bytes 10485760 | tf_op jit(solution)/shard_map/reduce_scatter | solution.py:314
  4067.5 208.9 %all-gather.119.cloned.1.call-start = ((), (), s32[]{:S(2)}) async-start(), calls=%async_computation.78 | async-start | bytes 5242880 | tf_op jit(solution)/shard_map/all_gather | solution.py:257
  4242.7 116.7 %all-gather.121.cloned.1.call-start = ((), (), s32[]{:S(2)}) async-start(), calls=%async_computation.79 | async-start | bytes 5242880 | tf_op jit(solution)/shard_map/all_gather | solution.py:94
  4245.0 277.0 %reduce-scatter.60.cloned.1.call-start = ((), (), s32[]{:S(2)}) async-start(), calls=%async_computation.80 | async-start | bytes 10485760 | tf_op jit(solution)/shard_map/reduce_scatter | solution.py:295
  4378.8 291.2 %reduce-scatter.62.cloned.1.call-start = ((), (), s32[]{:S(2)}) async-start(), calls=%async_computation.81 | async-start | bytes 10485760 | tf_op jit(solution)/shard_map/reduce_scatter | solution.py:296
  4386.9 358.7 %reduce-scatter.66.cloned.1.call-start = ((), (), s32[]{:S(2)}) async-start(), calls=%async_computation.84 | async-start | bytes 10485760 | tf_op jit(solution)/shard_map/reduce_scatter | solution.py:315
  4422.4 398.2 %reduce-scatter.64.cloned.1.call-start = ((), (), s32[]{:S(2)}) async-start(), calls=%async_computation.82 | async-start | bytes 10485760 | tf_op jit(solution)/shard_map/reduce_scatter | solution.py:314
  4685.3 217.7 %all-gather.83.cloned.1.call-start = ((), (), s32[]{:S(2)}) async-start(), calls=%async_computation.47 | async-start | bytes 5242880 | tf_op jit(solution)/shard_map/all_gather | solution.py:93
  4692.7 244.8 %all-gather.129.cloned.1.call-start = ((), (), s32[]{:S(2)}) async-start(), calls=%async_computation.87 | async-start | bytes 5242880 | tf_op jit(solution)/shard_map/all_gather | solution.py:257
  4861.1 158.7 %all-gather.131.cloned.1.call-start = ((), (), s32[]{:S(2)}) async-start(), calls=%async_computation.88 | async-start | bytes 5242880 | tf_op jit(solution)/shard_map/all_gather | solution.py:94
  4863.4 248.0 %all-gather.81.cloned.1.call-start = ((), (), s32[]{:S(2)}) async-start(), calls=%async_computation.46 | async-start | bytes 5242880 | tf_op jit(solution)/shard_map/all_gather | solution.py:94
  4865.8 517.7 %reduce-scatter.68.cloned.1.call-start = ((), (), s32[]{:S(2)}) async-start(), calls=%async_computation.89 | async-start | bytes 10485760 | tf_op jit(solution)/shard_map/reduce_scatter | solution.py:295
  5049.0 349.0 %reduce-scatter.70.cloned.1.call-start = ((), (), s32[]{:S(2)}) async-start(), calls=%async_computation.90 | async-start | bytes 10485760 | tf_op jit(solution)/shard_map/reduce_scatter | solution.py:296
  5055.9 468.2 %reduce-scatter.34.cloned.1.call-start = ((), (), s32[]{:S(2)}) async-start(), calls=%async_computation.49 | async-start | bytes 10485760 | tf_op jit(solution)/shard_map/reduce_scatter | solution.py:209
  5154.8 400.3 %reduce-scatter.74.cloned.1.call-start = ((), (), s32[]{:S(2)}) async-start(), calls=%async_computation.93 | async-start | bytes 10485760 | tf_op jit(solution)/shard_map/reduce_scatter | solution.py:315
  5273.0 345.2 %reduce-scatter.72.cloned.1.call-start = ((), (), s32[]{:S(2)}) async-start(), calls=%async_computation.91 | async-start | bytes 10485760 | tf_op jit(solution)/shard_map/reduce_scatter | solution.py:314
  5413.1 1048.3 %all-reduce.5.cloned.1.call-start = ((), (), s32[]{:S(2)}) async-start(), calls=%async_computation.95 | async-start | bytes 50331648 | tf_op jit(solution)/shard_map/psum | solution.py:338
  (269 other events, 10600.6 us)
Sparse Core Ops, SparseCore 0:
  16.0 37.1 all-gather.46
  55.3 34.4 all-gather.52
  91.4 80.7 all-gather.50
  173.6 79.2 all-gather.48
  296.5 70.2 reduce-scatter.25
  403.6 35.4 all-gather.54
  441.3 34.4 all-gather.60
  477.5 80.7 all-gather.58
  560.5 79.2 all-gather.56
  683.3 70.2 reduce-scatter.27
  791.2 35.4 all-gather.62
  828.8 34.4 all-gather.94
  865.4 34.4 all-gather.68
  901.9 80.7 all-gather.66
  984.7 79.2 all-gather.64
  1107.5 70.2 reduce-scatter.29
  1214.0 35.1 all-gather.70
  1251.3 34.4 all-gather.104
  1288.0 34.4 all-gather.76
  1324.6 80.7 all-gather.74
  1407.7 79.2 all-gather.72
  1530.2 70.2 reduce-scatter.31
  1640.8 35.4 all-gather.124
  1678.3 34.4 all-gather.78
  1751.5 34.4 all-gather.86
  1787.4 34.4 all-gather.134
  1823.5 80.7 all-gather.96
  1905.9 79.2 all-gather.106
  1987.2 79.2 all-gather.126
  2068.7 79.2 all-gather.116
  2149.6 79.2 all-gather.88
  2230.3 79.2 all-gather.90
  2345.8 34.4 all-gather.112
  2381.7 34.4 all-gather.122
  2417.7 34.4 all-gather.84
  2489.7 34.4 all-gather.132
  2526.6 144.4 reduce-scatter.35
  2673.4 145.1 reduce-scatter.37
  2821.2 72.4 reduce-scatter.41
  2896.3 71.6 reduce-scatter.39
  3042.7 80.7 all-gather.100
  3144.1 142.9 reduce-scatter.43
  3289.4 145.1 reduce-scatter.45
  3437.0 72.4 reduce-scatter.49
  3512.7 71.7 reduce-scatter.47
  3660.7 80.7 all-gather.110
  3761.2 143.0 reduce-scatter.51
  3907.0 145.1 reduce-scatter.53
  4054.8 72.4 reduce-scatter.57
  4130.6 71.6 reduce-scatter.55
  4278.6 80.7 all-gather.120
  4378.9 143.0 reduce-scatter.59
  4524.8 145.1 reduce-scatter.61
  4673.2 72.4 reduce-scatter.65
  4748.9 71.6 reduce-scatter.63
  4822.3 80.7 all-gather.82
  4938.9 80.7 all-gather.130
  5021.9 79.2 all-gather.80
  5103.4 143.0 reduce-scatter.67
  5248.7 145.1 reduce-scatter.69
  5397.0 72.4 reduce-scatter.33
  5472.3 71.7 reduce-scatter.73
  5546.5 71.7 reduce-scatter.71
  5622.0 839.2 all-reduce.4
  (7 shorter events, 235.3 us)
where the time goes:
time: 6520 us; the launch traced here: 6510 us
  waiting for transfers between devices  4430 us (68%)
  matrix products  1320 us (20%)
  other arithmetic  367 us (6%)
  local copies, waits for them, and re-layouts  241 us (4%)
  blocking collectives  102 us (2%)
    psum x1, waiting for transfers between devices, body(): lax.psum(shortened(tuple(big_totals)), 'ctx')  734 us
    all_gather x10, waiting for transfers between devices, block_forward(): lax.all_gather(key_low, 'ctx', axis=0, tiled=True)  667 us
    all_gather x10, waiting for transfers between devices, block_forward(): lax.all_gather(value_low, 'ctx', axis=0, tiled=True)  654 us
    reduce_scatter x5, waiting for transfers between devices, body(): lax.psum_scatter(d_value, 'ctx', scatter_dimension=0, tiled=True)  486 us
    reduce_scatter x5, waiting for transfers between devices, body(): lax.psum_scatter(d_one, 'tensor', scatter_dimension=0, tiled=True)  363 us
    reduce_scatter x5, waiting for transfers between devices, body(): lax.psum_scatter(branch_rows(jnp.int32(0), row_count * lax.axis_size('ten...  281 us
    reduce_scatter x5, waiting for transfers between devices, body(): lax.psum_scatter(d_key, 'ctx', scatter_dimension=0, tiled=True)  269 us
    all_gather x10, waiting for transfers between devices, block_forward(): lax.all_gather(local_one, 'tensor', axis=0, tiled=True)  252 us
  transfers between devices with their start and end apart: 79, of which 72 were waited for; matrix products, arithmetic and copies ran while one was open for 23% of the time, Pallas kernels for 0%

commit v1 on v0

v1 whole, which is shorter than its diff:
```python
from functools import partial

import jax
import jax.numpy as jnp
from jax import lax
from jax.experimental import pallas as pl
from jax.experimental.pallas import tpu as pltpu
from jax.sharding import PartitionSpec as P

ROT = 64
LAG = 2
LANES = 128
epsilon = 1e-05
masked_score = -1e30
f32 = jnp.float32
bf16 = jnp.bfloat16
NT = (((1,), (1,)), ((), ()))
TN = (((0,), (0,)), ((), ()))
NN = (((1,), (0,)), ((), ()))
VMEM_LIMIT = 50 * 1024 * 1024


def dot(a, b, dims=NN):
    return lax.dot_general(a, b, dims, preferred_element_type=f32)


def standardize(rows):
    values = rows.astype(f32)
    average = jnp.mean(values, axis=-1, keepdims=True)
    centred = values - average
    inverse = lax.rsqrt(jnp.mean(centred * centred, axis=-1, keepdims=True) + epsilon)
    return centred * inverse, inverse


def position_tables(section_rows, blocks, rows, tensor):
    half = ROT // 2
    frequency = 1.0 / 10000.0 ** (jnp.arange(0, ROT, 2, dtype=f32) / ROT)
    t, c, i = jnp.meshgrid(
        jnp.arange(tensor), jnp.arange(blocks), jnp.arange(rows), indexing="ij"
    )
    relative = (c * (rows * tensor) + t * rows + i).reshape(-1).astype(jnp.int32)
    tables = []
    for part in range(2):
        places = (relative + part * blocks * rows * tensor).astype(f32)
        angles = places[:, None] * frequency[None, :]
        cosine, sine = jnp.cos(angles), jnp.sin(angles)
        none = jnp.zeros_like(sine)
        rest = jnp.zeros((relative.shape[0], LANES - ROT), f32)
        tables.append(
            (
                jnp.concatenate([cosine, cosine, rest + 1.0], axis=-1),
                jnp.concatenate([-sine, none, rest], axis=-1),
                jnp.concatenate([none, sine, rest], axis=-1),
            )
        )
    return relative, tables


def turn(values, cosine, ahead, behind, sign):
    half = ROT // 2
    lead = values[:, :LANES]
    turned = pltpu.roll(lead, LANES - half, 1) * ahead + pltpu.roll(lead, half, 1) * behind
    return jnp.concatenate([lead * cosine + sign * turned, values[:, LANES:]], axis=1)


def project_kernel(heads, wide, slot, std, wq, bq, wi, bi, cosine, ahead, behind, *rest):
    qkv_out, std_out, act_out, dg_out = rest[-4:]
    step = pl.program_id(0)

    @pl.when(step == 0)
    def _():
        std_out[0] = std[...]

    @pl.when(step < heads)
    def _():
        size = wq.shape[1] // 3
        for part in range(3):
            columns = slice(part * size, (part + 1) * size)
            z = dot(std[...], wq[:, columns]) + bq[:, columns]
            if part < 2:
                z = turn(z, cosine[...], ahead[...], behind[...], 1.0)
            qkv_out[0, :, columns] = z.astype(bf16)

    @pl.when(step >= heads)
    def _():
        for at in range(0, wide, 256):
            columns = slice(at, at + 256)
            h = dot(std[...], wi[:, columns]) + bi[:, columns]
            phi = 0.5 + 0.5 * lax.erf(h * (0.5**0.5))
            density = jnp.exp(h * h * -0.5) * 0.3989422804014327
            act_out[0, :, columns] = (h * phi).astype(bf16)
            dg_out[0, :, columns] = (phi + h * density).astype(bf16)


def stacked_outputs(shapes, buffers, first_input):
    out_shape = [jax.ShapeDtypeStruct(s, d) for s, d in shapes]
    if buffers is None:
        return out_shape, [], [], {}
    aliases = {first_input + k: k for k in range(len(buffers))}
    return out_shape, list(buffers), [pl.BlockSpec(memory_space=pl.ANY)] * len(buffers), aliases


def params():
    return pltpu.CompilerParams(vmem_limit_bytes=VMEM_LIMIT)


def project(slot, std, wq, bq, wi, bi, table, slots, buffers):
    rows, width = std.shape
    heads = bq.shape[1] // 768
    head_cols = wq.shape[1] // heads
    units = wi.shape[1]
    wide = min(512, units)
    shapes = [
        ((slots, rows, wq.shape[1]), bf16),
        ((slots, rows, width), bf16),
        ((slots, rows, units), bf16),
        ((slots, rows, units), bf16),
    ]
    out_shape, extra, extra_specs, aliases = stacked_outputs(shapes, buffers, 9)
    head_of = lambda i, s: (0, jnp.minimum(i, heads - 1))
    unit_of = lambda i, s: (0, jnp.maximum(i - heads, 0))
    whole = lambda i, s: (0, 0)
    return pl.pallas_call(
        partial(project_kernel, heads, wide),
        out_shape=out_shape,
        grid_spec=pltpu.PrefetchScalarGridSpec(
            num_scalar_prefetch=1,
            grid=(heads + units // wide,),
            in_specs=[
                pl.BlockSpec((rows, width), whole),
                pl.BlockSpec((width, head_cols), head_of),
                pl.BlockSpec((1, head_cols), head_of),
                pl.BlockSpec((width, wide), unit_of),
                pl.BlockSpec((1, wide), unit_of),
                pl.BlockSpec((rows, LANES), whole),
                pl.BlockSpec((rows, LANES), whole),
                pl.BlockSpec((rows, LANES), whole),
            ]
            + extra_specs,
            out_specs=[
                pl.BlockSpec((1, rows, head_cols), lambda i, s: (s[0], 0, jnp.minimum(i, heads - 1))),
                pl.BlockSpec((1, rows, width), lambda i, s: (s[0], 0, 0)),
                pl.BlockSpec((1, rows, wide), lambda i, s: (s[0], 0, jnp.maximum(i - heads, 0))),
                pl.BlockSpec((1, rows, wide), lambda i, s: (s[0], 0, jnp.maximum(i - heads, 0))),
            ],
        ),
        input_output_aliases=aliases,
        compiler_params=params(),
        cost_estimate=pl.CostEstimate(
            flops=2 * rows * width * (wq.shape[1] + units),
            bytes_accessed=2 * width * (wq.shape[1] + units) + 8 * rows * width,
            transcendentals=2 * rows * units,
        ),
        name="project",
    )(slot, std, wq, bq, wi, bi, *table, *extra)


def attend_kernel(second, slot, *refs):
    if second:
        q, k, v, kp, vp, pq, pk = refs[:7]
    else:
        q, k, v, pq, pk = refs[:5]
    ctx_out, lse_out = refs[-2:]
    scale = q.shape[-1] ** -0.5
    s = dot(q[0], k[0], NT) * scale
    s = jnp.where(pq[...] >= pk[...], s, masked_score)
    peak = jnp.max(s, axis=-1, keepdims=True)
    if second:
        sp = dot(q[0], kp[0], NT) * scale
        peak = jnp.maximum(peak, jnp.max(sp, axis=-1, keepdims=True))
    p = jnp.exp(s - peak)
    total = jnp.sum(p, axis=-1, keepdims=True)
    if second:
        pp = jnp.exp(sp - peak)
        total = total + jnp.sum(pp, axis=-1, keepdims=True)
    share = 1.0 / total
    ctx = dot((p * share).astype(bf16), v[0])
    if second:
        ctx = ctx + dot((pp * share).astype(bf16), vp[0])
    ctx_out[0] = ctx.astype(bf16)
    lse_out[0] = jnp.broadcast_to(peak + jnp.log(total), lse_out.shape[1:])


def head_block(rows, part, back, size):
    return pl.BlockSpec((1, rows, size), lambda h, s: (s[0] - back, 0, 3 * h + part))


def attend(slot, qkv, places_q, places_k, heads, second, buffers):
    slots, rows, columns = qkv.shape
    size = columns // (3 * heads)
    shapes = [((slots, rows, heads * size), bf16), ((slots, rows, heads * LANES), f32)]
    count = 5 if second else 3
    out_shape, extra, extra_specs, aliases = stacked_outputs(shapes, buffers, count + 3)
    whole = lambda h, s: (0, 0)
    specs = [head_block(rows, part, 0, size) for part in range(3)]
    if second:
        specs += [head_block(rows, part, 1, size) for part in (1, 2)]
    keys = rows * (2 if second else 1)
    return pl.pallas_call(
        partial(attend_kernel, second),
        out_shape=out_shape,
        grid_spec=pltpu.PrefetchScalarGridSpec(
            num_scalar_prefetch=1,
            grid=(heads,),
            in_specs=specs + [pl.BlockSpec((rows, 1), whole), pl.BlockSpec((1, rows), whole)] + extra_specs,
            out_specs=[
                pl.BlockSpec((1, rows, size), lambda h, s: (s[0], 0, h)),
                pl.BlockSpec((1, rows, LANES), lambda h, s: (s[0], 0, h)),
            ],
        ),
        input_output_aliases=aliases,
        compiler_params=params(),
        cost_estimate=pl.CostEstimate(
            flops=4 * heads * rows * keys * size * 2,
            bytes_accessed=2 * rows * columns,
            transcendentals=heads * rows * keys,
        ),
        name="attend",
    )(slot, *([qkv] * count), places_q, places_k, *extra)


def combine_kernel(dims, slot, a, b, wa, wb, out):
    out[...] = (dot(a[0], wa[...], dims) + dot(b[0], wb[...], dims)).astype(bf16)


def combine(slot, a, b, wa, wb, transposed):
    rows = a.shape[1]
    width = wa.shape[0] if transposed else wa.shape[1]
    wide = min(512, width)
    if transposed:
        weight_specs = [pl.BlockSpec((wide, w.shape[1]), lambda i, s: (i, 0)) for w in (wa, wb)]
    else:
        weight_specs = [pl.BlockSpec((w.shape[0], wide), lambda i, s: (0, i)) for w in (wa, wb)]
    return pl.pallas_call(
        partial(combine_kernel, NT if transposed else NN),
        out_shape=jax.ShapeDtypeStruct((rows, width), bf16),
        grid_spec=pltpu.PrefetchScalarGridSpec(
            num_scalar_prefetch=1,
            grid=(width // wide,),
            in_specs=[
                pl.BlockSpec((1, rows, a.shape[2]), lambda i, s: (s[0], 0, 0)),
                pl.BlockSpec((1, rows, b.shape[2]), lambda i, s: (s[0], 0, 0)),
            ]
            + weight_specs,
            out_specs=pl.BlockSpec((rows, wide), lambda i, s: (0, i)),
        ),
        compiler_params=params(),
        cost_estimate=pl.CostEstimate(
            flops=2 * rows * width * (a.shape[2] + b.shape[2]),
            bytes_accessed=2 * width * (a.shape[2] + b.shape[2]) + 4 * rows * width,
            transcendentals=0,
        ),
        name="combine",
    )(slot, a, b, wa, wb)


def spread_kernel(slot, gy, wo, wd, dg, *rest):
    dctx_out, gy_out, dh_out = rest[-3:]
    step = pl.program_id(0)

    @pl.when(step == 0)
    def _():
        gy_out[0] = gy[...]
        dctx_out[...] = dot(gy[...], wo[...], NT).astype(bf16)

    @pl.when(step > 0)
    def _():
        for at in range(0, wd.shape[0], 256):
            part = slice(at, at + 256)
            dh_out[0, :, part] = (dot(gy[...], wd[part, :], NT) * dg[0, :, part].astype(f32)).astype(bf16)


def spread(slot, gy, wo, wd, dg, buffers):
    rows, width = gy.shape
    slots = dg.shape[0]
    units = wd.shape[0]
    wide = min(512, units)
    shapes = [
        ((rows, wo.shape[0]), bf16),
        ((slots, rows, width), bf16),
        ((slots, rows, units), bf16),
    ]
    out_shape = [jax.ShapeDtypeStruct(s, d) for s, d in shapes]
    extra, extra_specs, aliases = [], [], {}
    if buffers is not None:
        extra = list(buffers)
        extra_specs = [pl.BlockSpec(memory_space=pl.ANY)] * 2
        aliases = {5: 1, 6: 2}
    whole = lambda i, s: (0, 0)
    unit_of = lambda i, s: (s[0], 0, jnp.maximum(i - 1, 0))
    return pl.pallas_call(
        spread_kernel,
        out_shape=out_shape,
        grid_spec=pltpu.PrefetchScalarGridSpec(
            num_scalar_prefetch=1,
            grid=(1 + units // wide,),
            in_specs=[
                pl.BlockSpec((rows, width), whole),
                pl.BlockSpec(wo.shape, whole),
                pl.BlockSpec((wide, width), lambda i, s: (jnp.maximum(i - 1, 0), 0)),
                pl.BlockSpec((1, rows, wide), unit_of),
            ]
            + extra_specs,
            out_specs=[
                pl.BlockSpec((rows, wo.shape[0]), whole),
                pl.BlockSpec((1, rows, width), lambda i, s: (s[0], 0, 0)),
                pl.BlockSpec((1, rows, wide), unit_of),
            ],
        ),
        input_output_aliases=aliases,
        compiler_params=params(),
        cost_estimate=pl.CostEstimate(
            flops=2 * rows * width * (units + wo.shape[0]),
            bytes_accessed=2 * width * (units + wo.shape[0]) + 8 * rows * width,
            transcendentals=0,
        ),
        name="spread",
    )(slot, gy, wo, wd, dg, *extra)


def attend_back_kernel(second, slot, *refs):
    if second:
        q, k, v, dctx, ctx, lse, pq, pk, cosine, ahead, behind, kp, vp = refs[:13]
        out, dkp_out, dvp_out = refs[-3:]
    else:
        q, k, v, dctx, ctx, lse, pq, pk, cosine, ahead, behind, dk_in, dv_in = refs[:13]
        out = refs[-1]
    size = q.shape[-1]
    scale = size**-0.5
    logsum = lse[0][:, :1]
    delta = jnp.sum(dctx[...].astype(f32) * ctx[0].astype(f32), axis=-1, keepdims=True)

    def pieces(k, v, masked):
        s = dot(q[0], k[0], NT) * scale
        if masked:
            s = jnp.where(pq[...] >= pk[...], s, masked_score)
        p = jnp.exp(s - logsum)
        d_chance = dot(dctx[...], v[0], NT)
        d_scores = (p * (d_chance - delta)).astype(bf16)
        dq = dot(d_scores, k[0])
        dk = dot(d_scores, q[0], TN)
        dv = dot(p.astype(bf16), dctx[...], TN)
        return dq, dk, dv

    dq, dk, dv = pieces(k, v, True)
    if second:
        dq_more, dkp, dvp = pieces(kp, vp, False)
        dq = dq + dq_more
        dkp_out[...] = dkp
        dvp_out[...] = dvp
    else:
        dk = dk + dk_in[...]
        dv = dv + dv_in[...]
    table = (cosine[...], ahead[...], behind[...])
    out[0, :, 0:size] = turn(dq * scale, *table, -1.0).astype(bf16)
    out[0, :, size : 2 * size] = turn(dk * scale, *table, -1.0).astype(bf16)
    out[0, :, 2 * size :] = dv.astype(bf16)


def attend_back(slot, qkv, dctx, ctx, lse, places_q, places_k, table, heads, carry, buffer):
    slots, rows, columns = qkv.shape
    size = columns // (3 * heads)
    second = carry is None
    whole = lambda h, s: (0, 0)
    specs = [head_block(rows, part, 0, size) for part in range(3)]
    specs += [
        pl.BlockSpec((rows, size), lambda h, s: (0, h)),
        pl.BlockSpec((1, rows, size), lambda h, s: (s[0], 0, h)),
        pl.BlockSpec((1, rows, LANES), lambda h, s: (s[0], 0, h)),
        pl.BlockSpec((rows, 1), whole),
        pl.BlockSpec((1, rows), whole),
        pl.BlockSpec((rows, LANES), whole),
        pl.BlockSpec((rows, LANES), whole),
        pl.BlockSpec((rows, LANES), whole),
    ]
    out_shape = [jax.ShapeDtypeStruct((slots, rows, columns), bf16)]
    out_specs = [pl.BlockSpec((1, rows, 3 * size), lambda h, s: (s[0], 0, h))]
    column_spec = pl.BlockSpec((rows, size), lambda h, s: (0, h))
    if second:
        specs += [head_block(rows, part, 1, size) for part in (1, 2)]
        more = (qkv, qkv)
        out_shape += [jax.ShapeDtypeStruct((rows, heads * size), f32)] * 2
        out_specs += [column_spec] * 2
    else:
        specs += [column_spec] * 2
        more = carry
    extra, extra_specs, aliases = [], [], {}
    if buffer is not None:
        extra, extra_specs, aliases = [buffer], [pl.BlockSpec(memory_space=pl.ANY)], {14: 0}
    keys = rows * (2 if second else 1)
    return pl.pallas_call(
        partial(attend_back_kernel, second),
        out_shape=out_shape,
        grid_spec=pltpu.PrefetchScalarGridSpec(
            num_scalar_prefetch=1, grid=(heads,), in_specs=specs + extra_specs, out_specs=out_specs
        ),
        input_output_aliases=aliases,
        compiler_params=params(),
        cost_estimate=pl.CostEstimate(
            flops=10 * heads * rows * keys * size * 2,
            bytes_accessed=6 * rows * columns,
            transcendentals=heads * rows * keys,
        ),
        name="attend_back",
    )(slot, qkv, qkv, qkv, dctx, ctx, lse, places_q, places_k, *table, *more, *extra)


def exchange(blocks, axis):
    count = blocks.shape[0]
    me = lax.axis_index(axis)
    got = [lax.dynamic_index_in_dim(blocks, me, 0, keepdims=False)]
    for shift in range(1, count):
        piece = lax.dynamic_index_in_dim(blocks, (me + shift) % count, 0, keepdims=False)
        got.append(lax.ppermute(piece, axis, [(k, (k + shift) % count) for k in range(count)]))
    ring = jnp.stack(got[::-1] + got[::-1])
    return lax.dynamic_slice_in_dim(ring, (count - 1 - me) % count, count, 0)


def swap_cores(v, tensor):
    return lax.ppermute(v, "tensor", [(k, k ^ 1) for k in range(tensor)])


def shift_chips(v, tensor, shift):
    return lax.ppermute(v, "tensor", [(k, (k + 2 * shift) % tensor) for k in range(tensor)])


def gather_rows(own, tensor):
    chips = tensor // 2
    me = lax.axis_index("tensor")
    chip, core = me // 2, me % 2
    got = [own] + [shift_chips(own, tensor, shift) for shift in range(1, chips)]
    if chips == 2:
        mine = jnp.stack([jnp.where(chip == 0, got[0], got[1]), jnp.where(chip == 0, got[1], got[0])])
    else:
        ring = jnp.stack(got[::-1] + got[::-1])
        mine = lax.dynamic_slice_in_dim(ring, (chips - 1 - chip) % chips, chips, 0)
    theirs = swap_cores(mine, tensor)
    both = jnp.stack([jnp.where(core == 0, mine, theirs), jnp.where(core == 0, theirs, mine)], axis=1)
    return both.reshape(tensor * own.shape[0], own.shape[1])


def scatter_sum(partial_rows, tensor):
    chips = tensor // 2
    me = lax.axis_index("tensor")
    chip, core = me // 2, me % 2
    width = partial_rows.shape[1]
    parts = partial_rows.reshape(chips, 2, -1, width)
    mine = lax.dynamic_index_in_dim(parts, core, 1, keepdims=False)
    theirs = swap_cores(lax.dynamic_index_in_dim(parts, 1 - core, 1, keepdims=False), tensor)
    total = mine.astype(f32) + theirs.astype(f32)
    low = total.astype(bf16)
    own = lax.dynamic_index_in_dim(total, chip, 0, keepdims=False)
    for shift in range(1, chips):
        piece = lax.dynamic_index_in_dim(low, (chip + shift) % chips, 0, keepdims=False)
        own = own + shift_chips(piece, tensor, shift).astype(f32)
    return own


def body(
    inputs,
    out_grads,
    norm1_gain,
    norm1_bias,
    norm2_gain,
    norm2_bias,
    w_qkv,
    b_qkv,
    w_out,
    b_out,
    input_projection,
    input_bias_vector,
    down_projection,
    b_down,
):
    ctx_count = lax.axis_size("ctx")
    tensor = lax.axis_size("tensor")
    micro, _, rows, seqs, width = inputs.shape
    heads = w_qkv.shape[2]
    head_cols = w_qkv.shape[3]
    first = lax.axis_index("section") == 0
    per_device = micro * seqs // ctx_count
    blocks = ctx_count // 2
    own_rows = blocks * rows
    tasks = 2 * per_device
    slots = tasks + 1

    chosen = jnp.where(first, inputs[:, 0], out_grads[:, 0])
    chosen = chosen.transpose(0, 2, 1, 3).reshape(per_device, ctx_count, rows, width)
    own_chosen = []
    for j in range(per_device):
        moved = exchange(chosen[j], "ctx").reshape(2, own_rows, width)
        own_chosen += [moved[0], moved[1]]

    wq = w_qkv[0].reshape(width, heads * head_cols)
    wi = input_projection[0]
    wo = w_out[0].reshape(-1, width)
    wd = down_projection[0]
    gain_one, bias_one, gain_two, bias_two = norm1_gain[0], norm1_bias[0], norm2_gain[0], norm2_bias[0]
    wq_scaled = (wq.astype(f32) * gain_one[:, None]).astype(bf16)
    wi_scaled = (wi.astype(f32) * gain_two[:, None]).astype(bf16)
    bq = b_qkv[0].reshape(1, -1) + jnp.sum(wq.astype(f32) * bias_one[:, None], axis=0, keepdims=True)
    bi = input_bias_vector + jnp.sum(wi.astype(f32) * bias_two[:, None], axis=0, keepdims=True)
    out_bias = (b_out[0] + b_down[0])[None]

    relative, tables = position_tables(None, blocks, rows, tensor)
    places_q, places_k = relative[:, None], relative[None, :]

    arrived = {}
    kept = []
    produced = []
    forward_buffers = attend_buffers = None
    for step in range(tasks + LAG):
        x_own = own_chosen[min(step, tasks - 1)]
        if step >= LAG:
            x_own = jnp.where(first, x_own, arrived[step])
        kept.append(x_own)
        part = step % 2
        slot_first = step if step < tasks else tasks
        slot_second = step - LAG if step >= LAG else tasks
        slot = jnp.where(first, slot_first, slot_second).astype(jnp.int32).reshape(1)
        std = gather_rows(standardize(x_own)[0].astype(bf16), tensor)
        forward_buffers = project(
            slot, std, wq_scaled, bq, wi_scaled, bi, tables[part], slots, forward_buffers
        )
        attend_buffers = attend(
            slot, forward_buffers[0], places_q, places_k, heads, part == 1, attend_buffers
        )
        summed = scatter_sum(combine(slot, attend_buffers[0], forward_buffers[2], wo, wd, False), tensor)
        result = (x_own.astype(f32) + summed + out_bias).astype(bf16)
        produced.append(result)
        if step < tasks:
            arrived[step + LAG] = lax.ppermute(result, "section", [(0, 1)])
    qkv, std_all, act_all, dg_all = forward_buffers
    ctx_all, lse_all = attend_buffers

    back = {}
    back_list = []
    spread_buffers = None
    dproj_all = None
    carry = None
    bias_total = jnp.zeros((width,), f32)
    for step in range(tasks + LAG):
        part = 1 - step % 2
        task_first = max(step - LAG, 0)
        task_second = min(step, tasks - 1)
        slot_of = lambda task: (task // 2) * 2 + 1 - task % 2
        near, far = slot_of(task_first), slot_of(task_second)
        slot_first = near if step >= LAG else tasks
        slot_second = far if step < tasks else tasks
        slot = jnp.where(first, slot_first, slot_second).astype(jnp.int32).reshape(1)
        gy_own = own_chosen[far]
        if step >= LAG:
            gy_own = jnp.where(first, back[step], gy_own)
        gy = gather_rows(gy_own, tensor)
        dctx, *spread_buffers = spread(slot, gy, wo, wd, dg_all, spread_buffers)
        made = attend_back(
            slot,
            qkv,
            dctx,
            ctx_all,
            lse_all,
            places_q,
            places_k,
            tables[part],
            heads,
            None if part == 1 else carry,
            dproj_all,
        )
        dproj_all = made[0]
        carry = tuple(made[1:]) if part == 1 else None
        e = scatter_sum(combine(slot, dproj_all, spread_buffers[1], wq_scaled, wi_scaled, True), tensor)
        x_own = jnp.where(first, kept[near], kept[far + LAG])
        standard, inverse = standardize(x_own)
        gy_wide = gy_own.astype(f32)
        d_input = gy_wide + inverse * (
            e
            - jnp.mean(e, axis=-1, keepdims=True)
            - standard * jnp.mean(e * standard, axis=-1, keepdims=True)
        )
        back_list.append(d_input)
        valid = jnp.where(first, step >= LAG, step < tasks)
        bias_total = bias_total + jnp.where(valid, jnp.sum(gy_wide, axis=0), 0.0)
        if step < tasks:
            back[step + LAG] = lax.ppermute(d_input.astype(bf16), "section", [(1, 0)])
    gy_all, dh_all = spread_buffers

    def flat(v):
        return v[:tasks].reshape(-1, v.shape[-1])

    std_flat, gy_flat, dproj, dhidden = flat(std_all), flat(gy_all), flat(dproj_all), flat(dh_all)
    g_one = dot(std_flat, dproj, TN)
    g_two = dot(std_flat, dhidden, TN)
    d_b_qkv = jnp.sum(dproj, axis=0, dtype=f32)
    d_b_in = jnp.sum(dhidden, axis=0, dtype=f32)
    d_w_qkv = gain_one[:, None] * g_one + bias_one[:, None] * d_b_qkv[None]
    d_w_in = gain_two[:, None] * g_two + bias_two[:, None] * d_b_in[None]
    d_w_out = dot(flat(ctx_all), gy_flat, TN)
    d_w_down = dot(flat(act_all), gy_flat, TN)
    wq_wide, wi_wide = wq.astype(f32), wi.astype(f32)
    vectors = jnp.stack(
        [
            jnp.sum(wq_wide * g_one, axis=1),
            jnp.sum(wq_wide * d_b_qkv[None], axis=1),
            jnp.sum(wi_wide * g_two, axis=1),
            jnp.sum(wi_wide * d_b_in[None], axis=1),
            bias_total,
        ]
    )
    vectors = lax.psum(vectors, ("tensor", "ctx"))
    d_b_qkv, d_b_in = lax.psum((d_b_qkv, d_b_in), "ctx")
    big = lax.psum(tuple(v.astype(bf16) for v in (d_w_qkv, d_w_out, d_w_in, d_w_down)), "ctx")
    d_w_qkv, d_w_out, d_w_in, d_w_down = (v.astype(f32) for v in big)

    def homeward(pieces):
        stacked = jnp.stack(pieces).reshape(per_device, ctx_count, rows, width)
        moved = exchange(stacked.transpose(1, 0, 2, 3), "ctx")
        moved = moved.transpose(1, 0, 2, 3).reshape(micro, seqs, rows, width)
        return moved.transpose(0, 2, 1, 3)[None, :, None]

    states = homeward([jnp.where(first, produced[k], produced[k + LAG]) for k in range(tasks)])
    order = [(k // 2) * 2 + 1 - k % 2 for k in range(tasks)]
    input_grads = homeward(
        [jnp.where(first, back_list[k + LAG], back_list[k]).astype(bf16) for k in order]
    ).astype(f32)
    return (
        states,
        input_grads,
        vectors[0][None],
        vectors[1][None],
        vectors[2][None],
        vectors[3][None],
        d_w_qkv.reshape(w_qkv.shape),
        d_b_qkv.reshape(b_qkv.shape),
        d_w_out.reshape(w_out.shape),
        vectors[4][None],
        d_w_in[None],
        d_b_in[None],
        d_w_down[None],
        vectors[4][None],
    )


def solution(mesh):
    return jax.shard_map(
        body,
        mesh=mesh,
        in_specs=(
            P(None, "ctx", "tensor", None, None),
            P(None, "ctx", "tensor", None, None),
            P("section", None),
            P("section", None),
            P("section", None),
            P("section", None),
            P("section", None, "tensor", None),
            P("section", "tensor", None),
            P("section", "tensor", None, None),
            P("section", None),
            P("section", None, "tensor"),
            P("section", "tensor"),
            P("section", "tensor", None),
            P("section", None),
        ),
        out_specs=(
            P("section", None, "ctx", "tensor", None, None),
            P("section", None, "ctx", "tensor", None, None),
            P("section", None),
            P("section", None),
            P("section", None),
            P("section", None),
            P("section", None, "tensor", None),
            P("section", "tensor", None),
            P("section", "tensor", None, None),
            P("section", None),
            P("section", None, "tensor"),
            P("section", "tensor"),
            P("section", "tensor", None),
            P("section", None),
        ),
        check_vma=False,
    )
```

time: 6520 us -> 2570 us (0.39)
  waiting for transfers between devices: 4430 us -> 1080 us
  matrix products: 1320 us -> 143 us
  Pallas kernels: 0 us -> 590 us
  local copies, waits for them, and re-layouts: 241 us -> 121 us
  blocking collectives: 102 us -> 198 us
  starting transfers between devices: 24.4 us -> 110 us
  other arithmetic: 367 us -> 289 us
    all_gather x45 -> x0, waiting for transfers between devices: 1870 us -> none  [the longest x10 667 us: block_forward(): lax.all_gather(key_low, 'ctx', axis=0, tiled=True)]
    reduce_scatter x25 -> x0, waiting for transfers between devices: 1630 us -> none  [the longest x5 486 us: body(): lax.psum_scatter(d_value, 'ctx', scatter_dimension=0, tiled=True)]
    dot_general x105 -> x4, matrix products: 1320 us -> 143 us  [dot(): return lax.dot_general(a, b, dims, preferred_element_type=f32)]
    pallas_call x0 -> x60, Pallas kernels: none -> 590 us  [the longest x20 210 us: combine(): pl.pallas_call(partial(combine_kernel, NT if transposed else NN), out_sha...]
    ppermute x8 -> x114, waiting for transfers between devices: 188 us -> 663 us  [the longest x40 335 us: shift_chips(): lax.ppermute(v, 'tensor', [(k, (k + 2 * shift) % tensor) for k in range(t...]
    psum x1, waiting for transfers between devices: 734 us -> 420 us  [body(): lax.psum(tuple((v.astype(bf16) for v in (d_w_qkv, d_w_out, d_w_in, d_w_do...]
    another operation x20 -> x82, other arithmetic: 133 us -> 29.5 us  [the longest x40 13.9 us: gather_rows(): jnp.stack([jnp.where(core == 0, mine, theirs), jnp.where(core == 0, their...]
    psum x2, blocking collectives: 102 us -> 198 us  [the longest x1 117 us: body(): vectors = lax.psum(vectors, ('tensor', 'ctx'))]
  transfers between devices with their start and end apart: 79 -> 115, of which waited for: 72 -> 65; matrix products, arithmetic and copies ran while one was open for 23% -> 11% of each run, Pallas kernels for 0% -> 13%
where the time goes in v1:
time: 2570 us; the launch traced here: 2550 us
  waiting for transfers between devices  1080 us (42%)
  Pallas kernels  590 us (23%)
  other arithmetic  289 us (11%)
  blocking collectives  198 us (8%)
  matrix products  143 us (6%)
  local copies, waits for them, and re-layouts  121 us (5%)
  starting transfers between devices  110 us (4%)
    psum x1, waiting for transfers between devices, body(): lax.psum(tuple((v.astype(bf16) for v in (d_w_qkv, d_w_out, d_w_in, d_w_do...  420 us
    ppermute x40, waiting for transfers between devices, shift_chips(): lax.ppermute(v, 'tensor', [(k, (k + 2 * shift) % tensor) for k in range(t...  335 us
    pallas_call x20, Pallas kernels, combine(): pl.pallas_call(partial(combine_kernel, NT if transposed else NN), out_sha...  210 us
    ppermute x18, waiting for transfers between devices, exchange(): lax.ppermute(piece, axis, [(k, (k + shift) % count) for k in range(count)])  194 us
    pallas_call x10, Pallas kernels, project(): pl.pallas_call(partial(project_kernel, heads, wide), out_shape=out_shape,...  157 us
    dot_general x4, matrix products, dot(): return lax.dot_general(a, b, dims, preferred_element_type=f32)  143 us
    psum x1, blocking collectives, body(): vectors = lax.psum(vectors, ('tensor', 'ctx'))  117 us
    pallas_call x10, Pallas kernels, spread(): pl.pallas_call(spread_kernel, out_shape=out_shape, grid_spec=pltpu.Prefet...  116 us
  transfers between devices with their start and end apart: 115, of which 65 were waited for; matrix products, arithmetic and copies ran while one was open for 11% of the time, Pallas kernels for 13%

profile of v1, /device:TPU:0, one launch (start us, length us, event | category | flops | bytes accessed | tf_op | source)
XLA Modules:
  0.0 2553.2 jit_solution(18319684164076431090)
XLA Ops:
  7.3 16.2 fusion.21
  106.9 14.9 collective-permute-done.25
  141.5 16.1 project.10
  170.9 15.6 project.11
  207.6 11.6 collective-permute-done.18
  261.9 12.0 collective-permute-done.11
  283.9 15.6 project.12
  318.7 15.5 project.13
  362.0 12.3 collective-permute-done.28
  389.9 15.6 project.14
  427.0 11.4 collective-permute-done.31
  456.0 11.1 collective-permute-done.41
  467.7 15.8 project.15
  499.3 15.6 project.16
  578.2 11.5 collective-permute-done.46
  593.5 15.6 project.17
  631.6 11.7 collective-permute-done.49
  673.2 15.8 project.18
  703.9 15.6 project.19
  724.9 11.6 spread.10
  744.1 11.7 combine.31
  755.9 11.6 spread.11
  772.0 11.7 combine.30
  789.8 12.2 collective-permute-done.68
  817.2 13.4 collective-permute-done.74
  855.7 11.6 spread.12
  876.3 11.8 combine.33
  888.0 11.6 spread.13
  904.1 12.1 combine.32
  922.3 12.2 collective-permute-done.78
  951.2 14.1 collective-permute-done.84
  978.4 11.1 collective-permute-done.82
  991.3 11.7 spread.14
  1010.7 11.8 combine.35
  1022.5 11.6 spread.15
  1038.6 11.9 combine.34
  1056.6 12.2 collective-permute-done.88
  1085.5 14.1 collective-permute-done.94
  1124.6 11.7 spread.16
  1145.3 11.8 combine.37
  1157.1 11.6 spread.17
  1173.2 12.1 combine.36
  1191.4 12.2 collective-permute-done.98
  1220.2 14.1 collective-permute-done.104
  1247.1 12.8 collective-permute-done.105
  1272.0 11.7 spread.18
  1291.5 11.8 combine.39
  1304.5 11.6 spread.19
  1334.6 36.7 %fusion.13 = (bf16[2048,1536]{1,0:T(8,128)(2,1)}, f32[2048]{0:T(1024)S(1)}) fusion(f32[1536]{0:T(1024)S(1)} %convert_reduce_fusion.1, f32[2048]{0:T(1024)S(1)} %bitcast.941, f32[2048]{0:T(1024)S(1)} %bitcast.939, f32[2048,1536]{1,0:T(8,128)} %bitcast.912, bf16[9,512,2048]{2,1,0:T(8,128)(2,1)} %get-tuple-element.222, bf16[9,512,1536]{2,1,0:T(8,128)(2,1)} %attend_back.19.a), kind=kOutput, calls=%fused_computation.23 | convolution fusion | flops 25788676096 | bytes 50362368 | tf_op jit(solution)/shard_map/dot_general | solution.py:24
  1371.3 48.3 %fusion.3 = (f32[2048]{0:T(1024)S(1)}, f32[2048]{0:T(1024)S(1)}, bf16[1,2048,2048]{2,1,0:T(8,128)(2,1)}) fusion(bf16[1,2048,2048]{2,1,0:T(8,128)(2,1)} %param.24, f32[2048]{0:T(1024)S(1)} %convert_reduce_fusion, f32[2048]{0:T(1024)S(1)} %bitcast.943, f32[2048]{0:T(1024)S(1)} %bitcast.945, bf16[9,512,2048]{2,1,0:T(8,128)(2,1)} %get-tuple-element.222, ...), kind=kOutput, calls=%fused_computation.9 | convolution fusion | flops 34397487104 | bytes 52469760 | tf_op jit(solution)/shard_map/dot_general | solution.py:24
  1419.6 13.5 reshape.1007
  1433.1 15.1 bitcast_convert_fusion.1
  1448.3 43.3 %fusion.18 = bf16[1,2048,2048]{2,1,0:T(8,128)(2,1)} fusion(bf16[9,512,2048]{2,1,0:T(8,128)(2,1)} %get-tuple-element.175.b, bf16[9,512,2048]{2,1,0:T(8,128)(2,1)} %get-tuple-element.223), kind=kOutput, calls=%fused_computation.31 | convolution fusion | flops 34363932672 | bytes 44040192 | tf_op jit(solution)/shard_map/dot_general | solution.py:24
  1508.4 11.0 collective-permute-done.54
  1534.3 11.8 combine.38
  1546.2 49.4 %collective-permute-done.60 = bf16[4,64,2048]{2,1,0:T(8,128)(2,1)S(1)} collective-permute-done((bf16[4,64,2048]{2,1,0:T(8,128)(2,1)S(1)}, bf16[4,64,2048]{2,1,0:T(8,128)(2,1)S(1)}, u32[]{:S(2)}, u32[]{:S(2)}) %collective-permute-start.60) | collective-permute-done | bytes 1048608 | tf_op jit(solution)/shard_map/ppermute | solution.py:414
  1596.6 129.9 %collective-permute-done.61 = bf16[4,64,2048]{2,1,0:T(8,128)(2,1)S(1)} collective-permute-done((bf16[4,64,2048]{2,1,0:T(8,128)(2,1)S(1)}, bf16[4,64,2048]{2,1,0:T(8,128)(2,1)S(1)}, u32[]{:S(2)}, u32[]{:S(2)}) %collective-permute-start.61) | collective-permute-done | bytes 1048608 | tf_op jit(solution)/shard_map/ppermute | solution.py:414
  1764.0 91.4 %multiply_reduce_fusion = f32[2048]{0:T(1024)S(1)} fusion(bf16[1,2048,2,768]{3,2,1,0:T(2,128)(2,1)S(1)} %bitcast.910, f32[2,768]{1,0:T(2,128)S(1)} %mul.878), kind=kLoop, calls=%fused_computation.25 | loop fusion | flops 9435136 | bytes 6305792 | tf_op jit(solution)/shard_map/reduce_sum | solution.py:603
  1855.5 117.5 %psum.49 = f32[5,2048]{1,0:T(8,128)S(1)} all-reduce(f32[5,2048]{1,0:T(8,128)S(1)} %stack.698), channel_id=1, replica_groups=mesh['section'=2,'tensor'=4,'ctx'=4] {'tensor','ctx'}, use_global_device_ids=true, to_apply=%region_78.79 | all-reduce | flops 10240 | bytes 81920 | tf_op jit(solution)/shard_map/psum | solution.py:609
  1973.6 80.9 %all-reduce = (f32[1,2,768]{2,1,0:T(2,128)}, f32[1,2048]{1,0:T(1,128)}) all-reduce(f32[1,2,768]{2,1,0:T(2,128)S(1)} %reshape.1009, f32[1,2048]{1,0:T(1,128)S(1)} %bitcast.932), channel_id=1, replica_groups=mesh['section'=2,'tensor'=4,'ctx'=4] {'ctx'}, use_global_device_ids=true, to_apply=%region_80.81 | all-reduce | flops 3584 | bytes 28672 | tf_op jit(solution)/shard_map/psum | solution.py:610
  2077.9 12.3 copy.248
  2090.2 419.9 %all-reduce.4.cloned.1.call-done = (bf16[1,2048,2,768]{3,2,1,0:T(2,128)(2,1)}, bf16[1,2,256,2048]{3,2,1,0:T(8,128)(2,1)}, bf16[1,2048,2048]{2,1,0:T(8,128)(2,1)}, bf16[1,2048,2048]{2,1,0:T(8,128)(2,1)}) async-done(((bf16[1,2048,2,768]{3,2,1,0:T(2,128)(2,1)}, bf16[1,2,256,2048]{3,2,1,0:T(8,128)(2,1)}, bf16[1,2048,2048]{2,1,0:T(8,128)(2,1)}, bf16[1,2048,2048]{2,1,0:T(8,128)(2,1)}), ...) | async-done | bytes 25165840 | tf_op jit(solution)/shard_map/psum | solution.py:611
  2522.0 11.7 broadcast_in_dim.403
  2533.6 11.7 broadcast_in_dim.406
  (937 shorter events, 809.8 us)
Async XLA Ops:
  7.2 2502.9 %all-reduce.4.cloned.1.call-start = ((), (), s32[]{:S(2)}) async-start(), calls=%async_computation | async-start | bytes 50331648 | tf_op jit(solution)/shard_map/psum | solution.py:611
  27.5 51.5 %collective-permute-start = (bf16[64,2048]{1,0:T(8,128)(2,1)}, bf16[64,2048]{1,0:T(8,128)(2,1)}, u32[]{:S(2)}, u32[]{:S(2)}) collective-permute-start(bf16[64,2048]{1,0:T(8,128)(2,1)} %get-tuple-element.470), channel_id=1, source_target_pairs={{0,3},{1,0},{2,1},{3,2},{4,7},{5,4},{6,5},{7,6},{8,11},{9,8},{10,9... | collective-permute-start | bytes 786440 | tf_op jit(solution)/shard_map/ppermute | solution.py:414
  32.5 47.5 %collective-permute-start.1 = (bf16[64,2048]{1,0:T(8,128)(2,1)}, bf16[64,2048]{1,0:T(8,128)(2,1)}, u32[]{:S(2)}, u32[]{:S(2)}) collective-permute-start(bf16[64,2048]{1,0:T(8,128)(2,1)} %get-tuple-element.469), channel_id=1, source_target_pairs={{0,2},{1,3},{2,0},{3,1},{4,6},{5,7},{6,4},{7,5},{8,10},{9,11},{10,... | collective-permute-start | bytes 786440 | tf_op jit(solution)/shard_map/ppermute | solution.py:414
  32.5 52.4 %collective-permute-start.2 = (bf16[64,2048]{1,0:T(8,128)(2,1)}, bf16[64,2048]{1,0:T(8,128)(2,1)}, u32[]{:S(2)}, u32[]{:S(2)}) collective-permute-start(bf16[64,2048]{1,0:T(8,128)(2,1)} %get-tuple-element.468), channel_id=1, source_target_pairs={{0,1},{1,2},{2,3},{3,0},{4,5},{5,6},{6,7},{7,4},{8,9},{9,10},{10,1... | collective-permute-start | bytes 786440 | tf_op jit(solution)/shard_map/ppermute | solution.py:414
  34.4 56.9 %collective-permute-start.7 = (bf16[64,2048]{1,0:T(8,128)(2,1)}, bf16[64,2048]{1,0:T(8,128)(2,1)S(1)}, u32[]{:S(2)}, u32[]{:S(2)}) collective-permute-start(bf16[64,2048]{1,0:T(8,128)(2,1)} %get-tuple-element.465), channel_id=1, source_target_pairs={{0,3},{1,0},{2,1},{3,2},{4,7},{5,4},{6,5},{7,6},{8,11},{9,8},{10,9... | collective-permute-start | bytes 786440 | tf_op jit(solution)/shard_map/ppermute | solution.py:414
  37.4 54.5 %collective-permute-start.8 = (bf16[64,2048]{1,0:T(8,128)(2,1)}, bf16[64,2048]{1,0:T(8,128)(2,1)}, u32[]{:S(2)}, u32[]{:S(2)}) collective-permute-start(bf16[64,2048]{1,0:T(8,128)(2,1)} %get-tuple-element.464), channel_id=1, source_target_pairs={{0,2},{1,3},{2,0},{3,1},{4,6},{5,7},{6,4},{7,5},{8,10},{9,11},{10,... | collective-permute-start | bytes 786440 | tf_op jit(solution)/shard_map/ppermute | solution.py:414
  79.0 17.2 collective-permute-start.9
  80.1 25.6 %collective-permute-start.24 = (bf16[64,2048]{1,0:T(8,128)(2,1)}, bf16[64,2048]{1,0:T(8,128)(2,1)}, u32[]{:S(2)}, u32[]{:S(2)}) collective-permute-start(bf16[64,2048]{1,0:T(8,128)(2,1)} %get-tuple-element.456), channel_id=1, source_target_pairs={{0,3},{1,0},{2,1},{3,2},{4,7},{5,4},{6,5},{7,6},{8,11},{9,8},{10,9... | collective-permute-start | bytes 786440 | tf_op jit(solution)/shard_map/ppermute | solution.py:414
  84.9 36.9 %collective-permute-start.25 = (bf16[64,2048]{1,0:T(8,128)(2,1)}, bf16[64,2048]{1,0:T(8,128)(2,1)}, u32[]{:S(2)}, u32[]{:S(2)}) collective-permute-start(bf16[64,2048]{1,0:T(8,128)(2,1)} %get-tuple-element.455), channel_id=1, source_target_pairs={{0,2},{1,3},{2,0},{3,1},{4,6},{5,7},{6,4},{7,5},{8,10},{9,11},{10,... | collective-permute-start | bytes 786440 | tf_op jit(solution)/shard_map/ppermute | solution.py:414
  91.3 32.9 %collective-permute-start.26 = (bf16[64,2048]{1,0:T(8,128)(2,1)}, bf16[64,2048]{1,0:T(8,128)(2,1)S(1)}, u32[]{:S(2)}, u32[]{:S(2)}) collective-permute-start(bf16[64,2048]{1,0:T(8,128)(2,1)} %get-tuple-element.454), channel_id=1, source_target_pairs={{0,1},{1,2},{2,3},{3,0},{4,5},{5,6},{6,7},{7,4},{8,9},{9,10},{10,1... | collective-permute-start | bytes 786440 | tf_op jit(solution)/shard_map/ppermute | solution.py:414
  91.9 109.7 %collective-permute-start.37 = (bf16[64,2048]{1,0:T(8,128)(2,1)}, bf16[64,2048]{1,0:T(8,128)(2,1)S(1)}, u32[]{:S(2)}, u32[]{:S(2)}) collective-permute-start(bf16[64,2048]{1,0:T(8,128)(2,1)} %get-tuple-element.449), channel_id=1, source_target_pairs={{0,3},{1,0},{2,1},{3,2},{4,7},{5,4},{6,5},{7,6},{8,11},{9,8},{10,9... | collective-permute-start | bytes 786440 | tf_op jit(solution)/shard_map/ppermute | solution.py:414
  96.9 105.6 %collective-permute-start.38 = (bf16[64,2048]{1,0:T(8,128)(2,1)}, bf16[64,2048]{1,0:T(8,128)(2,1)S(1)}, u32[]{:S(2)}, u32[]{:S(2)}) collective-permute-start(bf16[64,2048]{1,0:T(8,128)(2,1)} %get-tuple-element.448), channel_id=1, source_target_pairs={{0,2},{1,3},{2,0},{3,1},{4,6},{5,7},{6,4},{7,5},{8,10},{9,11},{10,... | collective-permute-start | bytes 786440 | tf_op jit(solution)/shard_map/ppermute | solution.py:414
  105.7 101.9 %collective-permute-start.39 = (bf16[64,2048]{1,0:T(8,128)(2,1)}, bf16[64,2048]{1,0:T(8,128)(2,1)S(1)}, u32[]{:S(2)}, u32[]{:S(2)}) collective-permute-start(bf16[64,2048]{1,0:T(8,128)(2,1)} %get-tuple-element.447), channel_id=1, source_target_pairs={{0,1},{1,2},{2,3},{3,0},{4,5},{5,6},{6,7},{7,4},{8,9},{9,10},{10,1... | collective-permute-start | bytes 786440 | tf_op jit(solution)/shard_map/ppermute | solution.py:414
  206.4 23.5 collective-permute-start.6
  230.5 15.7 collective-permute-start.19
  233.9 22.1 collective-permute-start.10
  259.0 14.9 collective-permute-start.11
  261.3 21.4 collective-permute-start.20
  283.3 31.1 %collective-permute-start.21 = (bf16[2,128,2048]{2,1,0:T(8,128)(2,1)S(1)}, bf16[2,128,2048]{2,1,0:T(8,128)(2,1)}, u32[]{:S(2)}, u32[]{:S(2)}) collective-permute-start(bf16[2,128,2048]{2,1,0:T(8,128)(2,1)S(1)} %pad_maximum_fusion.23), channel_id=1, source_target_pairs={{0,4},{4,0},{8,12},{12,8},{1,5},{5,1},{9,13},{13,9},{2,6},{6,2},{1... | collective-permute-start | bytes 3145736 | tf_op jit(solution)/shard_map/ppermute | solution.py:420
  317.1 22.6 collective-permute-start.16
  340.9 16.0 collective-permute-start.27
  359.4 14.9 collective-permute-start.28
  360.4 23.4 collective-permute-start.23
  385.0 35.1 %collective-permute-start.32 = (bf16[128,2048]{1,0:T(8,128)(2,1)S(1)}, bf16[128,2048]{1,0:T(8,128)(2,1)S(1)}, u32[]{:S(2)}, u32[]{:S(2)}) collective-permute-start(bf16[128,2048]{1,0:T(8,128)(2,1)S(1)} %get-tuple-element.349), channel_id=1, source_target_pairs={{0,16},{1,17},{2,18},{3,19},{4,20},{5,21},{6,22},{7,23},{8,24},{9,... | collective-permute-start | bytes 1572872 | tf_op jit(solution)/shard_map/ppermute | solution.py:532
  424.5 24.7 collective-permute-start.33
  467.7 31.0 %collective-permute-start.42 = (bf16[2,128,2048]{2,1,0:T(8,128)(2,1)S(1)}, bf16[2,128,2048]{2,1,0:T(8,128)(2,1)S(1)}, u32[]{:S(2)}, u32[]{:S(2)}) collective-permute-start(bf16[2,128,2048]{2,1,0:T(8,128)(2,1)S(1)} %pad_maximum_fusion.26), channel_id=1, source_target_pairs={{0,4},{4,0},{8,12},{12,8},{1,5},{5,1},{9,13},{13,9},{2,6},{6,2},{1... | collective-permute-start | bytes 3145736 | tf_op jit(solution)/shard_map/ppermute | solution.py:420
  498.2 30.1 %collective-permute-start.35 = (bf16[2,128,2048]{2,1,0:T(8,128)(2,1)S(1)}, bf16[2,128,2048]{2,1,0:T(8,128)(2,1)S(1)}, u32[]{:S(2)}, u32[]{:S(2)}) collective-permute-start(bf16[2,128,2048]{2,1,0:T(8,128)(2,1)S(1)} %dynamic-slice_bitcast_fusion.21), channel_id=1, source_target_pairs={{0,4},{4,0},{8,12},{12,8},{1,5},{5,1},{9,13},{13,9},{2,6},{6,2},{1... | collective-permute-start | bytes 3145736 | tf_op jit(solution)/shard_map/ppermute | solution.py:420
  529.6 15.0 collective-permute-start.36
  533.5 22.5 collective-permute-start.44
  534.2 32.8 %collective-permute-start.65 = (bf16[128,2048]{1,0:T(8,128)(2,1)S(1)}, bf16[128,2048]{1,0:T(8,128)(2,1)S(1)}, u32[]{:S(2)}, u32[]{:S(2)}) collective-permute-start(bf16[128,2048]{1,0:T(8,128)(2,1)S(1)} %bitcast.913), channel_id=1, source_target_pairs={{0,8},{4,12},{8,0},{12,4},{1,9},{5,13},{9,1},{13,5},{2,10},{6,14},... | collective-permute-start | bytes 1572872 | tf_op jit(solution)/shard_map/ppermute | solution.py:424
  535.5 42.4 %collective-permute-start.63 = (bf16[128,2048]{1,0:T(8,128)(2,1)S(1)}, bf16[128,2048]{1,0:T(8,128)(2,1)S(1)}, u32[]{:S(2)}, u32[]{:S(2)}) collective-permute-start(bf16[128,2048]{1,0:T(8,128)(2,1)S(1)} %bitcast.914), channel_id=1, source_target_pairs={{0,8},{4,12},{8,0},{12,4},{1,9},{5,13},{9,1},{13,5},{2,10},{6,14},... | collective-permute-start | bytes 1572872 | tf_op jit(solution)/shard_map/ppermute | solution.py:424
  547.3 20.0 collective-permute-start.45
  558.1 15.3 collective-permute-start.50
  567.3 23.0 collective-permute-start.66
  629.3 24.3 collective-permute-start.51
  673.1 29.1 %collective-permute-start.57 = (bf16[2,128,2048]{2,1,0:T(8,128)(2,1)S(1)}, bf16[2,128,2048]{2,1,0:T(8,128)(2,1)S(1)}, u32[]{:S(2)}, u32[]{:S(2)}) collective-permute-start(bf16[2,128,2048]{2,1,0:T(8,128)(2,1)S(1)} %pad_maximum_fusion.29), channel_id=1, source_target_pairs={{0,4},{4,0},{8,12},{12,8},{1,5},{5,1},{9,13},{13,9},{2,6},{6,2},{1... | collective-permute-start | bytes 3145736 | tf_op jit(solution)/shard_map/ppermute | solution.py:420
  788.7 24.0 collective-permute-start.73
  813.7 16.9 collective-permute-start.74
  815.9 24.6 collective-permute-start.69
  855.0 19.5 collective-permute-start.71
  921.2 24.0 collective-permute-start.80
  948.6 16.7 collective-permute-start.84
  949.9 25.3 collective-permute-start.81
  990.7 19.4 collective-permute-start.83
  1055.5 24.0 collective-permute-start.90
  1082.9 16.7 collective-permute-start.94
  1084.2 25.3 collective-permute-start.91
  1124.0 19.5 collective-permute-start.93
  1190.3 24.0 collective-permute-start.100
  1217.6 16.7 collective-permute-start.104
  1218.9 25.2 collective-permute-start.101
  1245.6 23.3 collective-permute-start.102
  1270.1 20.7 collective-permute-start.103
  1506.8 23.1 collective-permute-start.59
  1532.2 63.3 %collective-permute-start.60 = (bf16[4,64,2048]{2,1,0:T(8,128)(2,1)S(1)}, bf16[4,64,2048]{2,1,0:T(8,128)(2,1)S(1)}, u32[]{:S(2)}, u32[]{:S(2)}) collective-permute-start(bf16[4,64,2048]{2,1,0:T(8,128)(2,1)S(1)} %get-tuple-element.366), channel_id=1, source_target_pairs={{0,3},{1,0},{2,1},{3,2},{4,7},{5,4},{6,5},{7,6},{8,11},{9,8},{10,9... | collective-permute-start | bytes 3145736 | tf_op jit(solution)/shard_map/ppermute | solution.py:414
  1532.3 194.2 %collective-permute-start.61 = (bf16[4,64,2048]{2,1,0:T(8,128)(2,1)S(1)}, bf16[4,64,2048]{2,1,0:T(8,128)(2,1)S(1)}, u32[]{:S(2)}, u32[]{:S(2)}) collective-permute-start(bf16[4,64,2048]{2,1,0:T(8,128)(2,1)S(1)} %get-tuple-element.365), channel_id=1, source_target_pairs={{0,2},{1,3},{2,0},{3,1},{4,6},{5,7},{6,4},{7,5},{8,10},{9,11},{10,... | collective-permute-start | bytes 3145736 | tf_op jit(solution)/shard_map/ppermute | solution.py:414
  1533.2 199.8 %collective-permute-start.62 = (bf16[4,64,2048]{2,1,0:T(8,128)(2,1)S(1)}, bf16[4,64,2048]{2,1,0:T(8,128)(2,1)S(1)}, u32[]{:S(2)}, u32[]{:S(2)}) collective-permute-start(bf16[4,64,2048]{2,1,0:T(8,128)(2,1)S(1)} %get-tuple-element.364), channel_id=1, source_target_pairs={{0,1},{1,2},{2,3},{3,0},{4,5},{5,6},{6,7},{7,4},{8,9},{9,10},{10,1... | collective-permute-start | bytes 3145736 | tf_op jit(solution)/shard_map/ppermute | solution.py:414
  1546.1 180.4 %collective-permute-start.107 = (bf16[2,128,2048]{2,1,0:T(8,128)(2,1)S(1)}, bf16[2,128,2048]{2,1,0:T(8,128)(2,1)S(1)}, u32[]{:S(2)}, u32[]{:S(2)}) collective-permute-start(bf16[2,128,2048]{2,1,0:T(8,128)(2,1)S(1)} %dynamic-slice_bitcast_fusion.5), channel_id=1, source_target_pairs={{0,4},{4,0},{8,12},{12,8},{1,5},{5,1},{9,13},{13,9},{2,6},{6,2},{1... | collective-permute-start | bytes 3145736 | tf_op jit(solution)/shard_map/ppermute | solution.py:420
  1596.6 133.0 %collective-permute-start.109 = (bf16[2,128,2048]{2,1,0:T(8,128)(2,1)S(1)}, bf16[2,128,2048]{2,1,0:T(8,128)(2,1)S(1)}, u32[]{:S(2)}, u32[]{:S(2)}) collective-permute-start(bf16[2,128,2048]{2,1,0:T(8,128)(2,1)S(1)} %dynamic-slice_bitcast_fusion.4), channel_id=1, source_target_pairs={{0,4},{4,0},{8,12},{12,8},{1,5},{5,1},{9,13},{13,9},{2,6},{6,2},{1... | collective-permute-start | bytes 3145736 | tf_op jit(solution)/shard_map/ppermute | solution.py:420
  1728.4 15.1 collective-permute-start.108
  1732.3 21.2 collective-permute-start.110
  1764.0 290.5 %collective-permute-start.111 = (bf16[4,64,2048]{2,1,0:T(8,128)(2,1)}, bf16[4,64,2048]{2,1,0:T(8,128)(2,1)S(1)}, u32[]{:S(2)}, u32[]{:S(2)}) collective-permute-start(bf16[4,64,2048]{2,1,0:T(8,128)(2,1)} %get-tuple-element.363), channel_id=1, source_target_pairs={{0,3},{1,0},{2,1},{3,2},{4,7},{5,4},{6,5},{7,6},{8,11},{9,8},{10,9... | collective-permute-start | bytes 3145736 | tf_op jit(solution)/shard_map/ppermute | solution.py:414
  1764.0 290.6 %collective-permute-start.112 = (bf16[4,64,2048]{2,1,0:T(8,128)(2,1)}, bf16[4,64,2048]{2,1,0:T(8,128)(2,1)S(1)}, u32[]{:S(2)}, u32[]{:S(2)}) collective-permute-start(bf16[4,64,2048]{2,1,0:T(8,128)(2,1)} %get-tuple-element.362), channel_id=1, source_target_pairs={{0,2},{1,3},{2,0},{3,1},{4,6},{5,7},{6,4},{7,5},{8,10},{9,11},{10,... | collective-permute-start | bytes 3145736 | tf_op jit(solution)/shard_map/ppermute | solution.py:414
  1973.0 81.7 %collective-permute-start.113 = (bf16[4,64,2048]{2,1,0:T(8,128)(2,1)}, bf16[4,64,2048]{2,1,0:T(8,128)(2,1)S(1)}, u32[]{:S(2)}, u32[]{:S(2)}) collective-permute-start(bf16[4,64,2048]{2,1,0:T(8,128)(2,1)} %get-tuple-element.361), channel_id=1, source_target_pairs={{0,1},{1,2},{2,3},{3,0},{4,5},{5,6},{6,7},{7,4},{8,9},{9,10},{10,1... | collective-permute-start | bytes 3145736 | tf_op jit(solution)/shard_map/ppermute | solution.py:414
  (199 other events, 3873.7 us)
Sparse Core Ops, SparseCore 0:
  1491.7 1018.2 all-reduce.3

commit v2 on v1

--- a/solution.py
+++ b/solution.py
@@ -219,20 +219,17 @@
     )(slot, *([qkv] * count), places_q, places_k, *extra)
 
 
-def combine_kernel(dims, slot, a, b, wa, wb, out):
-    out[...] = (dot(a[0], wa[...], dims) + dot(b[0], wb[...], dims)).astype(bf16)
-
-
-def combine(slot, a, b, wa, wb, transposed):
+def combine_kernel(slot, a, b, wa, wb, out):
+    out[...] = (dot(a[0], wa[...]) + dot(b[0], wb[...])).astype(bf16)
+
+
+def combine(slot, a, b, wa, wb):
     rows = a.shape[1]
-    width = wa.shape[0] if transposed else wa.shape[1]
+    width = wa.shape[1]
     wide = min(512, width)
-    if transposed:
-        weight_specs = [pl.BlockSpec((wide, w.shape[1]), lambda i, s: (i, 0)) for w in (wa, wb)]
-    else:
-        weight_specs = [pl.BlockSpec((w.shape[0], wide), lambda i, s: (0, i)) for w in (wa, wb)]
+    weight_specs = [pl.BlockSpec((w.shape[0], wide), lambda i, s: (0, i)) for w in (wa, wb)]
     return pl.pallas_call(
-        partial(combine_kernel, NT if transposed else NN),
+        combine_kernel,
         out_shape=jax.ShapeDtypeStruct((rows, width), bf16),
         grid_spec=pltpu.PrefetchScalarGridSpec(
             num_scalar_prefetch=1,
@@ -252,6 +249,47 @@
         ),
         name="combine",
     )(slot, a, b, wa, wb)
+
+
+def merge_kernel(slot, a, b, wa, wb, gains, std, out, vectors):
+    one = dot(a[0], wa[...], NT)
+    two = dot(b[0], wb[...], NT)
+    out[...] = (one * gains[0] + two * gains[1]).astype(bf16)
+    standard = std[0].astype(f32)
+    rows = (one * standard, one, two * standard, two)
+    vectors[...] = jnp.concatenate([jnp.sum(v, axis=0, keepdims=True) for v in rows])
+
+
+def merge(slot, a, b, wa, wb, gains, std):
+    rows, width = std.shape[1:]
+    wide = min(512, width)
+    return pl.pallas_call(
+        merge_kernel,
+        out_shape=[jax.ShapeDtypeStruct((rows, width), bf16), jax.ShapeDtypeStruct((4, width), f32)],
+        grid_spec=pltpu.PrefetchScalarGridSpec(
+            num_scalar_prefetch=1,
+            grid=(width // wide,),
+            in_specs=[
+                pl.BlockSpec((1, rows, a.shape[2]), lambda i, s: (s[0], 0, 0)),
+                pl.BlockSpec((1, rows, b.shape[2]), lambda i, s: (s[0], 0, 0)),
+                pl.BlockSpec((wide, wa.shape[1]), lambda i, s: (i, 0)),
+                pl.BlockSpec((wide, wb.shape[1]), lambda i, s: (i, 0)),
+                pl.BlockSpec((2, 1, wide), lambda i, s: (0, 0, i)),
+                pl.BlockSpec((1, rows, wide), lambda i, s: (s[0], 0, i)),
+            ],
+            out_specs=[
+                pl.BlockSpec((rows, wide), lambda i, s: (0, i)),
+                pl.BlockSpec((4, wide), lambda i, s: (0, i)),
+            ],
+        ),
+        compiler_params=params(),
+        cost_estimate=pl.CostEstimate(
+            flops=2 * rows * width * (a.shape[2] + b.shape[2]),
+            bytes_accessed=2 * width * (a.shape[2] + b.shape[2]) + 6 * rows * width,
+            transcendentals=0,
+        ),
+        name="merge",
+    )(slot, a, b, wa, wb, gains, std)
 
 
 def spread_kernel(slot, gy, wo, wd, dg, *rest):
@@ -405,6 +443,324 @@
     )(slot, qkv, qkv, qkv, dctx, ctx, lse, places_q, places_k, *table, *more, *extra)
 
 
+CHUNK = 256
+PIECE = 64
+SKEW = 2
+
+
+def reduce_kernel(
+    plan, act, ctx, dproj, dhid, gy, std, gains, biases, sums, small, out, small_out, from_left, from_right,
+    rhs, raw, lhs, own, inbox, outbox, stage, small_in,
+    rhs_sem, raw_sem, right_sem, left_sem, final_sem, load_sem, sent, stage_left, stage_right, out_sem,
+    small_sent, small_got,
+):
+    bounds, tasks, count, piece, skew, ring = plan
+    sources = (act, ctx, dproj, dhid)
+    total_chunks = bounds[-1]
+    per_chunk = CHUNK // piece
+    pieces = total_chunks * per_chunk
+    width = gy.shape[-1]
+    tile = width // per_chunk
+    block = raw.shape[2]
+    z = lax.axis_index("ctx")
+    last = count - 1
+    root = count // 2
+    turn_at = max(root, last - root)
+    low, high, middle = z < root, z > root, z == root
+
+    barrier = pltpu.get_barrier_semaphore()
+    for shift in range(1, count):
+        pl.semaphore_signal(
+            barrier,
+            inc=1,
+            device_id={"ctx": lax.rem(z + shift, count)},
+            device_id_type=pl.DeviceIdType.MESH,
+        )
+
+    def small_copy(source, target):
+        return pltpu.make_async_remote_copy(
+            src_ref=small,
+            dst_ref=small_in.at[source],
+            send_sem=small_sent.at[target],
+            recv_sem=small_got.at[source],
+            device_id={"ctx": target},
+            device_id_type=pl.DeviceIdType.MESH,
+        )
+
+    def rhs_copy(k):
+        return pltpu.make_async_copy((gy, std)[k].at[pl.ds(0, tasks)], rhs.at[k], rhs_sem.at[k])
+
+    def each_source(chunk, act_on):
+        for g, source in enumerate(sources):
+
+            @pl.when((chunk >= bounds[g]) & (chunk < bounds[g + 1]))
+            def _(g=g, source=source):
+                column = pl.multiple_of((chunk - bounds[g]) * CHUNK, CHUNK)
+                act_on(
+                    pltpu.make_async_copy(
+                        source.at[pl.ds(0, tasks), :, pl.ds(column, CHUNK)],
+                        raw.at[chunk % 2],
+                        raw_sem.at[chunk % 2],
+                    )
+                )
+
+    def take(chunk):
+        each_source(chunk, lambda copy: copy.wait())
+        for k in range(tasks):
+            lhs[:, k * block : (k + 1) * block] = raw[chunk % 2, k].T
+        each_source(chunk + 1, lambda copy: copy.start())
+
+    def multiply(chunk, part):
+        second = jnp.where(chunk >= bounds[2], 1, 0)
+        group = second + jnp.where(chunk >= bounds[3], 1, 0)
+        columns = pl.ds(pl.multiple_of(part * tile, tile), tile)
+        value = dot(lhs[:, :block], rhs[second, 0, :, columns])
+        for k in range(1, tasks):
+            value = value + dot(lhs[:, k * block : (k + 1) * block], rhs[second, k, :, columns])
+        row = pl.multiple_of(chunk * CHUNK, CHUNK)
+        value = value * gains[group, :, columns] + sums[pl.ds(row, CHUNK), :] * biases[group, :, columns]
+        own[chunk % ring, :, columns] = value.astype(bf16)
+
+    def rows_of(index):
+        return pl.ds(pl.multiple_of(index * piece, piece), piece)
+
+    def own_piece(index):
+        inner = pl.multiple_of((index % per_chunk) * piece, piece)
+        return own[(index // per_chunk) % ring, pl.ds(inner, piece), :]
+
+    def remote(source, target_rows, send_sem, recv_sem, target):
+        return pltpu.make_async_remote_copy(
+            src_ref=source,
+            dst_ref=target_rows,
+            send_sem=send_sem,
+            recv_sem=recv_sem,
+            device_id={"ctx": target},
+            device_id_type=pl.DeviceIdType.MESH,
+        )
+
+    def inward(index, right):
+        landing, arrived, target = (from_left, right_sem, z + 1) if right else (from_right, left_sem, z - 1)
+        return remote(
+            outbox.at[index % 2], landing.at[rows_of(index)], sent.at[index % 2], arrived.at[index], target
+        )
+
+    def announce(index, right):
+        return remote(
+            stage.at[index % 2],
+            out.at[rows_of(index)],
+            (stage_right if right else stage_left).at[index % 2],
+            final_sem.at[index],
+            z + 1 if right else z - 1,
+        )
+
+    def onward(index, right):
+        return remote(
+            out.at[rows_of(index)],
+            out.at[rows_of(index)],
+            sent.at[2 + index % 2],
+            final_sem.at[index],
+            z + 1 if right else z - 1,
+        )
+
+    def load(index, right):
+        landing = from_left if right else from_right
+        return pltpu.make_async_copy(
+            landing.at[rows_of(index)], inbox.at[0 if right else 1], load_sem.at[0 if right else 1]
+        )
+
+    def valid(index):
+        return (index >= 0) & (index < pieces)
+
+    def side(step, right):
+        mine = low if right else high
+        hops = z if right else last - z
+        inner = step - hops * skew
+        comes = hops > 0
+
+        @pl.when(mine & valid(inner) & comes)
+        def _():
+            inward(inner, right).wait_recv()
+            load(inner, right).start()
+
+        @pl.when(mine & valid(inner))
+        def _():
+            @pl.when(inner >= 2)
+            def _():
+                inward(inner - 2, right).wait_send()
+
+            @pl.when(comes)
+            def _():
+                load(inner, right).wait()
+                value = own_piece(inner).astype(f32) + inbox[0 if right else 1].astype(f32)
+                outbox[inner % 2] = value.astype(bf16)
+
+            @pl.when(jnp.logical_not(comes))
+            def _():
+                outbox[inner % 2] = own_piece(inner)
+
+            inward(inner, right).start()
+
+        away = root - z if right else z - root
+        outer = step - (turn_at + away) * skew
+
+        @pl.when(mine & valid(outer))
+        def _():
+            onward(outer, not right).wait_recv()
+
+            @pl.when(comes)
+            def _():
+                @pl.when(outer >= 2)
+                def _():
+                    onward(outer - 2, not right).wait_send()
+
+                onward(outer, not right).start()
+
+    def out_copy(index):
+        return pltpu.make_async_copy(stage.at[index % 2], out.at[rows_of(index)], out_sem.at[index % 2])
+
+    def stage_done(index):
+        out_copy(index).wait()
+        announce(index, False).wait_send()
+        if root < last:
+            announce(index, True).wait_send()
+
+    def centre(step):
+        index = step - turn_at * skew
+
+        @pl.when(middle & valid(index))
+        def _():
+            inward(index, True).wait_recv()
+            load(index, True).start()
+            if root < last:
+                inward(index, False).wait_recv()
+                load(index, False).start()
+
+            @pl.when(index >= 2)
+            def _():
+                stage_done(index - 2)
+
+            load(index, True).wait()
+            value = own_piece(index).astype(f32) + inbox[0].astype(f32)
+            if root < last:
+                load(index, False).wait()
+                value = value + inbox[1].astype(f32)
+            stage[index % 2] = value.astype(bf16)
+            announce(index, False).start()
+            if root < last:
+                announce(index, True).start()
+            out_copy(index).start()
+
+    rhs_copy(0).start()
+    each_source(0, lambda copy: copy.start())
+    rhs_copy(1).start()
+    take(0)
+    rhs_copy(0).wait()
+
+    @pl.loop(0, per_chunk)
+    def _(part):
+        multiply(0, part)
+
+    pl.semaphore_wait(barrier, count - 1)
+    small_in[z] = small[...]
+    for shift in range(1, count):
+        small_copy(z, lax.rem(z + shift, count)).start()
+
+    @pl.loop(0, pieces + (turn_at + max(root, last - root)) * skew)
+    def _(step):
+        side(step, True)
+        side(step, False)
+        centre(step)
+        chunk, part = step // per_chunk + 1, step % per_chunk
+
+        @pl.when(chunk < total_chunks)
+        def _():
+            @pl.when(part == 0)
+            def _():
+                take(chunk)
+
+                @pl.when(chunk == bounds[2])
+                def _():
+                    rhs_copy(1).wait()
+
+            multiply(chunk, part)
+
+    for shift in range(1, count):
+        other = lax.rem(z + shift, count)
+        small_copy(z, other).wait_send()
+        small_copy(other, other).wait_recv()
+    value = small_in[0]
+    for k in range(1, count):
+        value = value + small_in[k]
+    small_out[...] = value
+    for back in (2, 1):
+        for right in (True, False):
+
+            @pl.when(low if right else high)
+            def _(right=right, back=back):
+                inward(pieces - back, right).wait_send()
+
+                @pl.when((z > 0) & (z < last))
+                def _():
+                    onward(pieces - back, not right).wait_send()
+
+        @pl.when(middle)
+        def _(back=back):
+            stage_done(pieces - back)
+
+
+def reduce_gradients(act, ctx, dproj, dhid, gy, std, gains, biases, sums, small, tasks):
+    count = lax.axis_size("ctx")
+    block, width = gy.shape[1:]
+    bounds = [0]
+    for source in (act, ctx, dproj, dhid):
+        bounds.append(bounds[-1] + source.shape[2] // CHUNK)
+    total = bounds[-1] * CHUNK
+    pieces = total // PIECE
+    ring = count // 2 * SKEW // (CHUNK // PIECE) + 3
+    plan = (tuple(bounds), tasks, count, PIECE, SKEW, ring)
+    anywhere = pl.BlockSpec(memory_space=pl.ANY)
+    vmem = pl.BlockSpec(memory_space=pltpu.VMEM)
+    result = jax.ShapeDtypeStruct((total, width), bf16)
+    out, small_out, _, _ = pl.pallas_call(
+        partial(reduce_kernel, plan),
+        out_shape=[result, jax.ShapeDtypeStruct(small.shape, f32), result, result],
+        in_specs=[anywhere] * 6 + [vmem] * 4,
+        out_specs=[anywhere, vmem, anywhere, anywhere],
+        scratch_shapes=[
+            pltpu.VMEM((2, tasks, block, width), bf16),
+            pltpu.VMEM((2, tasks, block, CHUNK), bf16),
+            pltpu.VMEM((CHUNK, tasks * block), bf16),
+            pltpu.VMEM((ring, CHUNK, width), bf16),
+            pltpu.VMEM((2, PIECE, width), bf16),
+            pltpu.VMEM((2, PIECE, width), bf16),
+            pltpu.VMEM((2, PIECE, width), bf16),
+            pltpu.VMEM((count,) + small.shape, f32),
+            pltpu.SemaphoreType.DMA((2,)),
+            pltpu.SemaphoreType.DMA((2,)),
+            pltpu.SemaphoreType.DMA((pieces,)),
+            pltpu.SemaphoreType.DMA((pieces,)),
+            pltpu.SemaphoreType.DMA((pieces,)),
+            pltpu.SemaphoreType.DMA((2,)),
+            pltpu.SemaphoreType.DMA((4,)),
+            pltpu.SemaphoreType.DMA((2,)),
+            pltpu.SemaphoreType.DMA((2,)),
+            pltpu.SemaphoreType.DMA((2,)),
+            pltpu.SemaphoreType.DMA((count,)),
+            pltpu.SemaphoreType.DMA((count,)),
+        ],
+        compiler_params=pltpu.CompilerParams(
+            collective_id=7, has_side_effects=True, vmem_limit_bytes=60 * 1024 * 1024
+        ),
+        cost_estimate=pl.CostEstimate(
+            flops=2 * total * width * tasks * block,
+            bytes_accessed=8 * total * width,
+            transcendentals=0,
+        ),
+        name="reduce_gradients",
+    )(act, ctx, dproj, dhid, gy, std, gains, biases, sums, small)
+    return out, small_out
+
+
 def exchange(blocks, axis):
     count = blocks.shape[0]
     me = lax.axis_index(axis)
@@ -525,7 +881,7 @@
         attend_buffers = attend(
             slot, forward_buffers[0], places_q, places_k, heads, part == 1, attend_buffers
         )
-        summed = scatter_sum(combine(slot, attend_buffers[0], forward_buffers[2], wo, wd, False), tensor)
+        summed = scatter_sum(combine(slot, attend_buffers[0], forward_buffers[2], wo, wd), tensor)
         result = (x_own.astype(f32) + summed + out_bias).astype(bf16)
         produced.append(result)
         if step < tasks:
@@ -538,7 +894,8 @@
     spread_buffers = None
     dproj_all = None
     carry = None
-    bias_total = jnp.zeros((width,), f32)
+    vectors = jnp.zeros((5, width), f32)
+    gain_pair = jnp.stack([gain_one, gain_two])[:, None]
     for step in range(tasks + LAG):
         part = 1 - step % 2
         task_first = max(step - LAG, 0)
@@ -568,7 +925,8 @@
         )
         dproj_all = made[0]
         carry = tuple(made[1:]) if part == 1 else None
-        e = scatter_sum(combine(slot, dproj_all, spread_buffers[1], wq_scaled, wi_scaled, True), tensor)
+        e_part, vector_part = merge(slot, dproj_all, spread_buffers[1], wq, wi, gain_pair, std_all)
+        e = scatter_sum(e_part, tensor)
         x_own = jnp.where(first, kept[near], kept[far + LAG])
         standard, inverse = standardize(x_own)
         gy_wide = gy_own.astype(f32)
@@ -579,37 +937,41 @@
         )
         back_list.append(d_input)
         valid = jnp.where(first, step >= LAG, step < tasks)
-        bias_total = bias_total + jnp.where(valid, jnp.sum(gy_wide, axis=0), 0.0)
+        vector_part = jnp.concatenate([vector_part, jnp.sum(gy_wide, axis=0, keepdims=True)])
+        vectors = vectors + jnp.where(valid, vector_part, 0.0)
         if step < tasks:
             back[step + LAG] = lax.ppermute(d_input.astype(bf16), "section", [(1, 0)])
     gy_all, dh_all = spread_buffers
 
-    def flat(v):
-        return v[:tasks].reshape(-1, v.shape[-1])
-
-    std_flat, gy_flat, dproj, dhidden = flat(std_all), flat(gy_all), flat(dproj_all), flat(dh_all)
-    g_one = dot(std_flat, dproj, TN)
-    g_two = dot(std_flat, dhidden, TN)
-    d_b_qkv = jnp.sum(dproj, axis=0, dtype=f32)
-    d_b_in = jnp.sum(dhidden, axis=0, dtype=f32)
-    d_w_qkv = gain_one[:, None] * g_one + bias_one[:, None] * d_b_qkv[None]
-    d_w_in = gain_two[:, None] * g_two + bias_two[:, None] * d_b_in[None]
-    d_w_out = dot(flat(ctx_all), gy_flat, TN)
-    d_w_down = dot(flat(act_all), gy_flat, TN)
-    wq_wide, wi_wide = wq.astype(f32), wi.astype(f32)
-    vectors = jnp.stack(
-        [
-            jnp.sum(wq_wide * g_one, axis=1),
-            jnp.sum(wq_wide * d_b_qkv[None], axis=1),
-            jnp.sum(wi_wide * g_two, axis=1),
-            jnp.sum(wi_wide * d_b_in[None], axis=1),
-            bias_total,
-        ]
+    d_b_qkv = jnp.sum(dproj_all[:tasks], axis=(0, 1), dtype=f32)
+    d_b_in = jnp.sum(dh_all[:tasks], axis=(0, 1), dtype=f32)
+    units, inner = wd.shape[0], wo.shape[0]
+    sums = jnp.concatenate([jnp.zeros((units + inner,), f32), d_b_qkv, d_b_in])[:, None]
+    gains = jnp.stack([jnp.ones_like(gain_one), gain_one, gain_two])[:, None]
+    biases = jnp.stack([jnp.zeros_like(bias_one), bias_one, bias_two])[:, None]
+    mask = 1
+    while mask < tensor:
+        vectors = vectors + lax.ppermute(vectors, "tensor", [(k, k ^ mask) for k in range(tensor)])
+        mask *= 2
+    sides = jnp.concatenate([d_b_qkv, d_b_in])
+    side_rows = -(-sides.shape[0] // width)
+    small = jnp.zeros((-(-(5 + side_rows) // 8) * 8, width), f32)
+    small = small.at[:5].set(vectors)
+    small = small.at[5 : 5 + side_rows].set(
+        jnp.pad(sides, (0, side_rows * width - sides.shape[0])).reshape(side_rows, width)
     )
-    vectors = lax.psum(vectors, ("tensor", "ctx"))
-    d_b_qkv, d_b_in = lax.psum((d_b_qkv, d_b_in), "ctx")
-    big = lax.psum(tuple(v.astype(bf16) for v in (d_w_qkv, d_w_out, d_w_in, d_w_down)), "ctx")
-    d_w_qkv, d_w_out, d_w_in, d_w_down = (v.astype(f32) for v in big)
+    summed, small = reduce_gradients(
+        act_all, ctx_all, dproj_all, dh_all, gy_all, std_all, gains, biases, sums, small, tasks
+    )
+    vectors = small[:5]
+    sides = small[5 : 5 + side_rows].reshape(-1)
+    d_b_qkv, d_b_in = sides[: d_b_qkv.shape[0]], sides[d_b_qkv.shape[0] : sides.shape[0]]
+    d_b_in = d_b_in[: wi.shape[1]]
+    d_w_down = summed[:units].astype(f32)
+    d_w_out = summed[units : units + inner].astype(f32)
+    summed = summed[units + inner :]
+    d_w_qkv = summed[: wq.shape[1]].T.astype(f32)
+    d_w_in = summed[wq.shape[1] :].T.astype(f32)
 
     def homeward(pieces):
         stacked = jnp.stack(pieces).reshape(per_device, ctx_count, rows, width)

time: 2570 us -> 2190 us (0.85)
  Pallas kernels: 590 us -> 1190 us
  waiting for transfers between devices: 1080 us -> 530 us
  blocking collectives: 198 us -> 0 us
  matrix products: 143 us -> 0 us
  other arithmetic: 289 us -> 200 us
    pallas_call x20 -> x21, Pallas kernels: 210 us -> 812 us  [the longest x1 593 us: reduce_gradients(): pl.pallas_call(partial(reduce_kernel, plan), out_shape=[result, jax.Shape...]
    psum x1 -> x0, waiting for transfers between devices: 420 us -> none  [body(): lax.psum(tuple((v.astype(bf16) for v in (d_w_qkv, d_w_out, d_w_in, d_w_do...]
    psum x2 -> x0, blocking collectives: 198 us -> none  [the longest x1 117 us: body(): vectors = lax.psum(vectors, ('tensor', 'ctx'))]
    dot_general x4 -> x0, matrix products: 143 us -> none  [dot(): return lax.dot_general(a, b, dims, preferred_element_type=f32)]
    ppermute x18, waiting for transfers between devices: 194 us -> 86.6 us  [exchange(): lax.ppermute(piece, axis, [(k, (k + shift) % count) for k in range(count)])]
    reduce_sum x12 -> x11, other arithmetic: 116 us -> 22.9 us  [the longest x9 9.16 us: body(): jnp.sum(gy_wide, axis=0, keepdims=True)]
    unnamed x343 -> x347, local copies, waits for them, and re-layouts: 75.2 us -> 100 us
  transfers between devices with their start and end apart: 115 -> 116, of which waited for: 65 -> 60; matrix products, arithmetic and copies ran while one was open for 11% -> 11% of each run, Pallas kernels for 13% -> 46%
where the time goes in v2:
time: 2190 us; the launch traced here: 2170 us
  Pallas kernels  1190 us (54%)
  waiting for transfers between devices  530 us (24%)
  other arithmetic  200 us (9%)
  local copies, waits for them, and re-layouts  135 us (6%)
  starting transfers between devices  109 us (5%)
    pallas_call x1, Pallas kernels, reduce_gradients(): pl.pallas_call(partial(reduce_kernel, plan), out_shape=[result, jax.Shape...  593 us
    ppermute x40, waiting for transfers between devices, shift_chips(): lax.ppermute(v, 'tensor', [(k, (k + 2 * shift) % tensor) for k in range(t...  322 us
    pallas_call x10, Pallas kernels, project(): pl.pallas_call(partial(project_kernel, heads, wide), out_shape=out_shape,...  157 us
    pallas_call x10, Pallas kernels, merge(): pl.pallas_call(merge_kernel, out_shape=[jax.ShapeDtypeStruct((rows, width...  128 us
    pallas_call x10, Pallas kernels, spread(): pl.pallas_call(spread_kernel, out_shape=out_shape, grid_spec=pltpu.Prefet...  117 us
    unnamed x347, local copies, waits for them, and re-layouts  100 us
    pallas_call x10, Pallas kernels, combine(): pl.pallas_call(combine_kernel, out_shape=jax.ShapeDtypeStruct((rows, widt...  91.3 us
    ppermute x18, waiting for transfers between devices, exchange(): lax.ppermute(piece, axis, [(k, (k + shift) % count) for k in range(count)])  86.6 us
  transfers between devices with their start and end apart: 116, of which 60 were waited for; matrix products, arithmetic and copies ran while one was open for 11% of the time, Pallas kernels for 46%

profile of v2, /device:TPU:0, one launch (start us, length us, event | category | flops | bytes accessed | tf_op | source)
XLA Modules:
  0.0 2171.7 jit_solution(9508618791473300534)
XLA Ops:
  0.7 16.2 fusion.2
  134.5 16.0 project.10
  163.7 15.6 project.11
  200.3 11.7 collective-permute-done.18
  212.1 10.4 collective-permute-done.6
  256.5 12.0 collective-permute-done.11
  279.2 15.6 project.12
  314.0 15.5 project.13
  358.2 12.3 collective-permute-done.28
  386.3 15.6 project.14
  423.7 11.3 collective-permute-done.31
  452.0 11.3 collective-permute-done.41
  464.0 15.8 project.15
  496.5 15.6 project.16
  530.1 12.0 collective-permute-done.36
  574.1 11.8 collective-permute-done.46
  589.7 15.6 project.17
  626.9 11.8 collective-permute-done.49
  658.3 10.7 collective-permute-done.56
  670.6 15.6 project.18
  699.9 15.6 project.19
  721.0 11.6 spread.10
  740.2 12.6 merge.11
  752.8 11.6 spread.11
  769.0 12.6 merge.10
  788.0 11.9 collective-permute-done.68
  800.3 10.3 collective-permute-done.73
  817.2 12.2 collective-permute-done.74
  842.8 10.1 collective-permute-done.70
  854.6 11.6 spread.12
  875.3 12.6 merge.13
  888.0 11.6 spread.13
  904.2 13.0 merge.12
  923.3 12.2 collective-permute-done.78
  935.9 10.3 collective-permute-done.80
  953.0 13.1 collective-permute-done.84
  980.4 11.3 collective-permute-done.82
  993.3 11.6 spread.14
  1012.6 12.6 merge.15
  1025.3 11.6 spread.15
  1041.5 12.8 merge.14
  1061.0 12.2 collective-permute-done.88
  1073.6 10.4 collective-permute-done.90
  1117.6 12.0 collective-permute-done.92
  1131.3 12.0 spread.16
  1151.0 12.6 merge.17
  1163.7 11.6 spread.17
  1179.9 12.9 merge.16
  1200.8 12.2 collective-permute-done.98
  1213.4 10.4 collective-permute-done.100
  1231.0 13.0 collective-permute-done.104
  1255.1 44.2 %collective-permute-done.61 = bf16[4,64,2048]{2,1,0:T(8,128)(2,1)S(1)} collective-permute-done((bf16[4,64,2048]{2,1,0:T(8,128)(2,1)S(1)}, bf16[4,64,2048]{2,1,0:T(8,128)(2,1)S(1)}, u32[]{:S(2)}, u32[]{:S(2)}) %collective-permute-start.61) | collective-permute-done | bytes 1048608 | tf_op jit(solution)/shard_map/ppermute | solution.py:770
  1300.7 12.6 collective-permute-done.102
  1314.1 11.6 spread.18
  1333.4 12.6 merge.19
  1346.1 12.4 spread.19
  1370.4 13.0 merge.18
  1400.7 592.9 %reduce_gradients.1 = (bf16[6144,2048]{1,0:T(8,128)(2,1)}, f32[8,2048]{1,0:T(8,128)}, bf16[6144,2048]{1,0:T(8,128)(2,1)}, bf16[6144,2048]{1,0:T(8,128)(2,1)}) custom-call(bf16[9,512,2048]{2,1,0:T(8,128)(2,1)} %get-tuple-element.221.b.act, bf16[9,512,512]{2,1,0:T(8,128)(2,1)} %get-tuple-element.220.a.refs_4_.ctx, bf16[9,512,1536]{2,1,0:T(8,128)(2,1)} %attend_back.19.a.dproj, ...), custom_call_target="tpu_custom_call" | custom-call | flops 103079215104 | bytes 100663296 | tf_op jit(solution)/shard_map/reduce_gradients/pallas_call | solution.py:724
  1993.6 17.0 bitcast_convert_fusion
  2016.4 11.0 collective-permute-done.108
  2056.3 19.2 copy.231
  2078.6 17.6 copy.232
  2097.7 33.6 %collective-permute-done.112 = bf16[4,64,2048]{2,1,0:T(8,128)(2,1)} collective-permute-done((bf16[4,64,2048]{2,1,0:T(8,128)(2,1)}, bf16[4,64,2048]{2,1,0:T(8,128)(2,1)}, u32[]{:S(2)}, u32[]{:S(2)}) %collective-permute-start.112) | collective-permute-done | bytes 1048608 | tf_op jit(solution)/shard_map/ppermute | solution.py:770
  2158.6 12.2 copy.230
  (952 shorter events, 712.0 us)
Async XLA Ops:
  21.1 48.5 %collective-permute-start = (bf16[64,2048]{1,0:T(8,128)(2,1)}, bf16[64,2048]{1,0:T(8,128)(2,1)}, u32[]{:S(2)}, u32[]{:S(2)}) collective-permute-start(bf16[64,2048]{1,0:T(8,128)(2,1)} %get-tuple-element.543), channel_id=1, source_target_pairs={{0,3},{1,0},{2,1},{3,2},{4,7},{5,4},{6,5},{7,6},{8,11},{9,8},{10,9... | collective-permute-start | bytes 786440 | tf_op jit(solution)/shard_map/ppermute | solution.py:770
  26.2 44.5 %collective-permute-start.1 = (bf16[64,2048]{1,0:T(8,128)(2,1)}, bf16[64,2048]{1,0:T(8,128)(2,1)}, u32[]{:S(2)}, u32[]{:S(2)}) collective-permute-start(bf16[64,2048]{1,0:T(8,128)(2,1)} %get-tuple-element.542), channel_id=1, source_target_pairs={{0,2},{1,3},{2,0},{3,1},{4,6},{5,7},{6,4},{7,5},{8,10},{9,11},{10,... | collective-permute-start | bytes 786440 | tf_op jit(solution)/shard_map/ppermute | solution.py:770
  26.2 49.3 %collective-permute-start.2 = (bf16[64,2048]{1,0:T(8,128)(2,1)}, bf16[64,2048]{1,0:T(8,128)(2,1)}, u32[]{:S(2)}, u32[]{:S(2)}) collective-permute-start(bf16[64,2048]{1,0:T(8,128)(2,1)} %get-tuple-element.541), channel_id=1, source_target_pairs={{0,1},{1,2},{2,3},{3,0},{4,5},{5,6},{6,7},{7,4},{8,9},{9,10},{10,1... | collective-permute-start | bytes 786440 | tf_op jit(solution)/shard_map/ppermute | solution.py:770
  28.2 59.8 %collective-permute-start.7 = (bf16[64,2048]{1,0:T(8,128)(2,1)}, bf16[64,2048]{1,0:T(8,128)(2,1)S(1)}, u32[]{:S(2)}, u32[]{:S(2)}) collective-permute-start(bf16[64,2048]{1,0:T(8,128)(2,1)} %get-tuple-element.538), channel_id=1, source_target_pairs={{0,3},{1,0},{2,1},{3,2},{4,7},{5,4},{6,5},{7,6},{8,11},{9,8},{10,9... | collective-permute-start | bytes 786440 | tf_op jit(solution)/shard_map/ppermute | solution.py:770
  31.1 61.7 %collective-permute-start.8 = (bf16[64,2048]{1,0:T(8,128)(2,1)}, bf16[64,2048]{1,0:T(8,128)(2,1)S(1)}, u32[]{:S(2)}, u32[]{:S(2)}) collective-permute-start(bf16[64,2048]{1,0:T(8,128)(2,1)} %get-tuple-element.537), channel_id=1, source_target_pairs={{0,2},{1,3},{2,0},{3,1},{4,6},{5,7},{6,4},{7,5},{8,10},{9,11},{10,... | collective-permute-start | bytes 786440 | tf_op jit(solution)/shard_map/ppermute | solution.py:770
  69.6 24.5 %collective-permute-start.9 = (bf16[64,2048]{1,0:T(8,128)(2,1)}, bf16[64,2048]{1,0:T(8,128)(2,1)}, u32[]{:S(2)}, u32[]{:S(2)}) collective-permute-start(bf16[64,2048]{1,0:T(8,128)(2,1)} %get-tuple-element.536), channel_id=1, source_target_pairs={{0,1},{1,2},{2,3},{3,0},{4,5},{5,6},{6,7},{7,4},{8,9},{9,10},{10,1... | collective-permute-start | bytes 786440 | tf_op jit(solution)/shard_map/ppermute | solution.py:770
  70.7 17.9 collective-permute-start.24
  75.5 28.4 %collective-permute-start.25 = (bf16[64,2048]{1,0:T(8,128)(2,1)}, bf16[64,2048]{1,0:T(8,128)(2,1)}, u32[]{:S(2)}, u32[]{:S(2)}) collective-permute-start(bf16[64,2048]{1,0:T(8,128)(2,1)} %get-tuple-element.528), channel_id=1, source_target_pairs={{0,2},{1,3},{2,0},{3,1},{4,6},{5,7},{6,4},{7,5},{8,10},{9,11},{10,... | collective-permute-start | bytes 786440 | tf_op jit(solution)/shard_map/ppermute | solution.py:770
  87.9 18.4 collective-permute-start.26
  88.6 105.5 %collective-permute-start.37 = (bf16[64,2048]{1,0:T(8,128)(2,1)}, bf16[64,2048]{1,0:T(8,128)(2,1)}, u32[]{:S(2)}, u32[]{:S(2)}) collective-permute-start(bf16[64,2048]{1,0:T(8,128)(2,1)} %get-tuple-element.522), channel_id=1, source_target_pairs={{0,3},{1,0},{2,1},{3,2},{4,7},{5,4},{6,5},{7,6},{8,11},{9,8},{10,9... | collective-permute-start | bytes 786440 | tf_op jit(solution)/shard_map/ppermute | solution.py:770
  92.9 102.4 %collective-permute-start.38 = (bf16[64,2048]{1,0:T(8,128)(2,1)}, bf16[64,2048]{1,0:T(8,128)(2,1)S(1)}, u32[]{:S(2)}, u32[]{:S(2)}) collective-permute-start(bf16[64,2048]{1,0:T(8,128)(2,1)} %get-tuple-element.521), channel_id=1, source_target_pairs={{0,2},{1,3},{2,0},{3,1},{4,6},{5,7},{6,4},{7,5},{8,10},{9,11},{10,... | collective-permute-start | bytes 786440 | tf_op jit(solution)/shard_map/ppermute | solution.py:770
  94.1 106.2 %collective-permute-start.39 = (bf16[64,2048]{1,0:T(8,128)(2,1)}, bf16[64,2048]{1,0:T(8,128)(2,1)S(1)}, u32[]{:S(2)}, u32[]{:S(2)}) collective-permute-start(bf16[64,2048]{1,0:T(8,128)(2,1)} %get-tuple-element.520), channel_id=1, source_target_pairs={{0,1},{1,2},{2,3},{3,0},{4,5},{5,6},{6,7},{7,4},{8,9},{9,10},{10,1... | collective-permute-start | bytes 786440 | tf_op jit(solution)/shard_map/ppermute | solution.py:770
  106.4 21.7 collective-permute-start.13
  131.1 284.2 %collective-permute-start.65 = (bf16[128,2048]{1,0:T(8,128)(2,1)}, bf16[128,2048]{1,0:T(8,128)(2,1)}, u32[]{:S(2)}, u32[]{:S(2)}) collective-permute-start(bf16[128,2048]{1,0:T(8,128)(2,1)} %bitcast.46), channel_id=1, source_target_pairs={{0,8},{4,12},{8,0},{12,4},{1,9},{5,13},{9,1},{13,5},{2,10},{6,14},... | collective-permute-start | bytes 1572872 | tf_op jit(solution)/shard_map/ppermute | solution.py:780
  133.2 392.4 %collective-permute-start.63 = (bf16[128,2048]{1,0:T(8,128)(2,1)}, bf16[128,2048]{1,0:T(8,128)(2,1)}, u32[]{:S(2)}, u32[]{:S(2)}) collective-permute-start(bf16[128,2048]{1,0:T(8,128)(2,1)} %bitcast.9), channel_id=1, source_target_pairs={{0,8},{4,12},{8,0},{12,4},{1,9},{5,13},{9,1},{13,5},{2,10},{6,14},... | collective-permute-start | bytes 1572872 | tf_op jit(solution)/shard_map/ppermute | solution.py:780
  199.1 23.4 %collective-permute-start.6 = (bf16[128,2048]{1,0:T(8,128)(2,1)S(1)}, bf16[128,2048]{1,0:T(8,128)(2,1)S(1)}, u32[]{:S(2)}, u32[]{:S(2)}) collective-permute-start(bf16[128,2048]{1,0:T(8,128)(2,1)S(1)} %fusion.159), channel_id=1, source_target_pairs={{0,8},{4,12},{8,0},{12,4},{1,9},{5,13},{9,1},{13,5},{2,10},{6,14},... | collective-permute-start | bytes 1572872 | tf_op jit(solution)/shard_map/ppermute | solution.py:780
  224.2 15.8 collective-permute-start.19
  227.6 21.8 %collective-permute-start.10 = (bf16[128,2048]{1,0:T(8,128)(2,1)S(1)}, bf16[128,2048]{1,0:T(8,128)(2,1)S(1)}, u32[]{:S(2)}, u32[]{:S(2)}) collective-permute-start(bf16[128,2048]{1,0:T(8,128)(2,1)S(1)} %get-tuple-element.563), channel_id=1, source_target_pairs={{0,16},{1,17},{2,18},{3,19},{4,20},{5,21},{6,22},{7,23},{8,24},{9,... | collective-permute-start | bytes 1572872 | tf_op jit(solution)/shard_map/ppermute | solution.py:888
  253.5 14.9 collective-permute-start.11
  255.8 21.3 collective-permute-start.20
  278.6 31.2 %collective-permute-start.21 = (bf16[2,128,2048]{2,1,0:T(8,128)(2,1)}, bf16[2,128,2048]{2,1,0:T(8,128)(2,1)}, u32[]{:S(2)}, u32[]{:S(2)}) collective-permute-start(bf16[2,128,2048]{2,1,0:T(8,128)(2,1)} %pad_maximum_fusion.23), channel_id=1, source_target_pairs={{0,4},{4,0},{8,12},{12,8},{1,5},{5,1},{9,13},{13,9},{2,6},{6,2},{1... | collective-permute-start | bytes 3145736 | tf_op jit(solution)/shard_map/ppermute | solution.py:776
  312.5 22.5 %collective-permute-start.16 = (bf16[128,2048]{1,0:T(8,128)(2,1)S(1)}, bf16[128,2048]{1,0:T(8,128)(2,1)S(1)}, u32[]{:S(2)}, u32[]{:S(2)}) collective-permute-start(bf16[128,2048]{1,0:T(8,128)(2,1)S(1)} %fusion.160), channel_id=1, source_target_pairs={{0,8},{4,12},{8,0},{12,4},{1,9},{5,13},{9,1},{13,5},{2,10},{6,14},... | collective-permute-start | bytes 1572872 | tf_op jit(solution)/shard_map/ppermute | solution.py:780
  336.2 15.9 collective-permute-start.27
  355.6 14.9 collective-permute-start.28
  356.7 23.4 %collective-permute-start.23 = (bf16[128,2048]{1,0:T(8,128)(2,1)S(1)}, bf16[128,2048]{1,0:T(8,128)(2,1)S(1)}, u32[]{:S(2)}, u32[]{:S(2)}) collective-permute-start(bf16[128,2048]{1,0:T(8,128)(2,1)S(1)} %fusion.162), channel_id=1, source_target_pairs={{0,8},{4,12},{8,0},{12,4},{1,9},{5,13},{9,1},{13,5},{2,10},{6,14},... | collective-permute-start | bytes 1572872 | tf_op jit(solution)/shard_map/ppermute | solution.py:780
  381.3 35.3 %collective-permute-start.32 = (bf16[128,2048]{1,0:T(8,128)(2,1)S(1)}, bf16[128,2048]{1,0:T(8,128)(2,1)S(1)}, u32[]{:S(2)}, u32[]{:S(2)}) collective-permute-start(bf16[128,2048]{1,0:T(8,128)(2,1)S(1)} %get-tuple-element.423), channel_id=1, source_target_pairs={{0,16},{1,17},{2,18},{3,19},{4,20},{5,21},{6,22},{7,23},{8,24},{9,... | collective-permute-start | bytes 1572872 | tf_op jit(solution)/shard_map/ppermute | solution.py:888
  421.2 24.6 %collective-permute-start.33 = (bf16[128,2048]{1,0:T(8,128)(2,1)S(1)}, bf16[128,2048]{1,0:T(8,128)(2,1)S(1)}, u32[]{:S(2)}, u32[]{:S(2)}) collective-permute-start(bf16[128,2048]{1,0:T(8,128)(2,1)S(1)} %fusion.98), channel_id=1, source_target_pairs={{0,8},{4,12},{8,0},{12,4},{1,9},{5,13},{9,1},{13,5},{2,10},{6,14},... | collective-permute-start | bytes 1572872 | tf_op jit(solution)/shard_map/ppermute | solution.py:780
  423.7 134.9 %collective-permute-start.66 = (bf16[2,128,2048]{2,1,0:T(8,128)(2,1)}, bf16[2,128,2048]{2,1,0:T(8,128)(2,1)}, u32[]{:S(2)}, u32[]{:S(2)}) collective-permute-start(bf16[2,128,2048]{2,1,0:T(8,128)(2,1)} %pad_maximum_fusion.31), channel_id=1, source_target_pairs={{0,4},{4,0},{8,12},{12,8},{1,5},{5,1},{9,13},{13,9},{2,6},{6,2},{1... | collective-permute-start | bytes 3145736 | tf_op jit(solution)/shard_map/ppermute | solution.py:776
  463.9 32.0 %collective-permute-start.42 = (bf16[2,128,2048]{2,1,0:T(8,128)(2,1)S(1)}, bf16[2,128,2048]{2,1,0:T(8,128)(2,1)S(1)}, u32[]{:S(2)}, u32[]{:S(2)}) collective-permute-start(bf16[2,128,2048]{2,1,0:T(8,128)(2,1)S(1)} %pad_maximum_fusion.26), channel_id=1, source_target_pairs={{0,4},{4,0},{8,12},{12,8},{1,5},{5,1},{9,13},{13,9},{2,6},{6,2},{1... | collective-permute-start | bytes 3145736 | tf_op jit(solution)/shard_map/ppermute | solution.py:776
  495.4 31.4 %collective-permute-start.35 = (bf16[2,128,2048]{2,1,0:T(8,128)(2,1)}, bf16[2,128,2048]{2,1,0:T(8,128)(2,1)S(1)}, u32[]{:S(2)}, u32[]{:S(2)}) collective-permute-start(bf16[2,128,2048]{2,1,0:T(8,128)(2,1)} %dynamic-slice_bitcast_fusion.21), channel_id=1, source_target_pairs={{0,4},{4,0},{8,12},{12,8},{1,5},{5,1},{9,13},{13,9},{2,6},{6,2},{1... | collective-permute-start | bytes 3145736 | tf_op jit(solution)/shard_map/ppermute | solution.py:776
  528.6 24.3 %collective-permute-start.44 = (bf16[128,2048]{1,0:T(8,128)(2,1)S(1)}, bf16[128,2048]{1,0:T(8,128)(2,1)S(1)}, u32[]{:S(2)}, u32[]{:S(2)}) collective-permute-start(bf16[128,2048]{1,0:T(8,128)(2,1)S(1)} %fusion.165), channel_id=1, source_target_pairs={{0,8},{4,12},{8,0},{12,4},{1,9},{5,13},{9,1},{13,5},{2,10},{6,14},... | collective-permute-start | bytes 1572872 | tf_op jit(solution)/shard_map/ppermute | solution.py:780
  530.0 43.9 %collective-permute-start.64 = (bf16[2,128,2048]{2,1,0:T(8,128)(2,1)S(1)}, bf16[2,128,2048]{2,1,0:T(8,128)(2,1)S(1)}, u32[]{:S(2)}, u32[]{:S(2)}) collective-permute-start(bf16[2,128,2048]{2,1,0:T(8,128)(2,1)S(1)} %pad_maximum_fusion.30), channel_id=1, source_target_pairs={{0,4},{4,0},{8,12},{12,8},{1,5},{5,1},{9,13},{13,9},{2,6},{6,2},{1... | collective-permute-start | bytes 3145736 | tf_op jit(solution)/shard_map/ppermute | solution.py:776
  543.3 16.8 collective-permute-start.45
  554.1 15.4 collective-permute-start.50
  624.9 24.5 %collective-permute-start.51 = (bf16[128,2048]{1,0:T(8,128)(2,1)S(1)}, bf16[128,2048]{1,0:T(8,128)(2,1)S(1)}, u32[]{:S(2)}, u32[]{:S(2)}) collective-permute-start(bf16[128,2048]{1,0:T(8,128)(2,1)S(1)} %fusion.92), channel_id=1, source_target_pairs={{0,8},{4,12},{8,0},{12,4},{1,9},{5,13},{9,1},{13,5},{2,10},{6,14},... | collective-permute-start | bytes 1572872 | tf_op jit(solution)/shard_map/ppermute | solution.py:780
  670.6 28.8 %collective-permute-start.57 = (bf16[2,128,2048]{2,1,0:T(8,128)(2,1)}, bf16[2,128,2048]{2,1,0:T(8,128)(2,1)S(1)}, u32[]{:S(2)}, u32[]{:S(2)}) collective-permute-start(bf16[2,128,2048]{2,1,0:T(8,128)(2,1)} %pad_maximum_fusion.29), channel_id=1, source_target_pairs={{0,4},{4,0},{8,12},{12,8},{1,5},{5,1},{9,13},{13,9},{2,6},{6,2},{1... | collective-permute-start | bytes 3145736 | tf_op jit(solution)/shard_map/ppermute | solution.py:776
  786.5 24.0 %collective-permute-start.73 = (bf16[128,2048]{1,0:T(8,128)(2,1)S(1)}, bf16[128,2048]{1,0:T(8,128)(2,1)S(1)}, u32[]{:S(2)}, u32[]{:S(2)}) collective-permute-start(bf16[128,2048]{1,0:T(8,128)(2,1)S(1)} %fusion.170), channel_id=1, source_target_pairs={{0,8},{4,12},{8,0},{12,4},{1,9},{5,13},{9,1},{13,5},{2,10},{6,14},... | collective-permute-start | bytes 1572872 | tf_op jit(solution)/shard_map/ppermute | solution.py:780
  812.6 16.8 collective-permute-start.74
  815.9 23.5 %collective-permute-start.69 = (bf16[128,2048]{1,0:T(8,128)(2,1)S(1)}, bf16[128,2048]{1,0:T(8,128)(2,1)S(1)}, u32[]{:S(2)}, u32[]{:S(2)}) collective-permute-start(bf16[128,2048]{1,0:T(8,128)(2,1)S(1)} %convert_add_fusion.30), channel_id=1, source_target_pairs={{16,0},{17,1},{18,2},{19,3},{20,4},{21,5},{22,6},{23,7},{24,8},{25... | collective-permute-start | bytes 1572872 | tf_op jit(solution)/shard_map/ppermute | solution.py:943
  854.0 19.4 collective-permute-start.71
  922.2 24.0 %collective-permute-start.80 = (bf16[128,2048]{1,0:T(8,128)(2,1)S(1)}, bf16[128,2048]{1,0:T(8,128)(2,1)S(1)}, u32[]{:S(2)}, u32[]{:S(2)}) collective-permute-start(bf16[128,2048]{1,0:T(8,128)(2,1)S(1)} %fusion.172), channel_id=1, source_target_pairs={{0,8},{4,12},{8,0},{12,4},{1,9},{5,13},{9,1},{13,5},{2,10},{6,14},... | collective-permute-start | bytes 1572872 | tf_op jit(solution)/shard_map/ppermute | solution.py:780
  949.4 16.7 collective-permute-start.84
  951.6 24.3 %collective-permute-start.81 = (bf16[128,2048]{1,0:T(8,128)(2,1)S(1)}, bf16[128,2048]{1,0:T(8,128)(2,1)S(1)}, u32[]{:S(2)}, u32[]{:S(2)}) collective-permute-start(bf16[128,2048]{1,0:T(8,128)(2,1)S(1)} %get-tuple-element.404), channel_id=1, source_target_pairs={{16,0},{17,1},{18,2},{19,3},{20,4},{21,5},{22,6},{23,7},{24,8},{25... | collective-permute-start | bytes 1572872 | tf_op jit(solution)/shard_map/ppermute | solution.py:943
  979.5 76.2 %collective-permute-start.54 = (bf16[128,2048]{1,0:T(8,128)(2,1)}, bf16[128,2048]{1,0:T(8,128)(2,1)}, u32[]{:S(2)}, u32[]{:S(2)}) collective-permute-start(bf16[128,2048]{1,0:T(8,128)(2,1)} %fusion.167), channel_id=1, source_target_pairs={{0,8},{4,12},{8,0},{12,4},{1,9},{5,13},{9,1},{13,5},{2,10},{6,14},... | collective-permute-start | bytes 1572872 | tf_op jit(solution)/shard_map/ppermute | solution.py:780
  992.8 19.4 collective-permute-start.83
  1059.5 24.4 %collective-permute-start.90 = (bf16[128,2048]{1,0:T(8,128)(2,1)S(1)}, bf16[128,2048]{1,0:T(8,128)(2,1)S(1)}, u32[]{:S(2)}, u32[]{:S(2)}) collective-permute-start(bf16[128,2048]{1,0:T(8,128)(2,1)S(1)} %fusion.174), channel_id=1, source_target_pairs={{0,8},{4,12},{8,0},{12,4},{1,9},{5,13},{9,1},{13,5},{2,10},{6,14},... | collective-permute-start | bytes 1572872 | tf_op jit(solution)/shard_map/ppermute | solution.py:780
  1087.3 15.6 collective-permute-start.94
  1098.1 15.9 collective-permute-start.91
  1116.9 76.6 %collective-permute-start.59 = (bf16[128,2048]{1,0:T(8,128)(2,1)S(1)}, bf16[128,2048]{1,0:T(8,128)(2,1)}, u32[]{:S(2)}, u32[]{:S(2)}) collective-permute-start(bf16[128,2048]{1,0:T(8,128)(2,1)S(1)} %fusion.168), channel_id=1, source_target_pairs={{0,8},{4,12},{8,0},{12,4},{1,9},{5,13},{9,1},{13,5},{2,10},{6,14},... | collective-permute-start | bytes 1572872 | tf_op jit(solution)/shard_map/ppermute | solution.py:780
  1130.8 19.7 collective-permute-start.93
  1196.6 58.4 %collective-permute-start.60 = (bf16[4,64,2048]{2,1,0:T(8,128)(2,1)S(1)}, bf16[4,64,2048]{2,1,0:T(8,128)(2,1)S(1)}, u32[]{:S(2)}, u32[]{:S(2)}) collective-permute-start(bf16[4,64,2048]{2,1,0:T(8,128)(2,1)S(1)} %get-tuple-element.439), channel_id=1, source_target_pairs={{0,3},{1,0},{2,1},{3,2},{4,7},{5,4},{6,5},{7,6},{8,11},{9,8},{10,9... | collective-permute-start | bytes 3145736 | tf_op jit(solution)/shard_map/ppermute | solution.py:770
  1199.4 24.5 %collective-permute-start.100 = (bf16[128,2048]{1,0:T(8,128)(2,1)S(1)}, bf16[128,2048]{1,0:T(8,128)(2,1)S(1)}, u32[]{:S(2)}, u32[]{:S(2)}) collective-permute-start(bf16[128,2048]{1,0:T(8,128)(2,1)S(1)} %fusion.176), channel_id=1, source_target_pairs={{0,8},{4,12},{8,0},{12,4},{1,9},{5,13},{9,1},{13,5},{2,10},{6,14},... | collective-permute-start | bytes 1572872 | tf_op jit(solution)/shard_map/ppermute | solution.py:780
  1227.2 16.7 collective-permute-start.104
  1228.5 25.4 %collective-permute-start.101 = (bf16[128,2048]{1,0:T(8,128)(2,1)S(1)}, bf16[128,2048]{1,0:T(8,128)(2,1)S(1)}, u32[]{:S(2)}, u32[]{:S(2)}) collective-permute-start(bf16[128,2048]{1,0:T(8,128)(2,1)S(1)} %get-tuple-element.386), channel_id=1, source_target_pairs={{16,0},{17,1},{18,2},{19,3},{20,4},{21,5},{22,6},{23,7},{24,8},{25... | collective-permute-start | bytes 1572872 | tf_op jit(solution)/shard_map/ppermute | solution.py:943
  1229.9 69.4 %collective-permute-start.61 = (bf16[4,64,2048]{2,1,0:T(8,128)(2,1)S(1)}, bf16[4,64,2048]{2,1,0:T(8,128)(2,1)S(1)}, u32[]{:S(2)}, u32[]{:S(2)}) collective-permute-start(bf16[4,64,2048]{2,1,0:T(8,128)(2,1)S(1)} %get-tuple-element.438), channel_id=1, source_target_pairs={{0,2},{1,3},{2,0},{3,1},{4,6},{5,7},{6,4},{7,5},{8,10},{9,11},{10,... | collective-permute-start | bytes 3145736 | tf_op jit(solution)/shard_map/ppermute | solution.py:770
  1230.8 69.8 %collective-permute-start.62 = (bf16[4,64,2048]{2,1,0:T(8,128)(2,1)S(1)}, bf16[4,64,2048]{2,1,0:T(8,128)(2,1)S(1)}, u32[]{:S(2)}, u32[]{:S(2)}) collective-permute-start(bf16[4,64,2048]{2,1,0:T(8,128)(2,1)S(1)} %get-tuple-element.437), channel_id=1, source_target_pairs={{0,1},{1,2},{2,3},{3,0},{4,5},{5,6},{6,7},{7,4},{8,9},{9,10},{10,1... | collective-permute-start | bytes 3145736 | tf_op jit(solution)/shard_map/ppermute | solution.py:770
  1254.3 46.0 %collective-permute-start.105 = (bf16[128,2048]{1,0:T(8,128)(2,1)S(1)}, bf16[128,2048]{1,0:T(8,128)(2,1)S(1)}, u32[]{:S(2)}, u32[]{:S(2)}) collective-permute-start(bf16[128,2048]{1,0:T(8,128)(2,1)S(1)} %get-tuple-element.361), channel_id=1, source_target_pairs={{0,8},{4,12},{8,0},{12,4},{1,9},{5,13},{9,1},{13,5},{2,10},{6,14},... | collective-permute-start | bytes 1572872 | tf_op jit(solution)/shard_map/ppermute | solution.py:780
  1313.5 19.4 collective-permute-start.103
  1391.0 619.7 %collective-permute-start.107 = (bf16[2,128,2048]{2,1,0:T(8,128)(2,1)}, bf16[2,128,2048]{2,1,0:T(8,128)(2,1)}, u32[]{:S(2)}, u32[]{:S(2)}) collective-permute-start(bf16[2,128,2048]{2,1,0:T(8,128)(2,1)} %dynamic-slice_bitcast_fusion.5), channel_id=1, source_target_pairs={{0,4},{4,0},{8,12},{12,8},{1,5},{5,1},{9,13},{13,9},{2,6},{6,2},{1... | collective-permute-start | bytes 3145736 | tf_op jit(solution)/shard_map/ppermute | solution.py:776
  1392.5 620.7 %collective-permute-start.109 = (bf16[2,128,2048]{2,1,0:T(8,128)(2,1)}, bf16[2,128,2048]{2,1,0:T(8,128)(2,1)}, u32[]{:S(2)}, u32[]{:S(2)}) collective-permute-start(bf16[2,128,2048]{2,1,0:T(8,128)(2,1)} %dynamic-slice_bitcast_fusion.4), channel_id=1, source_target_pairs={{0,4},{4,0},{8,12},{12,8},{1,5},{5,1},{9,13},{13,9},{2,6},{6,2},{1... | collective-permute-start | bytes 3145736 | tf_op jit(solution)/shard_map/ppermute | solution.py:776
  2014.9 21.1 collective-permute-start.110
  2042.1 54.2 %collective-permute-start.111 = (bf16[4,64,2048]{2,1,0:T(8,128)(2,1)}, bf16[4,64,2048]{2,1,0:T(8,128)(2,1)}, u32[]{:S(2)}, u32[]{:S(2)}) collective-permute-start(bf16[4,64,2048]{2,1,0:T(8,128)(2,1)} %get-tuple-element.436), channel_id=1, source_target_pairs={{0,3},{1,0},{2,1},{3,2},{4,7},{5,4},{6,5},{7,6},{8,11},{9,8},{10,9... | collective-permute-start | bytes 3145736 | tf_op jit(solution)/shard_map/ppermute | solution.py:770
  2051.2 80.1 %collective-permute-start.112 = (bf16[4,64,2048]{2,1,0:T(8,128)(2,1)}, bf16[4,64,2048]{2,1,0:T(8,128)(2,1)}, u32[]{:S(2)}, u32[]{:S(2)}) collective-permute-start(bf16[4,64,2048]{2,1,0:T(8,128)(2,1)} %get-tuple-element.435), channel_id=1, source_target_pairs={{0,2},{1,3},{2,0},{3,1},{4,6},{5,7},{6,4},{7,5},{8,10},{9,11},{10,... | collective-permute-start | bytes 3145736 | tf_op jit(solution)/shard_map/ppermute | solution.py:770
  2052.7 79.8 %collective-permute-start.113 = (bf16[4,64,2048]{2,1,0:T(8,128)(2,1)}, bf16[4,64,2048]{2,1,0:T(8,128)(2,1)}, u32[]{:S(2)}, u32[]{:S(2)}) collective-permute-start(bf16[4,64,2048]{2,1,0:T(8,128)(2,1)} %get-tuple-element.434), channel_id=1, source_target_pairs={{0,1},{1,2},{2,3},{3,0},{4,5},{5,6},{6,7},{7,4},{8,9},{9,10},{10,1... | collective-permute-start | bytes 3145736 | tf_op jit(solution)/shard_map/ppermute | solution.py:770
  (200 other events, 3377.4 us)

commit v3 on v2

v3 whole, which is shorter than its diff:
```python
from functools import partial

import jax
import jax.numpy as jnp
from jax import lax
from jax.experimental import pallas as pl
from jax.experimental.pallas import tpu as pltpu
from jax.sharding import PartitionSpec as P

ROT = 64
LAG = 3
LANES = 128
epsilon = 1e-05
masked_score = -1e30
f32 = jnp.float32
bf16 = jnp.bfloat16
NT = (((1,), (1,)), ((), ()))
TN = (((0,), (0,)), ((), ()))
NN = (((1,), (0,)), ((), ()))
PASS_VMEM = 62 * 1024 * 1024


def dot(a, b, dims=NN):
    return lax.dot_general(a, b, dims, preferred_element_type=f32)


def standardize(rows):
    values = rows.astype(f32)
    average = jnp.mean(values, axis=-1, keepdims=True)
    centred = values - average
    inverse = lax.rsqrt(jnp.mean(centred * centred, axis=-1, keepdims=True) + epsilon)
    return centred * inverse, inverse


def position_tables(section_rows, blocks, rows, tensor):
    half = ROT // 2
    frequency = 1.0 / 10000.0 ** (jnp.arange(0, ROT, 2, dtype=f32) / ROT)
    t, c, i = jnp.meshgrid(
        jnp.arange(tensor), jnp.arange(blocks), jnp.arange(rows), indexing="ij"
    )
    relative = (c * (rows * tensor) + t * rows + i).reshape(-1).astype(jnp.int32)
    tables = []
    for part in range(2):
        places = (relative + part * blocks * rows * tensor).astype(f32)
        angles = places[:, None] * frequency[None, :]
        cosine, sine = jnp.cos(angles), jnp.sin(angles)
        none = jnp.zeros_like(sine)
        rest = jnp.zeros((relative.shape[0], LANES - ROT), f32)
        tables.append(
            (
                jnp.concatenate([cosine, cosine, rest + 1.0], axis=-1),
                jnp.concatenate([-sine, none, rest], axis=-1),
                jnp.concatenate([none, sine, rest], axis=-1),
            )
        )
    return relative, tables


def turn(values, cosine, ahead, behind, sign):
    half = ROT // 2
    lead = values[:, :LANES]
    turned = pltpu.roll(lead, LANES - half, 1) * ahead + pltpu.roll(lead, half, 1) * behind
    return jnp.concatenate([lead * cosine + sign * turned, values[:, LANES:]], axis=1)


class Moves:
    def __init__(self, plan, place, land, arrive, core_land, chip_land, own, theirs, low, handed, sems):
        self.tasks, self.chips, self.rows = plan
        self.place = place
        self.land, self.arrive, self.core_land, self.chip_land = land, arrive, core_land, chip_land
        self.own, self.theirs, self.low, self.handed = own, theirs, low, handed
        (
            self.got_chip, self.got_core, self.got_theirs, self.got_low, self.got_hand,
            self.put_chip, self.put_core, self.put_theirs, self.put_low, self.put_hand,
        ) = sems
        self.section = lax.axis_index("section")
        self.index = lax.axis_index("tensor")
        self.total = 2 * self.chips
        self.chip, self.core = self.index // 2, self.index % 2
        self.mate = self.chip * 2 + 1 - self.core

    def mate_on(self, shift):
        return lax.rem(self.index + 2 * shift, self.total)

    def part(self, member):
        return pl.ds(pl.multiple_of(member * self.rows, self.rows), self.rows)

    def remote(self, source, target, sent, arrived, **device):
        return pltpu.make_async_remote_copy(
            src_ref=source,
            dst_ref=target,
            send_sem=sent,
            recv_sem=arrived,
            device_id=device,
            device_id_type=pl.DeviceIdType.MESH,
        )

    def greet(self):
        barrier = pltpu.get_barrier_semaphore()
        peers = [{"section": 1 - self.section}, {"tensor": self.mate}]
        peers += [{"tensor": self.mate_on(shift)} for shift in range(1, self.chips)]
        for peer in peers:
            pl.semaphore_signal(barrier, inc=1, device_id=peer, device_id_type=pl.DeviceIdType.MESH)
        pl.semaphore_wait(barrier, len(peers))

    def gather_chip(self, task, shift, member=None):
        member = self.index if member is None else member
        return self.remote(
            self.own,
            self.land.at[self.place(task), self.part(member)],
            self.put_chip.at[shift - 1],
            self.got_chip.at[task, shift - 1],
            tensor=self.mate_on(shift),
        )

    def gather_chip_in(self, task, shift):
        return self.gather_chip(task, shift, lax.rem(self.index + self.total - 2 * shift, self.total))

    def gather_core(self, task, shift, member=None):
        if member is None:
            member = lax.rem(self.index + self.total - 2 * shift, self.total)
        target = self.land.at[self.place(task), self.part(member)]
        return self.remote(
            self.own if shift == 0 else target,
            target,
            self.put_core.at[shift],
            self.got_core.at[task, shift],
            tensor=self.mate,
        )

    def gather_core_in(self, task, shift):
        return self.gather_core(task, shift, lax.rem(self.mate + self.total - 2 * shift, self.total))

    def give_theirs(self, task):
        return self.remote(
            self.theirs, self.core_land.at[task], self.put_theirs, self.got_theirs.at[task], tensor=self.mate
        )

    def give_low(self, task, shift):
        return self.remote(
            self.low.at[lax.rem(self.chip + shift, self.chips)],
            self.chip_land.at[task, shift - 1],
            self.put_low.at[shift - 1],
            self.got_low.at[task, shift - 1],
            tensor=self.mate_on(shift),
        )

    def hand(self, task):
        return self.remote(
            self.handed, self.arrive.at[task], self.put_hand, self.got_hand.at[task], section=1 - self.section
        )


def reduce_first(moves, task, mine, core_in, load_sem):
    moves.give_theirs(task).wait_recv()
    load = pltpu.make_async_copy(moves.core_land.at[task], core_in, load_sem)
    load.start()

    @pl.when(task >= 1)
    def _():
        for shift in range(1, moves.chips):
            moves.give_low(task - 1, shift).wait_send()

    load.wait()
    for j in range(moves.chips):
        value = mine[j] + core_in[j].astype(f32)
        mine[j] = value
        moves.low[j] = value.astype(bf16)
    for shift in range(1, moves.chips):
        moves.give_low(task, shift).start()


def reduce_second(moves, task, mine, chip_in, load_sem):
    for shift in range(1, moves.chips):
        moves.give_low(task, shift).wait_recv()
    load = pltpu.make_async_copy(moves.chip_land.at[task], chip_in, load_sem)
    load.start()
    load.wait()
    value = mine[moves.chip]
    for shift in range(1, moves.chips):
        value = value + chip_in[shift - 1].astype(f32)
    return value


def gather_start(moves, task, keep_sem):
    pltpu.make_async_copy(
        moves.own, moves.land.at[moves.place(task), moves.part(moves.index)], keep_sem
    ).start()
    for shift in range(1, moves.chips):
        moves.gather_chip(task, shift).start()
    moves.gather_core(task, 0).start()


def gather_free(moves, task):
    for shift in range(1, moves.chips):
        moves.gather_chip(task, shift).wait_send()
    moves.gather_core(task, 0).wait_send()


def gather_pass(moves, task, keep_sem):
    pltpu.make_async_copy(
        moves.own, moves.land.at[moves.place(task), moves.part(moves.index)], keep_sem
    ).wait()
    for shift in range(1, moves.chips):
        moves.gather_chip_in(task, shift).wait_recv()

        @pl.when(task >= 1)
        def _():
            moves.gather_core(task - 1, shift).wait_send()

        moves.gather_core(task, shift).start()


def gather_wait(moves, task):
    for shift in range(moves.chips):
        moves.gather_core_in(task, shift).wait_recv()


def drain(moves, task):
    gather_free(moves, task)
    for shift in range(1, moves.chips):
        moves.gather_core(task, shift).wait_send()
        moves.give_low(task, shift).wait_send()
    moves.give_theirs(task).wait_send()


def when(condition):
    return pl.when(condition)


def forward_kernel(
    plan, xin, wq_all, wi_all, wo_all, wd_all, bq, bi, out_bias, cosine, ahead, behind, pq, pk,
    land, qkv_all, act_all, dg_all, ctx_all, lse_all, states, arrive, core_land, chip_land,
    wq, wi, wo, wd, std, qkv, act, dg, ctx, lse, kept, own, theirs, mine, core_in, low, chip_in, handed,
    weight_sem, load_sem, store_sem, keep_sem, state_sem, *sems,
):
    tasks, chips, rows, heads = plan
    size = wq.shape[1] // (3 * heads)
    moves = Moves(
        (tasks, chips, rows), lambda task: task, land, arrive, core_land, chip_land, own, theirs, low, handed, sems
    )
    first = moves.section == 0
    base = jnp.where(first, 0, LAG)

    weights = [
        pltpu.make_async_copy(a, b, weight_sem.at[k])
        for k, (a, b) in enumerate(((wq_all, wq), (wi_all, wi), (wo_all, wo), (wd_all, wd)))
    ]
    for copy in weights:
        copy.start()
    moves.greet()

    def valid(task):
        return (task >= 0) & (task < tasks)

    def store(k, task):
        return pltpu.make_async_copy(
            (qkv.at[task % 2], act, dg, ctx, lse)[k],
            (qkv_all, act_all, dg_all, ctx_all, lse_all)[k].at[task],
            store_sem.at[k],
        )

    def project(task):
        half = task % 2
        table = (cosine[half], ahead[half], behind[half])
        for h in range(heads):
            for k in range(3):
                columns = slice((3 * h + k) * size, (3 * h + k + 1) * size)
                z = dot(std[...], wq[:, columns]) + bq[:, columns]
                if k < 2:
                    z = turn(z, *table, 1.0)
                qkv[half, :, columns] = z.astype(bf16)

    def attend(task, second):
        half = 1 if second else 0
        scale = size**-0.5
        for h in range(heads):
            at = [slice((3 * h + k) * size, (3 * h + k + 1) * size) for k in range(3)]
            q = qkv[half, :, at[0]]
            s = dot(q, qkv[half, :, at[1]], NT) * scale
            s = jnp.where(pq[...] >= pk[...], s, masked_score)
            peak = jnp.max(s, axis=-1, keepdims=True)
            if second:
                sp = dot(q, qkv[0, :, at[1]], NT) * scale
                peak = jnp.maximum(peak, jnp.max(sp, axis=-1, keepdims=True))
            p = jnp.exp(s - peak)
            total = jnp.sum(p, axis=-1, keepdims=True)
            if second:
                pp = jnp.exp(sp - peak)
                total = total + jnp.sum(pp, axis=-1, keepdims=True)
            share = 1.0 / total
            value = dot((p * share).astype(bf16), qkv[half, :, at[2]])
            if second:
                value = value + dot((pp * share).astype(bf16), qkv[0, :, at[2]])
            ctx[:, h * size : (h + 1) * size] = value.astype(bf16)
            lse[:, h * LANES : (h + 1) * LANES] = jnp.broadcast_to(
                peak + jnp.log(total), (q.shape[0], LANES)
            )

    def expand():
        for at in range(0, wi.shape[1], 256):
            columns = slice(at, at + 256)
            h = dot(std[...], wi[:, columns]) + bi[:, columns]
            phi = 0.5 + 0.5 * lax.erf(h * (0.5**0.5))
            density = jnp.exp(h * h * -0.5) * 0.3989422804014327
            act[:, columns] = (h * phi).astype(bf16)
            dg[:, columns] = (phi + h * density).astype(bf16)

    def branch_rows(member):
        at = moves.part(member)
        return dot(ctx[at, :], wo[...]) + dot(act[at, :], wd[...])

    @pl.loop(0, tasks + LAG + 2)
    def _(step):
        g = step - base
        c = g - 1
        r = g - 2

        def load_rows(task, held):
            return pltpu.make_async_copy(held.at[task], kept.at[task % 4], load_sem.at[0])

        @when(valid(g) & first)
        def _():
            load_rows(g, xin).start()

        @when(valid(r))
        def _():
            reduce_first(moves, r, mine, core_in, load_sem.at[1])

        @when(valid(c))
        def _():
            gather_wait(moves, c)
            load = pltpu.make_async_copy(land.at[c], std, load_sem.at[2])
            load.start()

            @when(c == 0)
            def _():
                weights[0].wait()

            @when(c >= 1)
            def _():
                for k in range(5):
                    store(k, c - 1).wait()

            load.wait()
            project(c)
            store(0, c).start()

            @when(c % 2 == 0)
            def _():
                attend(c, False)

            @when(c % 2 == 1)
            def _():
                attend(c, True)

            store(3, c).start()
            store(4, c).start()

        @when(valid(g))
        def _():
            @when(jnp.logical_not(first))
            def _():
                moves.hand(g).wait_recv()
                load_rows(g, arrive).start()

            load_rows(g, xin).wait()

            @when(g >= 1)
            def _():
                gather_free(moves, g - 1)

            own[...] = standardize(kept[g % 4])[0].astype(bf16)
            gather_start(moves, g, keep_sem)

        @when(valid(c))
        def _():
            @when(c == 0)
            def _():
                weights[1].wait()

            expand()
            store(1, c).start()
            store(2, c).start()

        @when(valid(r))
        def _():
            value = reduce_second(moves, r, mine, chip_in, load_sem.at[1])

            @when(r >= 1)
            def _():
                pltpu.make_async_copy(handed, states.at[r - 1], state_sem).wait()

                @when(first)
                def _():
                    moves.hand(r - 1).wait_send()

            handed[...] = (kept[r % 4].astype(f32) + value + out_bias[...]).astype(bf16)
            pltpu.make_async_copy(handed, states.at[r], state_sem).start()

            @when(first)
            def _():
                moves.hand(r).start()

        @when(valid(c))
        def _():
            @when(c == 0)
            def _():
                weights[2].wait()
                weights[3].wait()

            @when(c >= 1)
            def _():
                moves.give_theirs(c - 1).wait_send()

            for j in range(chips):
                theirs[j] = branch_rows(2 * j + 1 - moves.core).astype(bf16)
            moves.give_theirs(c).start()
            for j in range(chips):
                mine[j] = branch_rows(2 * j + moves.core)

        @when(valid(g))
        def _():
            gather_pass(moves, g, keep_sem)

    drain(moves, tasks - 1)
    for k in range(5):
        store(k, tasks - 1).wait()
    pltpu.make_async_copy(handed, states.at[tasks - 1], state_sem).wait()

    @when(first)
    def _():
        moves.hand(tasks - 1).wait_send()


def move_semaphores(tasks, chips):
    dma = pltpu.SemaphoreType.DMA
    return [
        dma((tasks, chips - 1)),
        dma((tasks, chips)),
        dma((tasks,)),
        dma((tasks, chips - 1)),
        dma((tasks,)),
        dma((chips - 1,)),
        dma((chips,)),
        dma,
        dma((chips - 1,)),
        dma,
    ]


def forward_pass(xin, wq, wi, wo, wd, bq, bi, out_bias, tables, pq, pk, chips, heads):
    tasks, rows, width = xin.shape
    block = pq.shape[0]
    units, inner = wd.shape[0], wo.shape[0]
    anywhere = pl.BlockSpec(memory_space=pl.ANY)
    vmem = pl.BlockSpec(memory_space=pltpu.VMEM)
    shape = jax.ShapeDtypeStruct
    return pl.pallas_call(
        partial(forward_kernel, (tasks, chips, rows, heads)),
        out_shape=[
            shape((tasks, block, width), bf16),
            shape((tasks, block, 3 * inner), bf16),
            shape((tasks, block, units), bf16),
            shape((tasks, block, units), bf16),
            shape((tasks, block, inner), bf16),
            shape((tasks, block, heads * LANES), f32),
            shape((tasks, rows, width), bf16),
            shape((tasks, rows, width), bf16),
            shape((tasks, chips, rows, width), bf16),
            shape((tasks, chips - 1, rows, width), bf16),
        ],
        in_specs=[anywhere] * 5 + [vmem] * 8,
        out_specs=[anywhere] * 10,
        scratch_shapes=[
            pltpu.VMEM(wq.shape, bf16),
            pltpu.VMEM(wi.shape, bf16),
            pltpu.VMEM(wo.shape, bf16),
            pltpu.VMEM(wd.shape, bf16),
            pltpu.VMEM((block, width), bf16),
            pltpu.VMEM((2, block, 3 * inner), bf16),
            pltpu.VMEM((block, units), bf16),
            pltpu.VMEM((block, units), bf16),
            pltpu.VMEM((block, inner), bf16),
            pltpu.VMEM((block, heads * LANES), f32),
            pltpu.VMEM((4, rows, width), bf16),
            pltpu.VMEM((rows, width), bf16),
            pltpu.VMEM((chips, rows, width), bf16),
            pltpu.VMEM((chips, rows, width), f32),
            pltpu.VMEM((chips, rows, width), bf16),
            pltpu.VMEM((chips, rows, width), bf16),
            pltpu.VMEM((chips - 1, rows, width), bf16),
            pltpu.VMEM((rows, width), bf16),
            pltpu.SemaphoreType.DMA((4,)),
            pltpu.SemaphoreType.DMA((3,)),
            pltpu.SemaphoreType.DMA((5,)),
            pltpu.SemaphoreType.DMA,
            pltpu.SemaphoreType.DMA,
        ]
        + move_semaphores(tasks, chips),
        compiler_params=pltpu.CompilerParams(
            collective_id=3, has_side_effects=True, vmem_limit_bytes=PASS_VMEM
        ),
        cost_estimate=pl.CostEstimate(
            flops=2 * tasks * block * width * (3 * inner + 2 * units + inner),
            bytes_accessed=tasks * block * width * 16,
            transcendentals=0,
        ),
        name="forward_pass",
    )(xin, wq, wi, wo, wd, bq, bi, out_bias, *tables, pq, pk)


def backward_kernel(
    plan, gin, xin, xarrive, qkv_all, dg_all, ctx_all, lse_all, std_all, wq_all, wi_all, wo_all, wd_all,
    gains, cosine, ahead, behind, pq, pk,
    land, dproj_all, dh_all, dx_all, arrive, core_land, chip_land, vectors,
    wq, wi, wo, wd, gy, dg, dh, qkv, before, ctx, lse, std, dctx, dproj, dk_held, dv_held,
    kept, xrows, own, theirs, mine, core_in, low, chip_in, handed,
    weight_sem, load_sem, store_sem, keep_sem, state_sem, *sems,
):
    tasks, chips, rows, heads = plan
    size = wq.shape[1] // (3 * heads)
    scale = size**-0.5

    def place(task):
        return task + 1 - 2 * (task % 2)

    moves = Moves(
        (tasks, chips, rows), place, land, arrive, core_land, chip_land, own, theirs, low, handed, sems
    )
    first = moves.section == 0
    source = moves.section == 1
    base = jnp.where(source, 0, LAG)

    weights = [
        pltpu.make_async_copy(a, b, weight_sem.at[k])
        for k, (a, b) in enumerate(((wo_all, wo), (wd_all, wd), (wq_all, wq), (wi_all, wi)))
    ]
    for copy in weights:
        copy.start()
    vectors[...] = jnp.zeros_like(vectors)
    moves.greet()

    def valid(task):
        return (task >= 0) & (task < tasks)

    def store(k, task):
        return pltpu.make_async_copy(
            (dproj, dh)[k], (dproj_all, dh_all)[k].at[place(task)], store_sem.at[k]
        )

    def load(k, task):
        return pltpu.make_async_copy(
            (land, dg_all, qkv_all, ctx_all, lse_all, std_all)[k].at[place(task)],
            (gy, dg, qkv, ctx, lse, std)[k],
            load_sem.at[k],
        )

    def load_before(task):
        return pltpu.make_async_copy(qkv_all.at[place(task) - 1], before, load_sem.at[6])

    def spread():
        dctx[...] = dot(gy[...], wo[...], NT).astype(bf16)
        for at in range(0, wd.shape[0], 256):
            part = slice(at, at + 256)
            dh[:, part] = (dot(gy[...], wd[part, :], NT) * dg[:, part].astype(f32)).astype(bf16)

    def attend_back(second):
        half = 1 if second else 0
        table = (cosine[half], ahead[half], behind[half])
        for h in range(heads):
            at = [slice((3 * h + k) * size, (3 * h + k + 1) * size) for k in range(3)]
            mid = slice(h * size, (h + 1) * size)
            q = qkv[:, at[0]]
            d_ctx = dctx[:, mid]
            logsum = lse[:, h * LANES : h * LANES + 1]
            delta = jnp.sum(d_ctx.astype(f32) * ctx[:, mid].astype(f32), axis=-1, keepdims=True)

            def pieces(held, masked):
                k, v = held[:, at[1]], held[:, at[2]]
                s = dot(q, k, NT) * scale
                if masked:
                    s = jnp.where(pq[...] >= pk[...], s, masked_score)
                p = jnp.exp(s - logsum)
                d_chance = dot(d_ctx, v, NT)
                d_scores = (p * (d_chance - delta)).astype(bf16)
                return dot(d_scores, k), dot(d_scores, q, TN), dot(p.astype(bf16), d_ctx, TN)

            dq, dk, dv = pieces(qkv, True)
            if second:
                dq_more, dk_more, dv_more = pieces(before, False)
                dq = dq + dq_more
                dk_held[:, mid] = dk_more
                dv_held[:, mid] = dv_more
            else:
                dk = dk + dk_held[:, mid]
                dv = dv + dv_held[:, mid]
            dproj[:, at[0]] = turn(dq * scale, *table, -1.0).astype(bf16)
            dproj[:, at[1]] = turn(dk * scale, *table, -1.0).astype(bf16)
            dproj[:, at[2]] = dv.astype(bf16)

    def merge_rows(member):
        at = moves.part(member)
        one = dot(dproj[at, :], wq[...], NT)
        two = dot(dh[at, :], wi[...], NT)
        standard = std[at, :].astype(f32)
        for k, term in enumerate((one * standard, one, two * standard, two)):
            vectors[k : k + 1, :] += jnp.sum(term, axis=0, keepdims=True)
        return one * gains[0] + two * gains[1]

    @pl.loop(0, tasks + LAG + 2)
    def _(step):
        g = step - base
        c = g - 1
        r = g - 2

        def load_rows(task, held, number):
            return pltpu.make_async_copy(held.at[number], kept.at[task % 4], load_sem.at[7])

        def load_x(task, held):
            return pltpu.make_async_copy(held.at[place(task)], xrows, load_sem.at[8])

        @when(valid(g) & source)
        def _():
            load_rows(g, gin, place(g)).start()

        @when(valid(r))
        def _():
            @when(first)
            def _():
                load_x(r, xin).start()

            @when(jnp.logical_not(first))
            def _():
                load_x(r, xarrive).start()

            reduce_first(moves, r, mine, core_in, load_sem.at[9])

        @when(valid(c))
        def _():
            gather_wait(moves, c)
            for k in range(6):
                load(k, c).start()

            @when(c % 2 == 0)
            def _():
                load_before(c).start()

            @when(c == 0)
            def _():
                weights[0].wait()
                weights[1].wait()

            @when(c >= 1)
            def _():
                for k in range(2):
                    store(k, c - 1).wait()

            load(0, c).wait()
            load(1, c).wait()
            spread()
            store(1, c).start()
            for k in range(2, 6):
                load(k, c).wait()

        @when(valid(g))
        def _():
            @when(first)
            def _():
                moves.hand(g).wait_recv()
                load_rows(g, arrive, g).start()

            load_rows(g, gin, g).wait()

            @when(g >= 1)
            def _():
                gather_free(moves, g - 1)

            own[...] = kept[g % 4]
            gather_start(moves, g, keep_sem)
            vectors[4:5, :] += jnp.sum(kept[g % 4].astype(f32), axis=0, keepdims=True)

        @when(valid(c))
        def _():
            @when(c % 2 == 0)
            def _():
                load_before(c).wait()
                attend_back(True)

            @when(c % 2 == 1)
            def _():
                attend_back(False)

            store(0, c).start()

        @when(valid(r))
        def _():
            e = reduce_second(moves, r, mine, chip_in, load_sem.at[9])
            load_x(r, xin).wait()

            @when(r >= 1)
            def _():
                pltpu.make_async_copy(handed, dx_all.at[place(r - 1)], state_sem).wait()

                @when(source)
                def _():
                    moves.hand(r - 1).wait_send()

            standard, inverse = standardize(xrows[...])
            d_input = kept[r % 4].astype(f32) + inverse * (
                e
                - jnp.mean(e, axis=-1, keepdims=True)
                - standard * jnp.mean(e * standard, axis=-1, keepdims=True)
            )
            handed[...] = d_input.astype(bf16)
            pltpu.make_async_copy(handed, dx_all.at[place(r)], state_sem).start()

            @when(source)
            def _():
                moves.hand(r).start()

        @when(valid(c))
        def _():
            @when(c == 0)
            def _():
                weights[2].wait()
                weights[3].wait()

            @when(c >= 1)
            def _():
                moves.give_theirs(c - 1).wait_send()

            for j in range(chips):
                theirs[j] = merge_rows(2 * j + 1 - moves.core).astype(bf16)
            moves.give_theirs(c).start()
            for j in range(chips):
                mine[j] = merge_rows(2 * j + moves.core)

        @when(valid(g))
        def _():
            gather_pass(moves, g, keep_sem)

    drain(moves, tasks - 1)
    for k in range(2):
        store(k, tasks - 1).wait()
    pltpu.make_async_copy(handed, dx_all.at[place(tasks - 1)], state_sem).wait()

    @when(source)
    def _():
        moves.hand(tasks - 1).wait_send()


def backward_pass(gin, xin, xarrive, qkv, dg, ctx, lse, std, wq, wi, wo, wd, gains, tables, pq, pk, chips, heads):
    tasks, rows, width = xin.shape
    block = pq.shape[0]
    units, inner = wd.shape[0], wo.shape[0]
    anywhere = pl.BlockSpec(memory_space=pl.ANY)
    vmem = pl.BlockSpec(memory_space=pltpu.VMEM)
    shape = jax.ShapeDtypeStruct
    return pl.pallas_call(
        partial(backward_kernel, (tasks, chips, rows, heads)),
        out_shape=[
            shape((tasks, block, width), bf16),
            shape((tasks, block, 3 * inner), bf16),
            shape((tasks, block, units), bf16),
            shape((tasks, rows, width), bf16),
            shape((tasks, rows, width), bf16),
            shape((tasks, chips, rows, width), bf16),
            shape((tasks, chips - 1, rows, width), bf16),
            shape((8, width), f32),
        ],
        in_specs=[anywhere] * 12 + [vmem] * 6,
        out_specs=[anywhere] * 7 + [vmem],
        scratch_shapes=[
            pltpu.VMEM(wq.shape, bf16),
            pltpu.VMEM(wi.shape, bf16),
            pltpu.VMEM(wo.shape, bf16),
            pltpu.VMEM(wd.shape, bf16),
            pltpu.VMEM((block, width), bf16),
            pltpu.VMEM((block, units), bf16),
            pltpu.VMEM((block, units), bf16),
            pltpu.VMEM((block, 3 * inner), bf16),
            pltpu.VMEM((block, 3 * inner), bf16),
            pltpu.VMEM((block, inner), bf16),
            pltpu.VMEM((block, heads * LANES), f32),
            pltpu.VMEM((block, width), bf16),
            pltpu.VMEM((block, inner), bf16),
            pltpu.VMEM((block, 3 * inner), bf16),
            pltpu.VMEM((block, inner), f32),
            pltpu.VMEM((block, inner), f32),
            pltpu.VMEM((4, rows, width), bf16),
            pltpu.VMEM((rows, width), bf16),
            pltpu.VMEM((rows, width), bf16),
            pltpu.VMEM((chips, rows, width), bf16),
            pltpu.VMEM((chips, rows, width), f32),
            pltpu.VMEM((chips, rows, width), bf16),
            pltpu.VMEM((chips, rows, width), bf16),
            pltpu.VMEM((chips - 1, rows, width), bf16),
            pltpu.VMEM((rows, width), bf16),
            pltpu.SemaphoreType.DMA((4,)),
            pltpu.SemaphoreType.DMA((10,)),
            pltpu.SemaphoreType.DMA((2,)),
            pltpu.SemaphoreType.DMA,
            pltpu.SemaphoreType.DMA,
        ]
        + move_semaphores(tasks, chips),
        compiler_params=pltpu.CompilerParams(
            collective_id=5, has_side_effects=True, vmem_limit_bytes=PASS_VMEM
        ),
        cost_estimate=pl.CostEstimate(
            flops=2 * tasks * block * width * (3 * inner + 2 * units + inner),
            bytes_accessed=tasks * block * width * 20,
            transcendentals=0,
        ),
        name="backward_pass",
    )(gin, xin, xarrive, qkv, dg, ctx, lse, std, wq, wi, wo, wd, gains, *tables, pq, pk)


CHUNK = 256
PIECE = 64
SKEW = 2


def reduce_kernel(
    plan, act, ctx, dproj, dhid, gy, std, gains, biases, sums, small, out, small_out, from_left, from_right,
    rhs, raw, lhs, own, inbox, outbox, stage, small_in,
    rhs_sem, raw_sem, right_sem, left_sem, final_sem, load_sem, sent, stage_left, stage_right, out_sem,
    small_sent, small_got,
):
    bounds, tasks, count, piece, skew, ring = plan
    sources = (act, ctx, dproj, dhid)
    total_chunks = bounds[-1]
    per_chunk = CHUNK // piece
    pieces = total_chunks * per_chunk
    width = gy.shape[-1]
    tile = width // per_chunk
    block = raw.shape[2]
    z = lax.axis_index("ctx")
    last = count - 1
    root = count // 2
    turn_at = max(root, last - root)
    low, high, middle = z < root, z > root, z == root

    barrier = pltpu.get_barrier_semaphore()
    for shift in range(1, count):
        pl.semaphore_signal(
            barrier,
            inc=1,
            device_id={"ctx": lax.rem(z + shift, count)},
            device_id_type=pl.DeviceIdType.MESH,
        )

    def small_copy(source, target):
        return pltpu.make_async_remote_copy(
            src_ref=small,
            dst_ref=small_in.at[source],
            send_sem=small_sent.at[target],
            recv_sem=small_got.at[source],
            device_id={"ctx": target},
            device_id_type=pl.DeviceIdType.MESH,
        )

    def rhs_copy(k):
        return pltpu.make_async_copy((gy, std)[k].at[pl.ds(0, tasks)], rhs.at[k], rhs_sem.at[k])

    def each_source(chunk, act_on):
        for g, source in enumerate(sources):

            @pl.when((chunk >= bounds[g]) & (chunk < bounds[g + 1]))
            def _(g=g, source=source):
                column = pl.multiple_of((chunk - bounds[g]) * CHUNK, CHUNK)
                act_on(
                    pltpu.make_async_copy(
                        source.at[pl.ds(0, tasks), :, pl.ds(column, CHUNK)],
                        raw.at[chunk % 2],
                        raw_sem.at[chunk % 2],
                    )
                )

    def take(chunk):
        each_source(chunk, lambda copy: copy.wait())
        for k in range(tasks):
            lhs[:, k * block : (k + 1) * block] = raw[chunk % 2, k].T
        each_source(chunk + 1, lambda copy: copy.start())

    def multiply(chunk, part):
        second = jnp.where(chunk >= bounds[2], 1, 0)
        group = second + jnp.where(chunk >= bounds[3], 1, 0)
        columns = pl.ds(pl.multiple_of(part * tile, tile), tile)
        value = dot(lhs[:, :block], rhs[second, 0, :, columns])
        for k in range(1, tasks):
            value = value + dot(lhs[:, k * block : (k + 1) * block], rhs[second, k, :, columns])
        row = pl.multiple_of(chunk * CHUNK, CHUNK)
        value = value * gains[group, :, columns] + sums[pl.ds(row, CHUNK), :] * biases[group, :, columns]
        own[chunk % ring, :, columns] = value.astype(bf16)

    def rows_of(index):
        return pl.ds(pl.multiple_of(index * piece, piece), piece)

    def own_piece(index):
        inner = pl.multiple_of((index % per_chunk) * piece, piece)
        return own[(index // per_chunk) % ring, pl.ds(inner, piece), :]

    def remote(source, target_rows, send_sem, recv_sem, target):
        return pltpu.make_async_remote_copy(
            src_ref=source,
            dst_ref=target_rows,
            send_sem=send_sem,
            recv_sem=recv_sem,
            device_id={"ctx": target},
            device_id_type=pl.DeviceIdType.MESH,
        )

    def inward(index, right):
        landing, arrived, target = (from_left, right_sem, z + 1) if right else (from_right, left_sem, z - 1)
        return remote(
            outbox.at[index % 2], landing.at[rows_of(index)], sent.at[index % 2], arrived.at[index], target
        )

    def announce(index, right):
        return remote(
            stage.at[index % 2],
            out.at[rows_of(index)],
            (stage_right if right else stage_left).at[index % 2],
            final_sem.at[index],
            z + 1 if right else z - 1,
        )

    def onward(index, right):
        return remote(
            out.at[rows_of(index)],
            out.at[rows_of(index)],
            sent.at[2 + index % 2],
            final_sem.at[index],
            z + 1 if right else z - 1,
        )

    def load(index, right):
        landing = from_left if right else from_right
        return pltpu.make_async_copy(
            landing.at[rows_of(index)], inbox.at[0 if right else 1], load_sem.at[0 if right else 1]
        )

    def valid(index):
        return (index >= 0) & (index < pieces)

    def side(step, right):
        mine = low if right else high
        hops = z if right else last - z
        inner = step - hops * skew
        comes = hops > 0

        @pl.when(mine & valid(inner) & comes)
        def _():
            inward(inner, right).wait_recv()
            load(inner, right).start()

        @pl.when(mine & valid(inner))
        def _():
            @pl.when(inner >= 2)
            def _():
                inward(inner - 2, right).wait_send()

            @pl.when(comes)
            def _():
                load(inner, right).wait()
                value = own_piece(inner).astype(f32) + inbox[0 if right else 1].astype(f32)
                outbox[inner % 2] = value.astype(bf16)

            @pl.when(jnp.logical_not(comes))
            def _():
                outbox[inner % 2] = own_piece(inner)

            inward(inner, right).start()

        away = root - z if right else z - root
        outer = step - (turn_at + away) * skew

        @pl.when(mine & valid(outer))
        def _():
            onward(outer, not right).wait_recv()

            @pl.when(comes)
            def _():
                @pl.when(outer >= 2)
                def _():
                    onward(outer - 2, not right).wait_send()

                onward(outer, not right).start()

    def out_copy(index):
        return pltpu.make_async_copy(stage.at[index % 2], out.at[rows_of(index)], out_sem.at[index % 2])

    def stage_done(index):
        out_copy(index).wait()
        announce(index, False).wait_send()
        if root < last:
            announce(index, True).wait_send()

    def centre(step):
        index = step - turn_at * skew

        @pl.when(middle & valid(index))
        def _():
            inward(index, True).wait_recv()
            load(index, True).start()
            if root < last:
                inward(index, False).wait_recv()
                load(index, False).start()

            @pl.when(index >= 2)
            def _():
                stage_done(index - 2)

            load(index, True).wait()
            value = own_piece(index).astype(f32) + inbox[0].astype(f32)
            if root < last:
                load(index, False).wait()
                value = value + inbox[1].astype(f32)
            stage[index % 2] = value.astype(bf16)
            announce(index, False).start()
            if root < last:
                announce(index, True).start()
            out_copy(index).start()

    rhs_copy(0).start()
    each_source(0, lambda copy: copy.start())
    rhs_copy(1).start()
    take(0)
    rhs_copy(0).wait()

    @pl.loop(0, per_chunk)
    def _(part):
        multiply(0, part)

    pl.semaphore_wait(barrier, count - 1)
    small_in[z] = small[...]
    for shift in range(1, count):
        small_copy(z, lax.rem(z + shift, count)).start()

    @pl.loop(0, pieces + (turn_at + max(root, last - root)) * skew)
    def _(step):
        side(step, True)
        side(step, False)
        centre(step)
        chunk, part = step // per_chunk + 1, step % per_chunk

        @pl.when(chunk < total_chunks)
        def _():
            @pl.when(part == 0)
            def _():
                take(chunk)

                @pl.when(chunk == bounds[2])
                def _():
                    rhs_copy(1).wait()

            multiply(chunk, part)

    for shift in range(1, count):
        other = lax.rem(z + shift, count)
        small_copy(z, other).wait_send()
        small_copy(other, other).wait_recv()
    value = small_in[0]
    for k in range(1, count):
        value = value + small_in[k]
    small_out[...] = value
    for back in (2, 1):
        for right in (True, False):

            @pl.when(low if right else high)
            def _(right=right, back=back):
                inward(pieces - back, right).wait_send()

                @pl.when((z > 0) & (z < last))
                def _():
                    onward(pieces - back, not right).wait_send()

        @pl.when(middle)
        def _(back=back):
            stage_done(pieces - back)


def reduce_gradients(act, ctx, dproj, dhid, gy, std, gains, biases, sums, small, tasks):
    count = lax.axis_size("ctx")
    block, width = gy.shape[1:]
    bounds = [0]
    for source in (act, ctx, dproj, dhid):
        bounds.append(bounds[-1] + source.shape[2] // CHUNK)
    total = bounds[-1] * CHUNK
    pieces = total // PIECE
    ring = count // 2 * SKEW // (CHUNK // PIECE) + 3
    plan = (tuple(bounds), tasks, count, PIECE, SKEW, ring)
    anywhere = pl.BlockSpec(memory_space=pl.ANY)
    vmem = pl.BlockSpec(memory_space=pltpu.VMEM)
    result = jax.ShapeDtypeStruct((total, width), bf16)
    out, small_out, _, _ = pl.pallas_call(
        partial(reduce_kernel, plan),
        out_shape=[result, jax.ShapeDtypeStruct(small.shape, f32), result, result],
        in_specs=[anywhere] * 6 + [vmem] * 4,
        out_specs=[anywhere, vmem, anywhere, anywhere],
        scratch_shapes=[
            pltpu.VMEM((2, tasks, block, width), bf16),
            pltpu.VMEM((2, tasks, block, CHUNK), bf16),
            pltpu.VMEM((CHUNK, tasks * block), bf16),
            pltpu.VMEM((ring, CHUNK, width), bf16),
            pltpu.VMEM((2, PIECE, width), bf16),
            pltpu.VMEM((2, PIECE, width), bf16),
            pltpu.VMEM((2, PIECE, width), bf16),
            pltpu.VMEM((count,) + small.shape, f32),
            pltpu.SemaphoreType.DMA((2,)),
            pltpu.SemaphoreType.DMA((2,)),
            pltpu.SemaphoreType.DMA((pieces,)),
            pltpu.SemaphoreType.DMA((pieces,)),
            pltpu.SemaphoreType.DMA((pieces,)),
            pltpu.SemaphoreType.DMA((2,)),
            pltpu.SemaphoreType.DMA((4,)),
            pltpu.SemaphoreType.DMA((2,)),
            pltpu.SemaphoreType.DMA((2,)),
            pltpu.SemaphoreType.DMA((2,)),
            pltpu.SemaphoreType.DMA((count,)),
            pltpu.SemaphoreType.DMA((count,)),
        ],
        compiler_params=pltpu.CompilerParams(
            collective_id=7, has_side_effects=True, vmem_limit_bytes=60 * 1024 * 1024
        ),
        cost_estimate=pl.CostEstimate(
            flops=2 * total * width * tasks * block,
            bytes_accessed=8 * total * width,
            transcendentals=0,
        ),
        name="reduce_gradients",
    )(act, ctx, dproj, dhid, gy, std, gains, biases, sums, small)
    return out, small_out


def exchange(blocks, axis):
    count = blocks.shape[0]
    me = lax.axis_index(axis)
    got = [lax.dynamic_index_in_dim(blocks, me, 0, keepdims=False)]
    for shift in range(1, count):
        piece = lax.dynamic_index_in_dim(blocks, (me + shift) % count, 0, keepdims=False)
        got.append(lax.ppermute(piece, axis, [(k, (k + shift) % count) for k in range(count)]))
    ring = jnp.stack(got[::-1] + got[::-1])
    return lax.dynamic_slice_in_dim(ring, (count - 1 - me) % count, count, 0)


def body(
    inputs,
    out_grads,
    norm1_gain,
    norm1_bias,
    norm2_gain,
    norm2_bias,
    w_qkv,
    b_qkv,
    w_out,
    b_out,
    input_projection,
    input_bias_vector,
    down_projection,
    b_down,
):
    ctx_count = lax.axis_size("ctx")
    tensor = lax.axis_size("tensor")
    micro, _, rows, seqs, width = inputs.shape
    heads = w_qkv.shape[2]
    head_cols = w_qkv.shape[3]
    first = lax.axis_index("section") == 0
    per_device = micro * seqs // ctx_count
    blocks = ctx_count // 2
    own_rows = blocks * rows
    tasks = 2 * per_device

    chosen = jnp.where(first, inputs[:, 0], out_grads[:, 0])
    chosen = chosen.transpose(0, 2, 1, 3).reshape(per_device, ctx_count, rows, width)
    own_chosen = []
    for j in range(per_device):
        moved = exchange(chosen[j], "ctx").reshape(2, own_rows, width)
        own_chosen += [moved[0], moved[1]]

    wq = w_qkv[0].reshape(width, heads * head_cols)
    wi = input_projection[0]
    wo = w_out[0].reshape(-1, width)
    wd = down_projection[0]
    gain_one, bias_one, gain_two, bias_two = norm1_gain[0], norm1_bias[0], norm2_gain[0], norm2_bias[0]
    wq_scaled = (wq.astype(f32) * gain_one[:, None]).astype(bf16)
    wi_scaled = (wi.astype(f32) * gain_two[:, None]).astype(bf16)
    bq = b_qkv[0].reshape(1, -1) + jnp.sum(wq.astype(f32) * bias_one[:, None], axis=0, keepdims=True)
    bi = input_bias_vector + jnp.sum(wi.astype(f32) * bias_two[:, None], axis=0, keepdims=True)
    out_bias = (b_out[0] + b_down[0])[None]

    relative, tables = position_tables(None, blocks, rows, tensor)
    places_q, places_k = relative[:, None], relative[None, :]

    chips = tensor // 2
    chosen_rows = jnp.stack(own_chosen)
    stacked_tables = [jnp.stack(pair) for pair in zip(*tables)]
    std_all, qkv, act_all, dg_all, ctx_all, lse_all, states, arrive, _, _ = forward_pass(
        chosen_rows,
        wq_scaled,
        wi_scaled,
        wo,
        wd,
        bq,
        bi,
        out_bias,
        stacked_tables,
        places_q,
        places_k,
        chips,
        heads,
    )
    gains = jnp.stack([gain_one, gain_two])[:, None]
    gy_all, dproj_all, dh_all, dx_all, _, _, _, vectors = backward_pass(
        chosen_rows,
        chosen_rows,
        arrive,
        qkv,
        dg_all,
        ctx_all,
        lse_all,
        std_all,
        wq,
        wi,
        wo,
        wd,
        gains,
        stacked_tables,
        places_q,
        places_k,
        chips,
        heads,
    )
    vectors = vectors[:5]

    d_b_qkv = jnp.sum(dproj_all[:tasks], axis=(0, 1), dtype=f32)
    d_b_in = jnp.sum(dh_all[:tasks], axis=(0, 1), dtype=f32)
    units, inner = wd.shape[0], wo.shape[0]
    sums = jnp.concatenate([jnp.zeros((units + inner,), f32), d_b_qkv, d_b_in])[:, None]
    gains = jnp.stack([jnp.ones_like(gain_one), gain_one, gain_two])[:, None]
    biases = jnp.stack([jnp.zeros_like(bias_one), bias_one, bias_two])[:, None]
    mask = 1
    while mask < tensor:
        vectors = vectors + lax.ppermute(vectors, "tensor", [(k, k ^ mask) for k in range(tensor)])
        mask *= 2
    sides = jnp.concatenate([d_b_qkv, d_b_in])
    side_rows = -(-sides.shape[0] // width)
    small = jnp.zeros((-(-(5 + side_rows) // 8) * 8, width), f32)
    small = small.at[:5].set(vectors)
    small = small.at[5 : 5 + side_rows].set(
        jnp.pad(sides, (0, side_rows * width - sides.shape[0])).reshape(side_rows, width)
    )
    summed, small = reduce_gradients(
        act_all, ctx_all, dproj_all, dh_all, gy_all, std_all, gains, biases, sums, small, tasks
    )
    vectors = small[:5]
    sides = small[5 : 5 + side_rows].reshape(-1)
    d_b_qkv, d_b_in = sides[: d_b_qkv.shape[0]], sides[d_b_qkv.shape[0] : sides.shape[0]]
    d_b_in = d_b_in[: wi.shape[1]]
    d_w_down = summed[:units].astype(f32)
    d_w_out = summed[units : units + inner].astype(f32)
    summed = summed[units + inner :]
    d_w_qkv = summed[: wq.shape[1]].T.astype(f32)
    d_w_in = summed[wq.shape[1] :].T.astype(f32)

    def homeward(rows_of_tasks):
        stacked = rows_of_tasks.reshape(per_device, ctx_count, rows, width)
        moved = exchange(stacked.transpose(1, 0, 2, 3), "ctx")
        moved = moved.transpose(1, 0, 2, 3).reshape(micro, seqs, rows, width)
        return moved.transpose(0, 2, 1, 3)[None, :, None]

    states = homeward(states)
    input_grads = homeward(dx_all).astype(f32)
    return (
        states,
        input_grads,
        vectors[0][None],
        vectors[1][None],
        vectors[2][None],
        vectors[3][None],
        d_w_qkv.reshape(w_qkv.shape),
        d_b_qkv.reshape(b_qkv.shape),
        d_w_out.reshape(w_out.shape),
        vectors[4][None],
        d_w_in[None],
        d_b_in[None],
        d_w_down[None],
        vectors[4][None],
    )


def solution(mesh):
    return jax.shard_map(
        body,
        mesh=mesh,
        in_specs=(
            P(None, "ctx", "tensor", None, None),
            P(None, "ctx", "tensor", None, None),
            P("section", None),
            P("section", None),
            P("section", None),
            P("section", None),
            P("section", None, "tensor", None),
            P("section", "tensor", None),
            P("section", "tensor", None, None),
            P("section", None),
            P("section", None, "tensor"),
            P("section", "tensor"),
            P("section", "tensor", None),
            P("section", None),
        ),
        out_specs=(
            P("section", None, "ctx", "tensor", None, None),
            P("section", None, "ctx", "tensor", None, None),
            P("section", None),
            P("section", None),
            P("section", None),
            P("section", None),
            P("section", None, "tensor", None),
            P("section", "tensor", None),
            P("section", "tensor", None, None),
            P("section", None),
            P("section", None, "tensor"),
            P("section", "tensor"),
            P("section", "tensor", None),
            P("section", None),
        ),
        check_vma=False,
    )
```

time: 2190 us -> 1760 us (0.80)
  waiting for transfers between devices: 530 us -> 56.6 us
  Pallas kernels: 1190 us -> 1460 us
  other arithmetic: 200 us -> 91.1 us
  starting transfers between devices: 109 us -> 30.2 us
  local copies, waits for them, and re-layouts: 135 us -> 111 us
    ppermute x96 -> x0, waiting for transfers between devices: 440 us -> none  [the longest x40 322 us: shift_chips(): lax.ppermute(v, 'tensor', [(k, (k + 2 * shift) % tensor) for k in range(t...]
    pallas_call x60 -> x2, Pallas kernels: 600 us -> 743 us  [the longest x1 495 us: backward_pass(): pl.pallas_call(partial(backward_kernel, (tasks, chips, rows, heads)), out...]
    pallas_call x1, Pallas kernels: 593 us -> 713 us  [reduce_gradients(): pl.pallas_call(partial(reduce_kernel, plan), out_shape=[result, jax.Shape...]
    ppermute x96 -> x0, starting transfers between devices: 85.5 us -> none  [the longest x40 37.8 us: shift_chips(): lax.ppermute(v, 'tensor', [(k, (k + 2 * shift) % tensor) for k in range(t...]
    reduce_sum x52 -> x0, other arithmetic: 37.1 us -> none  [the longest x17 19.4 us: standardize(): average = jnp.mean(values, axis=-1, keepdims=True)]
    ppermute x18, waiting for transfers between devices: 86.6 us -> 56.6 us  [exchange(): lax.ppermute(piece, axis, [(k, (k + shift) % count) for k in range(count)])]
    another operation x83 -> x6, other arithmetic: 31.2 us -> 3.01 us  [the longest x5 2.99 us: body(): stacked_tables = [jnp.stack(pair) for pair in zip(*tables)]]
    unnamed x347 -> x100, local copies, waits for them, and re-layouts: 100 us -> 86.6 us
  transfers between devices with their start and end apart: 116 -> 20, of which waited for: 60 -> 4; matrix products, arithmetic and copies ran while one was open for 11% -> 7% of each run, Pallas kernels for 46% -> 41%
where the time goes in v3:
time: 1760 us; the launch traced here: 1750 us
  Pallas kernels  1460 us (83%)
  local copies, waits for them, and re-layouts  111 us (6%)
  other arithmetic  91.1 us (5%)
  waiting for transfers between devices  56.6 us (3%)
  starting transfers between devices  30.2 us (2%)
    pallas_call x1, Pallas kernels, reduce_gradients(): pl.pallas_call(partial(reduce_kernel, plan), out_shape=[result, jax.Shape...  713 us
    pallas_call x1, Pallas kernels, backward_pass(): pl.pallas_call(partial(backward_kernel, (tasks, chips, rows, heads)), out...  495 us
    pallas_call x1, Pallas kernels, forward_pass(): pl.pallas_call(partial(forward_kernel, (tasks, chips, rows, heads)), out_...  247 us
    unnamed x100, local copies, waits for them, and re-layouts  86.6 us
    ppermute x18, waiting for transfers between devices, exchange(): lax.ppermute(piece, axis, [(k, (k + shift) % count) for k in range(count)])  56.6 us
  transfers between devices with their start and end apart: 20, of which 4 were waited for; matrix products, arithmetic and copies ran while one was open for 7% of the time, Pallas kernels for 41%

profile of v3, /device:TPU:0, one launch (start us, length us, event | category | flops | bytes accessed | tf_op | source)
XLA Modules:
  0.0 1746.8 jit_solution(5284866696497465146)
XLA Ops:
  0.7 16.2 fusion.2
  16.9 1.4 fusion.14
  18.3 2.0 dynamic-slice_bitcast_fusion.7
  20.3 5.0 collective-permute-start.9
  25.4 1.0 collective-permute-start.11
  26.4 0.9 dynamic-slice_bitcast_fusion.10
  27.3 3.3 collective-permute-start.6
  30.6 1.1 collective-permute-start.7
  31.7 0.9 dynamic-slice_bitcast_fusion.13
  33.0 4.3 copy.43
  37.7 8.7 multiply_reduce_fusion
  46.6 1.9 multiply_sine_fusion.1
  50.5 3.8 multiply_convert_fusion.wq_all
  54.6 8.7 fusion.1
  64.1 0.9 add.269.pq
  69.6 3.9 collective-permute-start.3
  73.4 1.0 bitcast_dynamic-update-slice_fusion.38
  74.4 8.3 collective-permute-done.3
  82.7 1.7 collective-permute-start.4
  84.8 1.0 bitcast_dynamic-update-slice_fusion.28
  85.8 3.5 collective-permute-start
  89.4 1.0 bitcast_dynamic-update-slice_fusion.26
  90.4 1.0 bitcast_dynamic-update-slice_fusion.36
  91.4 1.1 collective-permute-start.2
  92.5 12.6 collective-permute-done.4
  105.4 1.0 bitcast_dynamic-update-slice_fusion.29
  106.3 1.0 bitcast_dynamic-update-slice_fusion.27
  107.3 1.0 bitcast_dynamic-update-slice_fusion.39
  108.3 1.0 bitcast_dynamic-update-slice_fusion.37
  109.7 14.9 collective-permute-done.1
  125.5 2.0 copy-done.9
  127.5 247.5 %forward_pass.1 = (bf16[8,512,2048]{2,1,0:T(8,128)(2,1)}, bf16[8,512,1536]{2,1,0:T(8,128)(2,1)}, bf16[8,512,2048]{2,1,0:T(8,128)(2,1)}, bf16[8,512,2048]{2,1,0:T...) custom-call(bf16[8,128,2048]{2,1,0:T(8,128)(2,1)} %copy-done.9, ...), custom_call_target="tpu_custom_call" | custom-call | flops 103079215104 | bytes 134217728 | tf_op jit(solution)/shard_map/forward_pass/pallas_call | solution.py:459
  375.0 495.3 %backward_pass.1 = (bf16[8,512,2048]{2,1,0:T(8,128)(2,1)}, bf16[8,512,1536]{2,1,0:T(8,128)(2,1)}, bf16[8,512,2048]{2,1,0:T(8,128)(2,1)}, bf16[8,128,2048]{2,1,0:...) custom-call(bf16[8,128,2048]{2,1,0:T(8,128)(2,1)} %copy-done.9, ...), custom_call_target="tpu_custom_call" | custom-call | flops 103079215104 | bytes 167772160 | tf_op jit(solution)/shard_map/backward_pass/pallas_call | solution.py:760
  870.2 7.4 convert_reduce_fusion
  877.7 6.5 convert_reduce_fusion.1
  884.2 1.7 dynamic-slice_bitcast_fusion.4
  886.0 2.2 copy.36.sums
  888.2 3.9 collective-permute-start.13
  892.0 2.0 collective-permute-start.14
  894.1 1.1 collective-permute-start.19
  895.1 3.6 dynamic-slice_bitcast_fusion.1
  898.8 1.8 collective-permute-start.15
  901.6 713.0 %reduce_gradients.1 = (bf16[6144,2048]{1,0:T(8,128)(2,1)}, f32[8,2048]{1,0:T(8,128)}, bf16[6144,2048]{1,0:T(8,128)(2,1)}, bf16[6144,2048]{1,0:T(8,128)(2,1)}) custom-call(bf16[8,512,2048]{2,1,0:T(8,128)(2,1)} %get-tuple-element.61.act, bf16[8,512,512]{2,1,0:T(8,128)(2,1)} %get-tuple-element.57.ctx_all.ctx, bf16[8,512,1536]{2,1,0:T(8,128)(2,1)} %get-tuple-element.62.dproj, ...), custom_call_target="tpu_custom_call" | custom-call | flops 103079215104 | bytes 100663296 | tf_op jit(solution)/shard_map/reduce_gradients/pallas_call | solution.py:1097
  1614.6 17.0 bitcast_convert_fusion
  1631.7 8.9 slice_convert_fusion
  1641.2 1.7 slice.172
  1643.6 17.6 %copy.40 = f32[1,2048,2048]{2,1,0:T(8,128)} copy(f32[1,2048,2048]{1,2,0:T(8,128)} %get-tuple-element.97) | data formatting | bytes 33554432
  1661.2 19.2 %copy.39 = f32[1,2048,2,768]{3,2,1,0:T(2,128)} copy(f32[1,2048,2,768]{1,3,2,0:T(8,128)} %bitcast.200) | data formatting | bytes 25165824
  1680.4 2.5 convert.8
  1683.8 1.4 bitcast_dynamic-update-slice_fusion.8
  1685.2 1.4 bitcast_dynamic-update-slice_fusion.12
  1686.7 1.4 bitcast_dynamic-update-slice_fusion.10
  1688.2 1.3 bitcast_dynamic-update-slice_fusion.6
  1689.5 20.7 %collective-permute-done.17 = bf16[4,64,2048]{2,1,0:T(8,128)(2,1)S(1)} collective-permute-done((bf16[4,64,2048]{2,1,0:T(8,128)(2,1)}, bf16[4,64,2048]{2,1,0:T(8,128)(2,1)S(1)}, u32[]{:S(2)}, u32[]{:S(2)}) %collective-permute-start.17) | collective-permute-done | bytes 1048608 | tf_op jit(solution)/shard_map/ppermute | solution.py:1143
  1710.6 2.1 bitcast_dynamic-update-slice_fusion.9
  1712.6 2.1 bitcast_dynamic-update-slice_fusion.7
  1715.0 4.3 convert_bitcast_fusion.1
  1719.3 12.2 copy.38
  1731.5 1.1 bitcast_dynamic-update-slice_fusion.15
  1732.5 2.3 bitcast_dynamic-update-slice_fusion.13
  1734.8 2.3 bitcast_dynamic-update-slice_fusion.11
  1737.2 1.1 bitcast_dynamic-update-slice_fusion.3
  1738.3 2.5 dynamic-slice_bitcast_fusion
  1740.8 5.3 copy.37
  (153 shorter events, 14.6 us)
Async XLA Ops:
  20.3 49.1 %collective-permute-start.9 = (bf16[64,2048]{1,0:T(8,128)(2,1)}, bf16[64,2048]{1,0:T(8,128)(2,1)S(1)}, u32[]{:S(2)}, u32[]{:S(2)}) collective-permute-start(bf16[64,2048]{1,0:T(8,128)(2,1)} %get-tuple-element.120), channel_id=1, source_target_pairs={{0,3},{1,0},{2,1},{3,2},{4,7},{5,4},{6,5},{7,6},{8,11},{9,8},{10,9... | collective-permute-start | bytes 786440 | tf_op jit(solution)/shard_map/ppermute | solution.py:1143
  25.4 59.1 %collective-permute-start.10 = (bf16[64,2048]{1,0:T(8,128)(2,1)}, bf16[64,2048]{1,0:T(8,128)(2,1)}, u32[]{:S(2)}, u32[]{:S(2)}) collective-permute-start(bf16[64,2048]{1,0:T(8,128)(2,1)} %get-tuple-element.119), channel_id=1, source_target_pairs={{0,2},{1,3},{2,0},{3,1},{4,6},{5,7},{6,4},{7,5},{8,10},{9,11},{10,... | collective-permute-start | bytes 786440 | tf_op jit(solution)/shard_map/ppermute | solution.py:1143
  25.4 60.4 %collective-permute-start.11 = (bf16[64,2048]{1,0:T(8,128)(2,1)}, bf16[64,2048]{1,0:T(8,128)(2,1)}, u32[]{:S(2)}, u32[]{:S(2)}) collective-permute-start(bf16[64,2048]{1,0:T(8,128)(2,1)} %get-tuple-element.118), channel_id=1, source_target_pairs={{0,1},{1,2},{2,3},{3,0},{4,5},{5,6},{6,7},{7,4},{8,9},{9,10},{10,1... | collective-permute-start | bytes 786440 | tf_op jit(solution)/shard_map/ppermute | solution.py:1143
  27.3 42.3 %collective-permute-start.6 = (bf16[64,2048]{1,0:T(8,128)(2,1)}, bf16[64,2048]{1,0:T(8,128)(2,1)}, u32[]{:S(2)}, u32[]{:S(2)}) collective-permute-start(bf16[64,2048]{1,0:T(8,128)(2,1)} %get-tuple-element.123), channel_id=1, source_target_pairs={{0,3},{1,0},{2,1},{3,2},{4,7},{5,4},{6,5},{7,6},{8,11},{9,8},{10,9... | collective-permute-start | bytes 786440 | tf_op jit(solution)/shard_map/ppermute | solution.py:1143
  30.6 59.8 %collective-permute-start.7 = (bf16[64,2048]{1,0:T(8,128)(2,1)}, bf16[64,2048]{1,0:T(8,128)(2,1)}, u32[]{:S(2)}, u32[]{:S(2)}) collective-permute-start(bf16[64,2048]{1,0:T(8,128)(2,1)} %get-tuple-element.122), channel_id=1, source_target_pairs={{0,2},{1,3},{2,0},{3,1},{4,6},{5,7},{6,4},{7,5},{8,10},{9,11},{10,... | collective-permute-start | bytes 786440 | tf_op jit(solution)/shard_map/ppermute | solution.py:1143
  33.0 4.3 slice-start
  33.0 4.7 slice-start.1
  33.0 4.7 copy-start.12
  37.3 13.2 copy-start
  37.3 9.1 copy-start.6
  37.3 9.1 copy-start.7
  50.5 3.8 copy-start.13
  54.5 11.2 copy-start.18
  54.6 13.0 copy-start.15
  54.6 14.2 copy-start.16
  54.6 14.2 copy-start.17
  67.6 37.6 %copy-start.4 = (bf16[1,4,64,2048]{3,2,1,0:T(8,128)(2,1)S(1)}, bf16[1,4,64,2048]{3,2,1,0:T(8,128)(2,1)}, u32[]{:S(2)}) copy-start(bf16[1,4,64,2048]{3,2,1,0:T(8,128)(2,1)} %get-tuple-element.106) | copy-start | bytes 3145732
  69.5 21.9 %collective-permute-start.8 = (bf16[64,2048]{1,0:T(8,128)(2,1)}, bf16[64,2048]{1,0:T(8,128)(2,1)S(1)}, u32[]{:S(2)}, u32[]{:S(2)}) collective-permute-start(bf16[64,2048]{1,0:T(8,128)(2,1)} %get-tuple-element.121), channel_id=1, source_target_pairs={{0,1},{1,2},{2,3},{3,0},{4,5},{5,6},{6,7},{7,4},{8,9},{9,10},{10,1... | collective-permute-start | bytes 786440 | tf_op jit(solution)/shard_map/ppermute | solution.py:1143
  69.6 13.1 collective-permute-start.3
  82.7 22.5 %collective-permute-start.4 = (bf16[64,2048]{1,0:T(8,128)(2,1)}, bf16[64,2048]{1,0:T(8,128)(2,1)S(1)}, u32[]{:S(2)}, u32[]{:S(2)}) collective-permute-start(bf16[64,2048]{1,0:T(8,128)(2,1)} %get-tuple-element.125), channel_id=1, source_target_pairs={{0,2},{1,3},{2,0},{3,1},{4,6},{5,7},{6,4},{7,5},{8,10},{9,11},{10,... | collective-permute-start | bytes 786440 | tf_op jit(solution)/shard_map/ppermute | solution.py:1143
  84.4 20.8 %collective-permute-start.5 = (bf16[64,2048]{1,0:T(8,128)(2,1)}, bf16[64,2048]{1,0:T(8,128)(2,1)S(1)}, u32[]{:S(2)}, u32[]{:S(2)}) collective-permute-start(bf16[64,2048]{1,0:T(8,128)(2,1)} %get-tuple-element.124), channel_id=1, source_target_pairs={{0,1},{1,2},{2,3},{3,0},{4,5},{5,6},{6,7},{7,4},{8,9},{9,10},{10,1... | collective-permute-start | bytes 786440 | tf_op jit(solution)/shard_map/ppermute | solution.py:1143
  85.8 23.7 %collective-permute-start = (bf16[64,2048]{1,0:T(8,128)(2,1)S(1)}, bf16[64,2048]{1,0:T(8,128)(2,1)S(1)}, u32[]{:S(2)}, u32[]{:S(2)}) collective-permute-start(bf16[64,2048]{1,0:T(8,128)(2,1)S(1)} %get-tuple-element.129), channel_id=1, source_target_pairs={{0,3},{1,0},{2,1},{3,2},{4,7},{5,4},{6,5},{7,6},{8,11},{9,8},{10,9... | collective-permute-start | bytes 786440 | tf_op jit(solution)/shard_map/ppermute | solution.py:1143
  90.3 34.3 %collective-permute-start.1 = (bf16[64,2048]{1,0:T(8,128)(2,1)S(1)}, bf16[64,2048]{1,0:T(8,128)(2,1)S(1)}, u32[]{:S(2)}, u32[]{:S(2)}) collective-permute-start(bf16[64,2048]{1,0:T(8,128)(2,1)S(1)} %get-tuple-element.128), channel_id=1, source_target_pairs={{0,2},{1,3},{2,0},{3,1},{4,6},{5,7},{6,4},{7,5},{8,10},{9,11},{10,... | collective-permute-start | bytes 786440 | tf_op jit(solution)/shard_map/ppermute | solution.py:1143
  91.4 33.4 %collective-permute-start.2 = (bf16[64,2048]{1,0:T(8,128)(2,1)S(1)}, bf16[64,2048]{1,0:T(8,128)(2,1)S(1)}, u32[]{:S(2)}, u32[]{:S(2)}) collective-permute-start(bf16[64,2048]{1,0:T(8,128)(2,1)S(1)} %get-tuple-element.127), channel_id=1, source_target_pairs={{0,1},{1,2},{2,3},{3,0},{4,5},{5,6},{6,7},{7,4},{8,9},{9,10},{10,1... | collective-permute-start | bytes 786440 | tf_op jit(solution)/shard_map/ppermute | solution.py:1143
  125.5 2.0 copy-start.9
  877.6 6.5 copy-start.8
  877.6 6.6 copy-start.1
  884.1 9.9 collective-permute-start.18
  888.2 795.4 %collective-permute-start.12 = (bf16[4,64,2048]{2,1,0:T(8,128)(2,1)}, bf16[4,64,2048]{2,1,0:T(8,128)(2,1)S(1)}, u32[]{:S(2)}, u32[]{:S(2)}) collective-permute-start(bf16[4,64,2048]{2,1,0:T(8,128)(2,1)} %get-tuple-element.105), channel_id=1, source_target_pairs={{0,3},{1,0},{2,1},{3,2},{4,7},{5,4},{6,5},{7,6},{8,11},{9,8},{10,9... | collective-permute-start | bytes 3145736 | tf_op jit(solution)/shard_map/ppermute | solution.py:1143
  888.2 797.1 %collective-permute-start.13 = (bf16[4,64,2048]{2,1,0:T(8,128)(2,1)}, bf16[4,64,2048]{2,1,0:T(8,128)(2,1)}, u32[]{:S(2)}, u32[]{:S(2)}) collective-permute-start(bf16[4,64,2048]{2,1,0:T(8,128)(2,1)} %get-tuple-element.104), channel_id=1, source_target_pairs={{0,2},{1,3},{2,0},{3,1},{4,6},{5,7},{6,4},{7,5},{8,10},{9,11},{10,... | collective-permute-start | bytes 3145736 | tf_op jit(solution)/shard_map/ppermute | solution.py:1143
  892.0 794.7 %collective-permute-start.14 = (bf16[4,64,2048]{2,1,0:T(8,128)(2,1)}, bf16[4,64,2048]{2,1,0:T(8,128)(2,1)}, u32[]{:S(2)}, u32[]{:S(2)}) collective-permute-start(bf16[4,64,2048]{2,1,0:T(8,128)(2,1)} %get-tuple-element.103), channel_id=1, source_target_pairs={{0,1},{1,2},{2,3},{3,0},{4,5},{5,6},{6,7},{7,4},{8,9},{9,10},{10,1... | collective-permute-start | bytes 3145736 | tf_op jit(solution)/shard_map/ppermute | solution.py:1143
  894.1 6.5 collective-permute-start.19
  898.8 785.0 %collective-permute-start.15 = (bf16[4,64,2048]{2,1,0:T(8,128)(2,1)}, bf16[4,64,2048]{2,1,0:T(8,128)(2,1)}, u32[]{:S(2)}, u32[]{:S(2)}) collective-permute-start(bf16[4,64,2048]{2,1,0:T(8,128)(2,1)} %get-tuple-element.102), channel_id=1, source_target_pairs={{0,3},{1,0},{2,1},{3,2},{4,7},{5,4},{6,5},{7,6},{8,11},{9,8},{10,9... | collective-permute-start | bytes 3145736 | tf_op jit(solution)/shard_map/ppermute | solution.py:1143
  900.6 787.6 %collective-permute-start.16 = (bf16[4,64,2048]{2,1,0:T(8,128)(2,1)}, bf16[4,64,2048]{2,1,0:T(8,128)(2,1)}, u32[]{:S(2)}, u32[]{:S(2)}) collective-permute-start(bf16[4,64,2048]{2,1,0:T(8,128)(2,1)} %get-tuple-element.101), channel_id=1, source_target_pairs={{0,2},{1,3},{2,0},{3,1},{4,6},{5,7},{6,4},{7,5},{8,10},{9,11},{10,... | collective-permute-start | bytes 3145736 | tf_op jit(solution)/shard_map/ppermute | solution.py:1143
  901.0 0.6 copy-start.10
  1631.7 8.9 copy-start.11
  1641.2 104.8 %copy-start.14 = (f32[1,2048]{1,0:T(1,128)}, f32[1,2048]{1,0:T(1,128)S(1)}, u32[]{:S(2)}) copy-start(f32[1,2048]{1,0:T(1,128)S(1)} %get-tuple-element.182) | copy-start | bytes 24580
  1683.5 26.7 %collective-permute-start.17 = (bf16[4,64,2048]{2,1,0:T(8,128)(2,1)}, bf16[4,64,2048]{2,1,0:T(8,128)(2,1)S(1)}, u32[]{:S(2)}, u32[]{:S(2)}) collective-permute-start(bf16[4,64,2048]{2,1,0:T(8,128)(2,1)} %get-tuple-element.100), channel_id=1, source_target_pairs={{0,1},{1,2},{2,3},{3,0},{4,5},{5,6},{6,7},{7,4},{8,9},{9,10},{10,1... | collective-permute-start | bytes 3145736 | tf_op jit(solution)/shard_map/ppermute | solution.py:1143
  1683.8 26.5 %copy-start.3 = (bf16[8,128,2048]{2,1,0:T(8,128)(2,1)S(1)}, bf16[8,128,2048]{2,1,0:T(8,128)(2,1)}, u32[]{:S(2)}) copy-start(bf16[8,128,2048]{2,1,0:T(8,128)(2,1)} %get-tuple-element.60) | copy-start | bytes 12582916
  1685.2 25.1 %copy-start.2 = (bf16[8,128,2048]{2,1,0:T(8,128)(2,1)S(1)}, bf16[8,128,2048]{2,1,0:T(8,128)(2,1)}, u32[]{:S(2)}) copy-start(bf16[8,128,2048]{2,1,0:T(8,128)(2,1)} %get-tuple-element.53) | copy-start | bytes 12582916
  1710.6 4.3 copy-start.5

commit v4 on v3

--- a/solution.py
+++ b/solution.py
@@ -35,10 +35,10 @@
 def position_tables(section_rows, blocks, rows, tensor):
     half = ROT // 2
     frequency = 1.0 / 10000.0 ** (jnp.arange(0, ROT, 2, dtype=f32) / ROT)
-    t, c, i = jnp.meshgrid(
-        jnp.arange(tensor), jnp.arange(blocks), jnp.arange(rows), indexing="ij"
+    core, chip, c, i = jnp.meshgrid(
+        jnp.arange(2), jnp.arange(tensor // 2), jnp.arange(blocks), jnp.arange(rows), indexing="ij"
     )
-    relative = (c * (rows * tensor) + t * rows + i).reshape(-1).astype(jnp.int32)
+    relative = (c * (rows * tensor) + (chip * 2 + core) * rows + i).reshape(-1).astype(jnp.int32)
     tables = []
     for part in range(2):
         places = (relative + part * blocks * rows * tensor).astype(f32)
@@ -83,7 +83,15 @@
         return lax.rem(self.index + 2 * shift, self.total)
 
     def part(self, member):
-        return pl.ds(pl.multiple_of(member * self.rows, self.rows), self.rows)
+        at = (member % 2) * self.chips + member // 2
+        return pl.ds(pl.multiple_of(at * self.rows, self.rows), self.rows)
+
+    def share(self, core):
+        size = self.chips * self.rows
+        return pl.ds(pl.multiple_of(core * size, size), size)
+
+    def of_chip(self, chip):
+        return pl.ds(pl.multiple_of(chip * self.rows, self.rows), self.rows)
 
     def remote(self, source, target, sent, arrived, **device):
         return pltpu.make_async_remote_copy(
@@ -95,9 +103,10 @@
             device_id_type=pl.DeviceIdType.MESH,
         )
 
-    def greet(self):
+    def greet(self, line):
         barrier = pltpu.get_barrier_semaphore()
         peers = [{"section": 1 - self.section}, {"tensor": self.mate}]
+        peers += [{"ctx": other} for other in line.others()]
         peers += [{"tensor": self.mate_on(shift)} for shift in range(1, self.chips)]
         for peer in peers:
             pl.semaphore_signal(barrier, inc=1, device_id=peer, device_id_type=pl.DeviceIdType.MESH)
@@ -138,7 +147,7 @@
 
     def give_low(self, task, shift):
         return self.remote(
-            self.low.at[lax.rem(self.chip + shift, self.chips)],
+            self.low.at[self.of_chip(lax.rem(self.chip + shift, self.chips))],
             self.chip_land.at[task, shift - 1],
             self.put_low.at[shift - 1],
             self.got_low.at[task, shift - 1],
@@ -151,6 +160,126 @@
         )
 
 
+class Line:
+    def __init__(self, rows):
+        self.rows = rows
+        self.count = lax.axis_size("ctx")
+        self.blocks = self.count // 2
+        self.z = lax.axis_index("ctx")
+
+    def others(self):
+        return [lax.rem(self.z + shift, self.count) for shift in range(1, self.count)]
+
+    def remote(self, source, target, sent, arrived, device):
+        return pltpu.make_async_remote_copy(
+            src_ref=source,
+            dst_ref=target,
+            send_sem=sent,
+            recv_sem=arrived,
+            device_id={"ctx": device},
+            device_id_type=pl.DeviceIdType.MESH,
+        )
+
+    def block(self, at):
+        return pl.ds(pl.multiple_of(at * self.rows, self.rows), self.rows)
+
+    def set_in(self, chosen, landed, put, got, kept):
+        self.chosen, self.landed, self.put_in, self.got_in, self.kept_in = chosen, landed, put, got, kept
+
+    def bring(self, j, shift, source=None):
+        source = self.z if source is None else source
+        half = source // self.blocks
+        return self.remote(
+            self.chosen.at[j, lax.rem(self.z + shift, self.count)],
+            self.landed.at[2 * j + half, self.block(source - half * self.blocks)],
+            self.put_in.at[j, shift - 1],
+            self.got_in.at[j, source],
+            lax.rem(self.z + shift, self.count),
+        )
+
+    def bring_own(self, j):
+        half = self.z // self.blocks
+        return pltpu.make_async_copy(
+            self.chosen.at[j, self.z],
+            self.landed.at[2 * j + half, self.block(self.z - half * self.blocks)],
+            self.kept_in.at[j],
+        )
+
+    def bring_start(self, j):
+        for shift in range(1, self.count):
+            self.bring(j, shift).start()
+        self.bring_own(j).start()
+
+    def bring_wait(self, task):
+        j, half = task // 2, task % 2
+        for k in range(self.blocks):
+            source = half * self.blocks + k
+
+            @pl.when(source != self.z)
+            def _():
+                self.bring(j, 1, source).wait_recv()
+
+            @pl.when(source == self.z)
+            def _():
+                self.bring_own(j).wait()
+
+    def bring_done(self, count):
+        for j in range(count):
+            for shift in range(1, self.count):
+                self.bring(j, shift).wait_send()
+
+    def set_home(self, handed, home, put, got, kept):
+        self.handed, self.home, self.put_home, self.got_home, self.kept_home = handed, home, put, got, kept
+
+    def take_home(self, task, k, source=None):
+        j, half = task // 2, task % 2
+        source = self.z if source is None else source
+        return self.remote(
+            self.handed.at[pl.ds(k * self.rows, self.rows)],
+            self.home.at[j * self.count + source],
+            self.put_home.at[k],
+            self.got_home.at[j, source],
+            half * self.blocks + k,
+        )
+
+    def keep_home(self, task, k):
+        return pltpu.make_async_copy(
+            self.handed.at[pl.ds(k * self.rows, self.rows)],
+            self.home.at[(task // 2) * self.count + self.z],
+            self.kept_home,
+        )
+
+    def home_each(self, task, begin):
+        half = task % 2
+        for k in range(self.blocks):
+            there = half * self.blocks + k
+
+            @pl.when(there != self.z)
+            def _():
+                copy = self.take_home(task, k)
+                copy.start() if begin else copy.wait_send()
+
+            @pl.when(there == self.z)
+            def _():
+                copy = self.keep_home(task, k)
+                copy.start() if begin else copy.wait()
+
+    def home_wait(self, tasks):
+        for j in range(tasks // 2):
+            for other in self.others():
+                self.take_home(2 * j, 0, other).wait_recv()
+
+
+def line_semaphores(tasks, count):
+    dma = pltpu.SemaphoreType.DMA
+    half = tasks // 2
+    return [dma((half, count - 1)), dma((half, count)), dma((half,))], [
+        dma((count // 2,)),
+        dma((half, count)),
+        dma,
+    ]
+
+
 def reduce_first(moves, task, mine, core_in, load_sem):
     moves.give_theirs(task).wait_recv()
     load = pltpu.make_async_copy(moves.core_land.at[task], core_in, load_sem)
@@ -162,10 +291,9 @@
             moves.give_low(task - 1, shift).wait_send()
 
     load.wait()
-    for j in range(moves.chips):
-        value = mine[j] + core_in[j].astype(f32)
-        mine[j] = value
-        moves.low[j] = value.astype(bf16)
+    value = mine[...] + core_in[...].astype(f32)
+    mine[...] = value
+    moves.low[...] = value.astype(bf16)
     for shift in range(1, moves.chips):
         moves.give_low(task, shift).start()
 
@@ -176,7 +304,7 @@
     load = pltpu.make_async_copy(moves.chip_land.at[task], chip_in, load_sem)
     load.start()
     load.wait()
-    value = mine[moves.chip]
+    value = mine[moves.of_chip(moves.chip), :]
     for shift in range(1, moves.chips):
         value = value + chip_in[shift - 1].astype(f32)
     return value
@@ -229,12 +357,16 @@
 
 
 def forward_kernel(
-    plan, xin, wq_all, wi_all, wo_all, wd_all, bq, bi, out_bias, cosine, ahead, behind, pq, pk,
-    land, qkv_all, act_all, dg_all, ctx_all, lse_all, states, arrive, core_land, chip_land,
-    wq, wi, wo, wd, std, qkv, act, dg, ctx, lse, kept, own, theirs, mine, core_in, low, chip_in, handed,
-    weight_sem, load_sem, store_sem, keep_sem, state_sem, *sems,
+    plan, chosen, wq_all, wi_all, wo_all, wd_all, bq_in, bi_in, norms, out_bias, cosine, ahead, behind, pq, pk,
+    land, qkv_all, act_all, dg_all, ctx_all, lse_all, xin, home, arrive, core_land, chip_land,
+    wq, wi, wo, wd, bq, bi, std, qkv, act, dg, ctx, lse, kept, own, theirs, mine, core_in, low, chip_in, handed,
+    weight_sem, load_sem, store_sem, keep_sem,
+    put_in, got_in, kept_in, put_home, got_home, kept_home, *sems,
 ):
     tasks, chips, rows, heads = plan
+    line = Line(chosen.shape[2])
+    line.set_in(chosen, xin, put_in, got_in, kept_in)
+    line.set_home(handed, home, put_home, got_home, kept_home)
     size = wq.shape[1] // (3 * heads)
     moves = Moves(
         (tasks, chips, rows), lambda task: task, land, arrive, core_land, chip_land, own, theirs, low, handed, sems
@@ -246,12 +378,26 @@
         pltpu.make_async_copy(a, b, weight_sem.at[k])
         for k, (a, b) in enumerate(((wq_all, wq), (wi_all, wi), (wo_all, wo), (wd_all, wd)))
     ]
+    moves.greet(line)
+    line.bring_start(0)
     for copy in weights:
         copy.start()
-    moves.greet()
 
     def valid(task):
         return (task >= 0) & (task < tasks)
+
+    def fold(weight, bias_in, bias, gain_column):
+        bias[...] = bias_in[...]
+        step = 256
+
+        @pl.loop(0, weight.shape[0] // step)
+        def _(k):
+            at = pl.ds(pl.multiple_of(k * step, step), step)
+            value = weight[at, :].astype(f32)
+            gain = norms[at, gain_column : gain_column + 1]
+            shift = norms[at, gain_column + 1 : gain_column + 2]
+            bias[...] += jnp.sum(value * shift, axis=0, keepdims=True)
+            weight[at, :] = (value * gain).astype(bf16)
 
     def store(k, task):
         return pltpu.make_async_copy(
@@ -306,9 +452,12 @@
             act[:, columns] = (h * phi).astype(bf16)
             dg[:, columns] = (phi + h * density).astype(bf16)
 
-    def branch_rows(member):
-        at = moves.part(member)
-        return dot(ctx[at, :], wo[...]) + dot(act[at, :], wd[...])
+    def branch_rows(core, result):
+        at = moves.share(core)
+        for column in range(0, wo.shape[1], 512):
+            columns = slice(column, column + 512)
+            value = dot(ctx[at, :], wo[:, columns]) + dot(act[at, :], wd[:, columns])
+            result[:, columns] = value.astype(result.dtype)
 
     @pl.loop(0, tasks + LAG + 2)
     def _(step):
@@ -319,9 +468,9 @@
         def load_rows(task, held):
             return pltpu.make_async_copy(held.at[task], kept.at[task % 4], load_sem.at[0])
 
-        @when(valid(g) & first)
-        def _():
-            load_rows(g, xin).start()
+        @when((step % 2 == 0) & (step // 2 + 1 < tasks // 2))
+        def _():
+            line.bring_start(step // 2 + 1)
 
         @when(valid(r))
         def _():
@@ -333,10 +482,6 @@
             load = pltpu.make_async_copy(land.at[c], std, load_sem.at[2])
             load.start()
 
-            @when(c == 0)
-            def _():
-                weights[0].wait()
-
             @when(c >= 1)
             def _():
                 for k in range(5):
@@ -357,8 +502,16 @@
             store(3, c).start()
             store(4, c).start()
 
+        @when(step < tasks)
+        def _():
+            line.bring_wait(step)
+
         @when(valid(g))
         def _():
+            @when(first)
+            def _():
+                load_rows(g, xin).start()
+
             @when(jnp.logical_not(first))
             def _():
                 moves.hand(g).wait_recv()
@@ -373,12 +526,17 @@
             own[...] = standardize(kept[g % 4])[0].astype(bf16)
             gather_start(moves, g, keep_sem)
 
+        @when(step == 0)
+        def _():
+            weights[0].wait()
+            fold(wq, bq_in, bq, 0)
+            weights[1].wait()
+            fold(wi, bi_in, bi, 2)
+            weights[2].wait()
+            weights[3].wait()
+
         @when(valid(c))
         def _():
-            @when(c == 0)
-            def _():
-                weights[1].wait()
-
             expand()
             store(1, c).start()
             store(2, c).start()
@@ -389,35 +547,29 @@
 
             @when(r >= 1)
             def _():
-                pltpu.make_async_copy(handed, states.at[r - 1], state_sem).wait()
+                line.home_each(r - 1, False)
 
                 @when(first)
                 def _():
                     moves.hand(r - 1).wait_send()
 
             handed[...] = (kept[r % 4].astype(f32) + value + out_bias[...]).astype(bf16)
-            pltpu.make_async_copy(handed, states.at[r], state_sem).start()
 
             @when(first)
             def _():
                 moves.hand(r).start()
 
+            line.home_each(r, True)
+
         @when(valid(c))
         def _():
-            @when(c == 0)
-            def _():
-                weights[2].wait()
-                weights[3].wait()
-
             @when(c >= 1)
             def _():
                 moves.give_theirs(c - 1).wait_send()
 
-            for j in range(chips):
-                theirs[j] = branch_rows(2 * j + 1 - moves.core).astype(bf16)
+            branch_rows(1 - moves.core, theirs)
             moves.give_theirs(c).start()
-            for j in range(chips):
-                mine[j] = branch_rows(2 * j + moves.core)
+            branch_rows(moves.core, mine)
 
         @when(valid(g))
         def _():
@@ -426,7 +578,9 @@
     drain(moves, tasks - 1)
     for k in range(5):
         store(k, tasks - 1).wait()
-    pltpu.make_async_copy(handed, states.at[tasks - 1], state_sem).wait()
+    line.home_each(tasks - 1, False)
+    line.home_wait(tasks)
+    line.bring_done(tasks // 2)
 
     @when(first)
     def _():
@@ -449,8 +603,10 @@
     ]
 
 
-def forward_pass(xin, wq, wi, wo, wd, bq, bi, out_bias, tables, pq, pk, chips, heads):
-    tasks, rows, width = xin.shape
+def forward_pass(chosen, wq, wi, wo, wd, bq, bi, norms, out_bias, tables, pq, pk, chips, heads):
+    per_device, count, part_rows, width = chosen.shape
+    tasks, rows = 2 * per_device, count // 2 * part_rows
+    in_sems, home_sems = line_semaphores(tasks, count)
     block = pq.shape[0]
     units, inner = wd.shape[0], wo.shape[0]
     anywhere = pl.BlockSpec(memory_space=pl.ANY)
@@ -466,17 +622,20 @@
             shape((tasks, block, inner), bf16),
             shape((tasks, block, heads * LANES), f32),
             shape((tasks, rows, width), bf16),
+            shape((per_device * count, part_rows, width), bf16),
             shape((tasks, rows, width), bf16),
-            shape((tasks, chips, rows, width), bf16),
+            shape((tasks, chips * rows, width), bf16),
             shape((tasks, chips - 1, rows, width), bf16),
         ],
-        in_specs=[anywhere] * 5 + [vmem] * 8,
-        out_specs=[anywhere] * 10,
+        in_specs=[anywhere] * 5 + [vmem] * 9,
+        out_specs=[anywhere] * 11,
         scratch_shapes=[
             pltpu.VMEM(wq.shape, bf16),
             pltpu.VMEM(wi.shape, bf16),
             pltpu.VMEM(wo.shape, bf16),
             pltpu.VMEM(wd.shape, bf16),
+            pltpu.VMEM(bq.shape, f32),
+            pltpu.VMEM(bi.shape, f32),
             pltpu.VMEM((block, width), bf16),
             pltpu.VMEM((2, block, 3 * inner), bf16),
             pltpu.VMEM((block, units), bf16),
@@ -485,18 +644,19 @@
             pltpu.VMEM((block, heads * LANES), f32),
             pltpu.VMEM((4, rows, width), bf16),
             pltpu.VMEM((rows, width), bf16),
-            pltpu.VMEM((chips, rows, width), bf16),
-            pltpu.VMEM((chips, rows, width), f32),
-            pltpu.VMEM((chips, rows, width), bf16),
-            pltpu.VMEM((chips, rows, width), bf16),
+            pltpu.VMEM((chips * rows, width), bf16),
+            pltpu.VMEM((chips * rows, width), f32),
+            pltpu.VMEM((chips * rows, width), bf16),
+            pltpu.VMEM((chips * rows, width), bf16),
             pltpu.VMEM((chips - 1, rows, width), bf16),
             pltpu.VMEM((rows, width), bf16),
             pltpu.SemaphoreType.DMA((4,)),
             pltpu.SemaphoreType.DMA((3,)),
             pltpu.SemaphoreType.DMA((5,)),
             pltpu.SemaphoreType.DMA,
-            pltpu.SemaphoreType.DMA,
         ]
+        + in_sems
+        + home_sems
         + move_semaphores(tasks, chips),
         compiler_params=pltpu.CompilerParams(
             collective_id=3, has_side_effects=True, vmem_limit_bytes=PASS_VMEM
@@ -507,18 +667,20 @@
             transcendentals=0,
         ),
         name="forward_pass",
-    )(xin, wq, wi, wo, wd, bq, bi, out_bias, *tables, pq, pk)
+    )(chosen, wq, wi, wo, wd, bq, bi, norms, out_bias, *tables, pq, pk)
 
 
 def backward_kernel(
     plan, gin, xin, xarrive, qkv_all, dg_all, ctx_all, lse_all, std_all, wq_all, wi_all, wo_all, wd_all,
     gains, cosine, ahead, behind, pq, pk,
-    land, dproj_all, dh_all, dx_all, arrive, core_land, chip_land, vectors,
+    land, dproj_all, dh_all, home, arrive, core_land, chip_land, vectors, side_q, side_h,
     wq, wi, wo, wd, gy, dg, dh, qkv, before, ctx, lse, std, dctx, dproj, dk_held, dv_held,
     kept, xrows, own, theirs, mine, core_in, low, chip_in, handed,
-    weight_sem, load_sem, store_sem, keep_sem, state_sem, *sems,
+    weight_sem, load_sem, store_sem, keep_sem, put_home, got_home, kept_home, *sems,
 ):
     tasks, chips, rows, heads = plan
+    line = Line(home.shape[1])
+    line.set_home(handed, home, put_home, got_home, kept_home)
     size = wq.shape[1] // (3 * heads)
     scale = size**-0.5
 
@@ -538,8 +700,9 @@
     ]
     for copy in weights:
         copy.start()
-    vectors[...] = jnp.zeros_like(vectors)
-    moves.greet()
+    for total in (vectors, side_q, side_h):
+        total[...] = jnp.zeros_like(total)
+    moves.greet(line)
 
     def valid(task):
         return (task >= 0) & (task < tasks)
@@ -563,7 +726,9 @@
         dctx[...] = dot(gy[...], wo[...], NT).astype(bf16)
         for at in range(0, wd.shape[0], 256):
             part = slice(at, at + 256)
-            dh[:, part] = (dot(gy[...], wd[part, :], NT) * dg[:, part].astype(f32)).astype(bf16)
+            value = (dot(gy[...], wd[part, :], NT) * dg[:, part].astype(f32)).astype(bf16)
+            dh[:, part] = value
+            side_h[:, part] += jnp.sum(value.astype(f32), axis=0, keepdims=True)
 
     def attend_back(second):
         half = 1 if second else 0
@@ -595,18 +760,23 @@
             else:
                 dk = dk + dk_held[:, mid]
                 dv = dv + dv_held[:, mid]
-            dproj[:, at[0]] = turn(dq * scale, *table, -1.0).astype(bf16)
-            dproj[:, at[1]] = turn(dk * scale, *table, -1.0).astype(bf16)
-            dproj[:, at[2]] = dv.astype(bf16)
-
-    def merge_rows(member):
-        at = moves.part(member)
-        one = dot(dproj[at, :], wq[...], NT)
-        two = dot(dh[at, :], wi[...], NT)
-        standard = std[at, :].astype(f32)
-        for k, term in enumerate((one * standard, one, two * standard, two)):
-            vectors[k : k + 1, :] += jnp.sum(term, axis=0, keepdims=True)
-        return one * gains[0] + two * gains[1]
+            made = (turn(dq * scale, *table, -1.0), turn(dk * scale, *table, -1.0), dv)
+            for k in range(3):
+                value = made[k].astype(bf16)
+                dproj[:, at[k]] = value
+                side_q[:, at[k]] += jnp.sum(value.astype(f32), axis=0, keepdims=True)
+
+    def merge_rows(core, result):
+        at = moves.share(core)
+        for column in range(0, wq.shape[0], 512):
+            columns = slice(column, column + 512)
+            one = dot(dproj[at, :], wq[columns, :], NT)
+            two = dot(dh[at, :], wi[columns, :], NT)
+            standard = std[at, columns].astype(f32)
+            vectors[0:1, columns] += jnp.sum(one * standard, axis=0, keepdims=True)
+            vectors[2:3, columns] += jnp.sum(two * standard, axis=0, keepdims=True)
+            value = one * gains[0, :, columns] + two * gains[1, :, columns]
+            result[:, columns] = value.astype(result.dtype)
 
     @pl.loop(0, tasks + LAG + 2)
     def _(step):
@@ -700,7 +870,7 @@
 
             @when(r >= 1)
             def _():
-                pltpu.make_async_copy(handed, dx_all.at[place(r - 1)], state_sem).wait()
+                line.home_each(place(r - 1), False)
 
                 @when(source)
                 def _():
@@ -713,11 +883,12 @@
                 - standard * jnp.mean(e * standard, axis=-1, keepdims=True)
             )
             handed[...] = d_input.astype(bf16)
-            pltpu.make_async_copy(handed, dx_all.at[place(r)], state_sem).start()
 
             @when(source)
             def _():
                 moves.hand(r).start()
+
+            line.home_each(place(r), True)
 
         @when(valid(c))
         def _():
@@ -730,11 +901,9 @@
             def _():
                 moves.give_theirs(c - 1).wait_send()
 
-            for j in range(chips):
-                theirs[j] = merge_rows(2 * j + 1 - moves.core).astype(bf16)
+            merge_rows(1 - moves.core, theirs)
             moves.give_theirs(c).start()
-            for j in range(chips):
-                mine[j] = merge_rows(2 * j + moves.core)
+            merge_rows(moves.core, mine)
 
         @when(valid(g))
         def _():
@@ -743,7 +912,14 @@
     drain(moves, tasks - 1)
     for k in range(2):
         store(k, tasks - 1).wait()
-    pltpu.make_async_copy(handed, dx_all.at[place(tasks - 1)], state_sem).wait()
+    for k, (side, weight) in enumerate(((side_q, wq), (side_h, wi))):
+        value = side[...]
+        high = value.astype(bf16)
+        rest = (value - high.astype(f32)).astype(bf16)
+        pair = jnp.concatenate([high, rest, jnp.zeros((14, value.shape[1]), bf16)])
+        vectors[2 * k + 1 : 2 * k + 2, :] = jnp.sum(dot(pair, weight[...], NT), axis=0, keepdims=True)
+    line.home_each(place(tasks - 1), False)
+    line.home_wait(tasks)
 
     @when(source)
     def _():
@@ -752,6 +928,8 @@
 
 def backward_pass(gin, xin, xarrive, qkv, dg, ctx, lse, std, wq, wi, wo, wd, gains, tables, pq, pk, chips, heads):
     tasks, rows, width = xin.shape
+    count = lax.axis_size("ctx")
+    home_sems = line_semaphores(tasks, count)[1]
     block = pq.shape[0]
     units, inner = wd.shape[0], wo.shape[0]
     anywhere = pl.BlockSpec(memory_space=pl.ANY)
@@ -763,14 +941,16 @@
             shape((tasks, block, width), bf16),
             shape((tasks, block, 3 * inner), bf16),
             shape((tasks, block, units), bf16),
+            shape((tasks // 2 * count, 2 * rows // count, width), bf16),
             shape((tasks, rows, width), bf16),
-            shape((tasks, rows, width), bf16),
-            shape((tasks, chips, rows, width), bf16),
+            shape((tasks, chips * rows, width), bf16),
             shape((tasks, chips - 1, rows, width), bf16),
             shape((8, width), f32),
+            shape((1, 3 * inner), f32),
+            shape((1, units), f32),
         ],
         in_specs=[anywhere] * 12 + [vmem] * 6,
-        out_specs=[anywhere] * 7 + [vmem],
+        out_specs=[anywhere] * 7 + [vmem] * 3,
         scratch_shapes=[
             pltpu.VMEM(wq.shape, bf16),
             pltpu.VMEM(wi.shape, bf16),
@@ -791,18 +971,18 @@
             pltpu.VMEM((4, rows, width), bf16),
             pltpu.VMEM((rows, width), bf16),
             pltpu.VMEM((rows, width), bf16),
-            pltpu.VMEM((chips, rows, width), bf16),
-            pltpu.VMEM((chips, rows, width), f32),
-            pltpu.VMEM((chips, rows, width), bf16),
-            pltpu.VMEM((chips, rows, width), bf16),
+            pltpu.VMEM((chips * rows, width), bf16),
+            pltpu.VMEM((chips * rows, width), f32),
+            pltpu.VMEM((chips * rows, width), bf16),
+            pltpu.VMEM((chips * rows, width), bf16),
             pltpu.VMEM((chips - 1, rows, width), bf16),
             pltpu.VMEM((rows, width), bf16),
             pltpu.SemaphoreType.DMA((4,)),
             pltpu.SemaphoreType.DMA((10,)),
             pltpu.SemaphoreType.DMA((2,)),
             pltpu.SemaphoreType.DMA,
-            pltpu.SemaphoreType.DMA,
         ]
+        + home_sems
         + move_semaphores(tasks, chips),
         compiler_params=pltpu.CompilerParams(
             collective_id=5, has_side_effects=True, vmem_limit_bytes=PASS_VMEM
@@ -817,7 +997,7 @@
 
 
 CHUNK = 256
-PIECE = 64
+PIECE = 32
 SKEW = 2
 
 
@@ -828,7 +1008,7 @@
     small_sent, small_got,
 ):
     bounds, tasks, count, piece, skew, ring = plan
-    sources = (act, ctx, dproj, dhid)
+    sources = (dproj, dhid, act, ctx)
     total_chunks = bounds[-1]
     per_chunk = CHUNK // piece
     pieces = total_chunks * per_chunk
@@ -861,7 +1041,7 @@
         )
 
     def rhs_copy(k):
-        return pltpu.make_async_copy((gy, std)[k].at[pl.ds(0, tasks)], rhs.at[k], rhs_sem.at[k])
+        return pltpu.make_async_copy((std, gy)[k].at[pl.ds(0, tasks)], rhs.at[k], rhs_sem.at[k])
 
     def each_source(chunk, act_on):
         for g, source in enumerate(sources):
@@ -885,7 +1065,7 @@
 
     def multiply(chunk, part):
         second = jnp.where(chunk >= bounds[2], 1, 0)
-        group = second + jnp.where(chunk >= bounds[3], 1, 0)
+        group = second + jnp.where(chunk >= bounds[1], 1, 0)
         columns = pl.ds(pl.multiple_of(part * tile, tile), tile)
         value = dot(lhs[:, :block], rhs[second, 0, :, columns])
         for k in range(1, tasks):
@@ -1085,7 +1265,7 @@
     count = lax.axis_size("ctx")
     block, width = gy.shape[1:]
     bounds = [0]
-    for source in (act, ctx, dproj, dhid):
+    for source in (dproj, dhid, act, ctx):
         bounds.append(bounds[-1] + source.shape[2] // CHUNK)
     total = bounds[-1] * CHUNK
     pieces = total // PIECE
@@ -1134,15 +1314,40 @@
     return out, small_out
 
 
-def exchange(blocks, axis):
-    count = blocks.shape[0]
-    me = lax.axis_index(axis)
-    got = [lax.dynamic_index_in_dim(blocks, me, 0, keepdims=False)]
-    for shift in range(1, count):
-        piece = lax.dynamic_index_in_dim(blocks, (me + shift) % count, 0, keepdims=False)
-        got.append(lax.ppermute(piece, axis, [(k, (k + shift) % count) for k in range(count)]))
-    ring = jnp.stack(got[::-1] + got[::-1])
-    return lax.dynamic_slice_in_dim(ring, (count - 1 - me) % count, count, 0)
+def turned_kernel(part, out):
+    out[...] = part[...].astype(f32).T
+
+
+def turned(total, start, count):
+    width = total.shape[1]
+    return pl.pallas_call(
+        turned_kernel,
+        out_shape=jax.ShapeDtypeStruct((width, count), f32),
+        grid=(count // CHUNK,),
+        in_specs=[pl.BlockSpec((CHUNK, width), lambda i: (start // CHUNK + i, 0))],
+        out_specs=pl.BlockSpec((width, CHUNK), lambda i: (0, i)),
+        compiler_params=pltpu.CompilerParams(vmem_limit_bytes=32 * 1024 * 1024),
+        name="turned",
+    )(total)
+
+
+def turned_heads_kernel(heads, part, out):
+    size = part.shape[0] // heads
+    for h in range(heads):
+        out[:, h, :] = part[h * size : (h + 1) * size, :].astype(f32).T
+
+
+def turned_heads(total, start, count, heads):
+    width = total.shape[1]
+    return pl.pallas_call(
+        partial(turned_heads_kernel, heads),
+        out_shape=jax.ShapeDtypeStruct((width, heads, count // heads), f32),
+        grid=(width // CHUNK,),
+        in_specs=[pl.BlockSpec((count, CHUNK), lambda i: (start // count, i))],
+        out_specs=pl.BlockSpec((CHUNK, heads, count // heads), lambda i: (i, 0, 0)),
+        compiler_params=pltpu.CompilerParams(vmem_limit_bytes=32 * 1024 * 1024),
+        name="turned_heads",
+    )(total)
 
 
 def body(
@@ -1169,41 +1374,33 @@
     first = lax.axis_index("section") == 0
     per_device = micro * seqs // ctx_count
     blocks = ctx_count // 2
-    own_rows = blocks * rows
     tasks = 2 * per_device
 
     chosen = jnp.where(first, inputs[:, 0], out_grads[:, 0])
     chosen = chosen.transpose(0, 2, 1, 3).reshape(per_device, ctx_count, rows, width)
-    own_chosen = []
-    for j in range(per_device):
-        moved = exchange(chosen[j], "ctx").reshape(2, own_rows, width)
-        own_chosen += [moved[0], moved[1]]
 
     wq = w_qkv[0].reshape(width, heads * head_cols)
     wi = input_projection[0]
     wo = w_out[0].reshape(-1, width)
     wd = down_projection[0]
     gain_one, bias_one, gain_two, bias_two = norm1_gain[0], norm1_bias[0], norm2_gain[0], norm2_bias[0]
-    wq_scaled = (wq.astype(f32) * gain_one[:, None]).astype(bf16)
-    wi_scaled = (wi.astype(f32) * gain_two[:, None]).astype(bf16)
-    bq = b_qkv[0].reshape(1, -1) + jnp.sum(wq.astype(f32) * bias_one[:, None], axis=0, keepdims=True)
-    bi = input_bias_vector + jnp.sum(wi.astype(f32) * bias_two[:, None], axis=0, keepdims=True)
+    norms = jnp.stack([gain_one, bias_one, gain_two, bias_two], axis=1)
     out_bias = (b_out[0] + b_down[0])[None]
 
     relative, tables = position_tables(None, blocks, rows, tensor)
     places_q, places_k = relative[:, None], relative[None, :]
 
     chips = tensor // 2
-    chosen_rows = jnp.stack(own_chosen)
     stacked_tables = [jnp.stack(pair) for pair in zip(*tables)]
-    std_all, qkv, act_all, dg_all, ctx_all, lse_all, states, arrive, _, _ = forward_pass(
-        chosen_rows,
-        wq_scaled,
-        wi_scaled,
+    std_all, qkv, act_all, dg_all, ctx_all, lse_all, chosen_rows, states, arrive, _, _ = forward_pass(
+        chosen,
+        wq,
+        wi,
         wo,
         wd,
-        bq,
-        bi,
+        b_qkv[0].reshape(1, -1),
+        input_bias_vector,
+        norms,
         out_bias,
         stacked_tables,
         places_q,
@@ -1212,7 +1409,7 @@
         heads,
     )
     gains = jnp.stack([gain_one, gain_two])[:, None]
-    gy_all, dproj_all, dh_all, dx_all, _, _, _, vectors = backward_pass(
+    gy_all, dproj_all, dh_all, dx_home, _, _, _, vectors, side_q, side_h = backward_pass(
         chosen_rows,
         chosen_rows,
         arrive,
@@ -1234,12 +1431,11 @@
     )
     vectors = vectors[:5]
 
-    d_b_qkv = jnp.sum(dproj_all[:tasks], axis=(0, 1), dtype=f32)
-    d_b_in = jnp.sum(dh_all[:tasks], axis=(0, 1), dtype=f32)
+    d_b_qkv, d_b_in = side_q[0], side_h[0]
     units, inner = wd.shape[0], wo.shape[0]
-    sums = jnp.concatenate([jnp.zeros((units + inner,), f32), d_b_qkv, d_b_in])[:, None]
-    gains = jnp.stack([jnp.ones_like(gain_one), gain_one, gain_two])[:, None]
-    biases = jnp.stack([jnp.zeros_like(bias_one), bias_one, bias_two])[:, None]
+    sums = jnp.concatenate([d_b_qkv, d_b_in, jnp.zeros((units + inner,), f32)])[:, None]
+    gains = jnp.stack([gain_one, gain_two, jnp.ones_like(gain_one)])[:, None]
+    biases = jnp.stack([bias_one, bias_two, jnp.zeros_like(bias_one)])[:, None]
     mask = 1
     while mask < tensor:
         vectors = vectors + lax.ppermute(vectors, "tensor", [(k, k ^ mask) for k in range(tensor)])
@@ -1254,24 +1450,21 @@
     summed, small = reduce_gradients(
         act_all, ctx_all, dproj_all, dh_all, gy_all, std_all, gains, biases, sums, small, tasks
     )
+    columns = wq.shape[1]
     vectors = small[:5]
     sides = small[5 : 5 + side_rows].reshape(-1)
     d_b_qkv, d_b_in = sides[: d_b_qkv.shape[0]], sides[d_b_qkv.shape[0] : sides.shape[0]]
     d_b_in = d_b_in[: wi.shape[1]]
-    d_w_down = summed[:units].astype(f32)
-    d_w_out = summed[units : units + inner].astype(f32)
-    summed = summed[units + inner :]
-    d_w_qkv = summed[: wq.shape[1]].T.astype(f32)
-    d_w_in = summed[wq.shape[1] :].T.astype(f32)
-
-    def homeward(rows_of_tasks):
-        stacked = rows_of_tasks.reshape(per_device, ctx_count, rows, width)
-        moved = exchange(stacked.transpose(1, 0, 2, 3), "ctx")
-        moved = moved.transpose(1, 0, 2, 3).reshape(micro, seqs, rows, width)
-        return moved.transpose(0, 2, 1, 3)[None, :, None]
+    d_w_qkv = turned_heads(summed, 0, columns, heads)
+    d_w_in = turned(summed, columns, units)
+    d_w_down = summed[columns + units : columns + 2 * units].astype(f32)
+    d_w_out = summed[columns + 2 * units :].astype(f32)
+
+    def homeward(pieces):
+        return pieces.reshape(micro, seqs, rows, width).transpose(0, 2, 1, 3)[None, :, None]
 
     states = homeward(states)
-    input_grads = homeward(dx_all).astype(f32)
+    input_grads = homeward(dx_home).astype(f32)
     return (
         states,
         input_grads,

time: 1760 us -> 1390 us (0.79)
  Pallas kernels: 1460 us -> 1300 us
  local copies, waits for them, and re-layouts: 111 us -> 39.6 us
  waiting for transfers between devices: 56.6 us -> 0.01 us
  other arithmetic: 91.1 us -> 34.7 us
  starting transfers between devices: 30.2 us -> 0.34 us
    pallas_call x1, Pallas kernels: 713 us -> 584 us  [reduce_gradients(): pl.pallas_call(partial(reduce_kernel, plan), out_shape=[result, jax.Shape...]
    unnamed x100 -> x25, local copies, waits for them, and re-layouts: 86.6 us -> 10.3 us
    pallas_call x1, Pallas kernels: 495 us -> 429 us  [backward_pass(): pl.pallas_call(partial(backward_kernel, (tasks, chips, rows, heads)), out...]
    ppermute x18 -> x0, waiting for transfers between devices: 56.6 us -> none  [exchange(): lax.ppermute(piece, axis, [(k, (k + shift) % count) for k in range(count)])]
    reduce_sum x4 -> x0, other arithmetic: 31.3 us -> none  [the longest x1 8.72 us: body(): jnp.sum(wq.astype(f32) * bias_one[:, None], axis=0, keepdims=True)]
    ppermute x18 -> x0, starting transfers between devices: 29 us -> none  [exchange(): lax.ppermute(piece, axis, [(k, (k + shift) % count) for k in range(count)])]
    pallas_call x0 -> x2, Pallas kernels: none -> 21.4 us  [the longest x1 11.1 us: turned(): pl.pallas_call(turned_kernel, out_shape=jax.ShapeDtypeStruct((width, coun...]
    pallas_call x1, Pallas kernels: 247 us -> 267 us  [forward_pass(): pl.pallas_call(partial(forward_kernel, (tasks, chips, rows, heads)), out_...]
  transfers between devices with their start and end apart: 20 -> 2, of which waited for: 4 -> 0; matrix products, arithmetic and copies ran while one was open for 7% -> 2% of each run, Pallas kernels for 41% -> 0%
where the time goes in v4:
time: 1390 us; the launch traced here: 1380 us
  Pallas kernels  1300 us (94%)
  local copies, waits for them, and re-layouts  39.6 us (3%)
  other arithmetic  34.7 us (2%)
    pallas_call x1, Pallas kernels, reduce_gradients(): pl.pallas_call(partial(reduce_kernel, plan), out_shape=[result, jax.Shape...  584 us
    pallas_call x1, Pallas kernels, backward_pass(): pl.pallas_call(partial(backward_kernel, (tasks, chips, rows, heads)), out...  429 us
    pallas_call x1, Pallas kernels, forward_pass(): pl.pallas_call(partial(forward_kernel, (tasks, chips, rows, heads)), out_...  267 us
  transfers between devices with their start and end apart: 2, of which 0 were waited for; matrix products, arithmetic and copies ran while one was open for 2% of the time, Pallas kernels for 0%

profile of v4, /device:TPU:0, one launch (start us, length us, event | category | flops | bytes accessed | tf_op | source)
XLA Modules:
  0.0 1377.1 jit_solution(4959682598005282230)
XLA Ops:
  0.7 0.1 iota_add_fusion
  0.8 0.7 add.213.pk
  1.4 0.9 add.217.pq
  2.3 0.1 pad.46.clone
  2.4 0.1 pad.38.clone
  2.5 1.3 copy.52
  3.8 0.1 reshape.268
  3.9 0.1 reshape.261
  3.9 0.7 pad_maximum_fusion.9
  4.7 0.6 broadcast_in_dim.142.gains
  5.3 0.8 pad_maximum_fusion.7
  6.1 1.3 copy.45.norms
  7.4 6.9 copy.51
  14.3 0.0 copy-done.8
  14.3 0.0 copy-done.9
  14.3 0.6 add.205.out_bias
  14.9 1.9 multiply_sine_fusion.1
  16.8 0.3 fusion.2
  17.1 0.8 pad_maximum_fusion.2.behind
  18.0 0.2 maximum_bitcast_fusion
  18.2 0.8 pad_maximum_fusion.cosine
  19.0 0.8 pad_maximum_fusion.1.ahead
  19.8 0.0 copy-done
  19.8 0.0 copy-done.1
  19.8 10.2 fusion.chosen
  30.1 266.8 %forward_pass.1 = (bf16[8,512,2048]{2,1,0:T(8,128)(2,1)}, bf16[8,512,1536]{2,1,0:T(8,128)(2,1)}, bf16[8,512,2048]{2,1,0:T(8,128)(2,1)}, bf16[8,512,2048]{2,1,0:T...) custom-call(bf16[4,4,64,2048]{3,2,1,0:T(8,128)(2,1)} %fusion.chosen,, ...), custom_call_target="tpu_custom_call" | custom-call | flops 103079215104 | bytes 134217728 | tf_op jit(solution)/shard_map/forward_pass/pallas_call | solution.py:615
  296.9 0.0 copy-start.6
  296.9 0.0 copy-start.7
  296.9 0.0 copy-start.2
  296.9 0.0 copy-start.3
  296.9 429.3 %backward_pass.1 = (bf16[8,512,2048]{2,1,0:T(8,128)(2,1)}, bf16[8,512,1536]{2,1,0:T(8,128)(2,1)}, bf16[8,512,2048]{2,1,0:T(8,128)(2,1)}, bf16[16,64,2048]{2,1,0:...) custom-call(bf16[8,128,2048]{2,1,0:T(8,128)(2,1)} %get-tuple-element, ...), custom_call_target="tpu_custom_call" | custom-call | flops 103079215104 | bytes 167772160 | tf_op jit(solution)/shard_map/backward_pass/pallas_call | solution.py:938
  726.3 0.1 collective-permute-start
  726.3 0.1 pad.20.clone
  726.4 0.1 pad.17.clone
  726.5 0.0 copy-done.6
  726.5 0.0 copy-done.7
  726.5 0.1 maximum_maximum_fusion.1
  726.6 0.1 maximum_maximum_fusion
  726.6 0.7 reduce.4
  727.4 0.7 pad_maximum_fusion.8
  728.1 0.0 collective-permute-done
  728.1 0.8 slice_add_fusion
  728.9 0.3 collective-permute-start.1
  729.2 0.7 select_maximum_fusion
  729.9 0.6 broadcast_in_dim.144.biases
  730.5 0.6 broadcast_in_dim.143.gains
  731.2 7.5 copy.61
  738.6 2.2 copy.50.sums
  740.8 9.5 copy.60
  750.3 0.0 collective-permute-done.1
  750.3 0.3 scatter.9.small
  750.7 0.0 copy-start.4
  750.7 0.6 copy-done.4
  751.3 583.8 %reduce_gradients.1 = (bf16[6144,2048]{1,0:T(8,128)(2,1)}, f32[8,2048]{1,0:T(8,128)}, bf16[6144,2048]{1,0:T(8,128)(2,1)}, bf16[6144,2048]{1,0:T(8,128)(2,1)}) custom-call(bf16[8,512,2048]{2,1,0:T(8,128)(2,1)} %get-tuple-element.65.act, bf16[8,512,512]{2,1,0:T(8,128)(2,1)} %get-tuple-element.61.ctx_all.ctx, bf16[8,512,1536]{2,1,0:T(8,128)(2,1)} %get-tuple-element.66.dproj, ...), custom_call_target="tpu_custom_call" | custom-call | flops 103079215104 | bytes 100663296 | tf_op jit(solution)/shard_map/reduce_gradients/pallas_call | solution.py:1277
  1335.1 0.8 slice_bitcast_fusion
  1335.9 1.7 fusion.12
  1337.6 0.6 slice.87
  1338.2 1.7 slice.82
  1339.9 10.3 turned_heads.1
  1350.2 11.7 bitcast_convert_fusion
  1361.9 11.1 turned.1
  1373.0 0.6 reshape.258
  1373.6 2.5 convert.6
  1376.1 0.6 copy.64
  (19 shorter events, 0.1 us)
Async XLA Ops:
  7.4 6.9 copy-start.8
  7.4 6.9 copy-start.9
  14.3 5.5 copy-start
  14.3 5.5 copy-start.1
  296.9 429.6 %copy-start.6 = (f32[1,2048]{1,0:T(1,128)S(1)}, f32[1,2048]{1,0:T(1,128)}, u32[]{:S(2)}) copy-start(f32[1,2048]{1,0:T(1,128)} %param.23) | copy-start | bytes 24580
  296.9 429.6 %copy-start.7 = (f32[1,2048]{1,0:T(1,128)S(1)}, f32[1,2048]{1,0:T(1,128)}, u32[]{:S(2)}) copy-start(f32[1,2048]{1,0:T(1,128)} %param.21) | copy-start | bytes 24580
  296.9 429.7 %copy-start.2 = (f32[1,2048]{1,0:T(1,128)S(1)}, f32[1,2048]{1,0:T(1,128)}, u32[]{:S(2)}) copy-start(f32[1,2048]{1,0:T(1,128)} %param.22) | copy-start | bytes 24580
  296.9 429.6 %copy-start.3 = (f32[1,2048]{1,0:T(1,128)S(1)}, f32[1,2048]{1,0:T(1,128)}, u32[]{:S(2)}) copy-start(f32[1,2048]{1,0:T(1,128)} %param.20) | copy-start | bytes 24580
  726.3 1.8 collective-permute-start
  728.9 21.4 %collective-permute-start.1 = (f32[5,2048]{1,0:T(8,128)S(1)}, f32[5,2048]{1,0:T(8,128)S(1)}, u32[]{:S(2)}, u32[]{:S(2)}) collective-permute-start(f32[5,2048]{1,0:T(8,128)S(1)} %slice_add_fusion), channel_id=1, source_target_pairs={{0,8},{4,12},{8,0},{12,4},{1,9},{5,13},{9,1},{13,5},{2,10},{6,14},... | collective-permute-start | bytes 122888 | tf_op jit(solution)/shard_map/ppermute | solution.py:1441
  750.7 0.6 copy-start.4
  1337.6 38.5 %copy-start.5 = (f32[1,2048]{1,0:T(1,128)}, f32[1,2048]{1,0:T(1,128)S(1)}, u32[]{:S(2)}) copy-start(f32[1,2048]{1,0:T(1,128)S(1)} %get-tuple-element.126) | copy-start | bytes 24580

commit v5 on v4

--- a/solution.py
+++ b/solution.py
@@ -64,11 +64,11 @@
 
 
 class Moves:
-    def __init__(self, plan, place, land, arrive, core_land, chip_land, own, theirs, low, handed, sems):
+    def __init__(self, plan, land, arrive, core_land, chip_land, theirs, low, handed, sems):
         self.tasks, self.chips, self.rows = plan
-        self.place = place
         self.land, self.arrive, self.core_land, self.chip_land = land, arrive, core_land, chip_land
-        self.own, self.theirs, self.low, self.handed = own, theirs, low, handed
+        self.theirs, self.low, self.handed = theirs, low, handed
+        self.slots = land.shape[0]
         (
             self.got_chip, self.got_core, self.got_theirs, self.got_low, self.got_hand,
             self.put_chip, self.put_core, self.put_theirs, self.put_low, self.put_hand,
@@ -113,10 +113,10 @@
         pl.semaphore_wait(barrier, len(peers))
 
     def gather_chip(self, task, shift, member=None):
-        member = self.index if member is None else member
+        rows = self.land.at[task % self.slots, self.part(self.index if member is None else member)]
         return self.remote(
-            self.own,
-            self.land.at[self.place(task), self.part(member)],
+            rows,
+            rows,
             self.put_chip.at[shift - 1],
             self.got_chip.at[task, shift - 1],
             tensor=self.mate_on(shift),
@@ -128,10 +128,10 @@
     def gather_core(self, task, shift, member=None):
         if member is None:
             member = lax.rem(self.index + self.total - 2 * shift, self.total)
-        target = self.land.at[self.place(task), self.part(member)]
+        rows = self.land.at[task % self.slots, self.part(member)]
         return self.remote(
-            self.own if shift == 0 else target,
-            target,
+            rows,
+            rows,
             self.put_core.at[shift],
             self.got_core.at[task, shift],
             tensor=self.mate,
@@ -142,13 +142,13 @@
 
     def give_theirs(self, task):
         return self.remote(
-            self.theirs, self.core_land.at[task], self.put_theirs, self.got_theirs.at[task], tensor=self.mate
+            self.theirs, self.core_land.at[task % 2], self.put_theirs, self.got_theirs.at[task], tensor=self.mate
         )
 
     def give_low(self, task, shift):
         return self.remote(
             self.low.at[self.of_chip(lax.rem(self.chip + shift, self.chips))],
-            self.chip_land.at[task, shift - 1],
+            self.chip_land.at[task % 2, shift - 1],
             self.put_low.at[shift - 1],
             self.got_low.at[task, shift - 1],
             tensor=self.mate_on(shift),
@@ -156,7 +156,11 @@
 
     def hand(self, task):
         return self.remote(
-            self.handed, self.arrive.at[task], self.put_hand, self.got_hand.at[task], section=1 - self.section
+            self.handed.at[task % 2],
+            self.arrive.at[task],
+            self.put_hand.at[task % 2],
+            self.got_hand.at[task],
+            section=1 - self.section,
         )
 
 
@@ -228,92 +232,154 @@
             for shift in range(1, self.count):
                 self.bring(j, shift).wait_send()
 
-    def set_home(self, handed, home, put, got, kept):
-        self.handed, self.home, self.put_home, self.got_home, self.kept_home = handed, home, put, got, kept
-
-    def take_home(self, task, k, source=None):
-        j, half = task // 2, task % 2
-        source = self.z if source is None else source
-        return self.remote(
-            self.handed.at[pl.ds(k * self.rows, self.rows)],
-            self.home.at[j * self.count + source],
-            self.put_home.at[k],
-            self.got_home.at[j, source],
-            half * self.blocks + k,
-        )
-
-    def keep_home(self, task, k):
+
+class Home:
+    def __init__(self, line, source, home, put, got, kept):
+        self.line, self.source, self.home = line, source, home
+        self.put, self.got, self.kept = put, got, kept
+
+    def take(self, task, k, sender=None):
+        line = self.line
+        sender = line.z if sender is None else sender
+        return line.remote(
+            self.source(task).at[pl.ds(k * line.rows, line.rows)],
+            self.home.at[(task // 2) * line.count + sender],
+            self.put.at[task, k],
+            self.got.at[task // 2, sender],
+            (task % 2) * line.blocks + k,
+        )
+
+    def keep(self, task, k):
+        line = self.line
         return pltpu.make_async_copy(
-            self.handed.at[pl.ds(k * self.rows, self.rows)],
-            self.home.at[(task // 2) * self.count + self.z],
-            self.kept_home,
-        )
-
-    def home_each(self, task, begin):
-        half = task % 2
-        for k in range(self.blocks):
-            there = half * self.blocks + k
-
-            @pl.when(there != self.z)
-            def _():
-                copy = self.take_home(task, k)
+            self.source(task).at[pl.ds(k * line.rows, line.rows)],
+            self.home.at[(task // 2) * line.count + line.z],
+            self.kept.at[task],
+        )
+
+    def each(self, task, begin):
+        line = self.line
+        for k in range(line.blocks):
+            there = (task % 2) * line.blocks + k
+
+            @pl.when(there != line.z)
+            def _():
+                copy = self.take(task, k)
                 copy.start() if begin else copy.wait_send()
 
-            @pl.when(there == self.z)
-            def _():
-                copy = self.keep_home(task, k)
+            @pl.when(there == line.z)
+            def _():
+                copy = self.keep(task, k)
                 copy.start() if begin else copy.wait()
 
-    def home_wait(self, tasks):
+    def wait(self, tasks):
         for j in range(tasks // 2):
-            for other in self.others():
-                self.take_home(2 * j, 0, other).wait_recv()
+            for other in self.line.others():
+                self.take(2 * j, 0, other).wait_recv()
 
 
 def line_semaphores(tasks, count):
     dma = pltpu.SemaphoreType.DMA
     half = tasks // 2
     return [dma((half, count - 1)), dma((half, count)), dma((half,))], [
-        dma((count // 2,)),
+        dma((tasks, count // 2)),
         dma((half, count)),
-        dma,
+        dma((tasks,)),
     ]
 
 
-def reduce_first(moves, task, mine, core_in, load_sem):
+class Early:
+    def __init__(self, moves, source, gathered, got_chip, got_core, put_chip, put_core, kept):
+        self.moves, self.source, self.gathered = moves, source, gathered
+        self.got_chip, self.got_core, self.put_chip, self.put_core = got_chip, got_core, put_chip, put_core
+        self.kept = kept
+
+    def at(self, task, member):
+        return self.gathered.at[task, self.moves.part(member)]
+
+    def behind(self, start, shift):
+        return lax.rem(start + self.moves.total - 2 * shift, self.moves.total)
+
+    def chip(self, task, shift, member=None):
+        member = self.moves.index if member is None else member
+        return self.moves.remote(
+            self.source.at[task],
+            self.at(task, member),
+            self.put_chip.at[task, shift - 1],
+            self.got_chip.at[task, shift - 1],
+            tensor=self.moves.mate_on(shift),
+        )
+
+    def core(self, task, shift, member=None):
+        member = self.behind(self.moves.index, shift) if member is None else member
+        rows = self.at(task, member)
+        return self.moves.remote(
+            self.source.at[task] if shift == 0 else rows,
+            rows,
+            self.put_core.at[task, shift],
+            self.got_core.at[task, shift],
+            tensor=self.moves.mate,
+        )
+
+    def keep(self, task):
+        return pltpu.make_async_copy(
+            self.source.at[task], self.at(task, self.moves.index), self.kept.at[task]
+        )
+
+    def start(self, task):
+        for shift in range(1, self.moves.chips):
+            self.chip(task, shift).start()
+        self.core(task, 0).start()
+        self.keep(task).start()
+
+    def hand_on(self, task):
+        for shift in range(1, self.moves.chips):
+            self.chip(task, shift, self.behind(self.moves.index, shift)).wait_recv()
+            self.core(task, shift).start()
+
+    def finish(self, task):
+        self.keep(task).wait()
+        for shift in range(1, self.moves.chips):
+            self.chip(task, shift).wait_send()
+        for shift in range(self.moves.chips):
+            self.core(task, shift).wait_send()
+            self.core(task, shift, self.behind(self.moves.mate, shift)).wait_recv()
+
+
+def early_semaphores(tasks, chips):
+    dma = pltpu.SemaphoreType.DMA
+    return [dma((tasks, chips - 1)), dma((tasks, chips)), dma((tasks, chips - 1)), dma((tasks, chips)), dma((tasks,))]
+
+
+def opposite(task):
+    return task + 1 - 2 * (task % 2)
+
+
+def reduce_first(moves, task, mine):
     moves.give_theirs(task).wait_recv()
-    load = pltpu.make_async_copy(moves.core_land.at[task], core_in, load_sem)
-    load.start()
 
     @pl.when(task >= 1)
     def _():
         for shift in range(1, moves.chips):
             moves.give_low(task - 1, shift).wait_send()
 
-    load.wait()
-    value = mine[...] + core_in[...].astype(f32)
+    value = mine[...] + moves.core_land[task % 2].astype(f32)
     mine[...] = value
     moves.low[...] = value.astype(bf16)
     for shift in range(1, moves.chips):
         moves.give_low(task, shift).start()
 
 
-def reduce_second(moves, task, mine, chip_in, load_sem):
+def reduce_second(moves, task, mine):
+    value = mine[moves.of_chip(moves.chip), :]
     for shift in range(1, moves.chips):
         moves.give_low(task, shift).wait_recv()
-    load = pltpu.make_async_copy(moves.chip_land.at[task], chip_in, load_sem)
-    load.start()
-    load.wait()
-    value = mine[moves.of_chip(moves.chip), :]
-    for shift in range(1, moves.chips):
-        value = value + chip_in[shift - 1].astype(f32)
+        value = value + moves.chip_land[task % 2, shift - 1].astype(f32)
     return value
 
 
-def gather_start(moves, task, keep_sem):
-    pltpu.make_async_copy(
-        moves.own, moves.land.at[moves.place(task), moves.part(moves.index)], keep_sem
-    ).start()
+def gather_start(moves, task, value):
+    moves.land[task % moves.slots, moves.part(moves.index), :] = value
     for shift in range(1, moves.chips):
         moves.gather_chip(task, shift).start()
     moves.gather_core(task, 0).start()
@@ -322,20 +388,13 @@
 def gather_free(moves, task):
     for shift in range(1, moves.chips):
         moves.gather_chip(task, shift).wait_send()
-    moves.gather_core(task, 0).wait_send()
-
-
-def gather_pass(moves, task, keep_sem):
-    pltpu.make_async_copy(
-        moves.own, moves.land.at[moves.place(task), moves.part(moves.index)], keep_sem
-    ).wait()
+    for shift in range(moves.chips):
+        moves.gather_core(task, shift).wait_send()
+
+
+def gather_pass(moves, task):
     for shift in range(1, moves.chips):
         moves.gather_chip_in(task, shift).wait_recv()
-
-        @pl.when(task >= 1)
-        def _():
-            moves.gather_core(task - 1, shift).wait_send()
-
         moves.gather_core(task, shift).start()
 
 
@@ -345,9 +404,7 @@
 
 
 def drain(moves, task):
-    gather_free(moves, task)
     for shift in range(1, moves.chips):
-        moves.gather_core(task, shift).wait_send()
         moves.give_low(task, shift).wait_send()
     moves.give_theirs(task).wait_send()
 
@@ -358,21 +415,20 @@
 
 def forward_kernel(
     plan, chosen, wq_all, wi_all, wo_all, wd_all, bq_in, bi_in, norms, out_bias, cosine, ahead, behind, pq, pk,
-    land, qkv_all, act_all, dg_all, ctx_all, lse_all, xin, home, arrive, core_land, chip_land,
-    wq, wi, wo, wd, bq, bi, std, qkv, act, dg, ctx, lse, kept, own, theirs, mine, core_in, low, chip_in, handed,
-    weight_sem, load_sem, store_sem, keep_sem,
-    put_in, got_in, kept_in, put_home, got_home, kept_home, *sems,
+    std_all, qkv_all, act_all, dg_all, ctx_all, lse_all, xin, states, arrive, early_all,
+    wq, wi, wo, wd, bq, bi, land, qkv, act, dg, ctx, lse, kept, theirs, mine, core_land, low, chip_land, handed,
+    weight_sem, load_sem, store_sem, state_sem, put_in, got_in, kept_in,
+    early_a, early_b, early_c, early_d, early_e, *sems,
 ):
     tasks, chips, rows, heads = plan
     line = Line(chosen.shape[2])
     line.set_in(chosen, xin, put_in, got_in, kept_in)
-    line.set_home(handed, home, put_home, got_home, kept_home)
     size = wq.shape[1] // (3 * heads)
-    moves = Moves(
-        (tasks, chips, rows), lambda task: task, land, arrive, core_land, chip_land, own, theirs, low, handed, sems
-    )
+    moves = Moves((tasks, chips, rows), land, arrive, core_land, chip_land, theirs, low, handed, sems)
     first = moves.section == 0
     base = jnp.where(first, 0, LAG)
+    early = Early(moves, xin, early_all, early_a, early_b, early_c, early_d, early_e)
+    early_count = min(tasks, 2 * (LAG - 1))
 
     weights = [
         pltpu.make_async_copy(a, b, weight_sem.at[k])
@@ -383,8 +439,16 @@
     for copy in weights:
         copy.start()
 
+    @when(jnp.logical_not(first))
+    def _():
+        for j in range(1, tasks // 2):
+            line.bring_start(j)
+
     def valid(task):
         return (task >= 0) & (task < tasks)
+
+    def keep_state(task):
+        return pltpu.make_async_copy(handed.at[task % 2], states.at[task], state_sem.at[task % 2])
 
     def fold(weight, bias_in, bias, gain_column):
         bias[...] = bias_in[...]
@@ -401,8 +465,8 @@
 
     def store(k, task):
         return pltpu.make_async_copy(
-            (qkv.at[task % 2], act, dg, ctx, lse)[k],
-            (qkv_all, act_all, dg_all, ctx_all, lse_all)[k].at[task],
+            (qkv.at[task % 2], act, dg, ctx, lse, land.at[task % 3])[k],
+            (qkv_all, act_all, dg_all, ctx_all, lse_all, std_all)[k].at[task],
             store_sem.at[k],
         )
 
@@ -412,7 +476,7 @@
         for h in range(heads):
             for k in range(3):
                 columns = slice((3 * h + k) * size, (3 * h + k + 1) * size)
-                z = dot(std[...], wq[:, columns]) + bq[:, columns]
+                z = dot(land[task % 3], wq[:, columns]) + bq[:, columns]
                 if k < 2:
                     z = turn(z, *table, 1.0)
                 qkv[half, :, columns] = z.astype(bf16)
@@ -443,10 +507,10 @@
                 peak + jnp.log(total), (q.shape[0], LANES)
             )
 
-    def expand():
+    def expand(task):
         for at in range(0, wi.shape[1], 256):
             columns = slice(at, at + 256)
-            h = dot(std[...], wi[:, columns]) + bi[:, columns]
+            h = dot(land[task % 3], wi[:, columns]) + bi[:, columns]
             phi = 0.5 + 0.5 * lax.erf(h * (0.5**0.5))
             density = jnp.exp(h * h * -0.5) * 0.3989422804014327
             act[:, columns] = (h * phi).astype(bf16)
@@ -466,31 +530,55 @@
         r = g - 2
 
         def load_rows(task, held):
-            return pltpu.make_async_copy(held.at[task], kept.at[task % 4], load_sem.at[0])
-
-        @when((step % 2 == 0) & (step // 2 + 1 < tasks // 2))
+            return pltpu.make_async_copy(held.at[task], kept.at[task % 3], load_sem)
+
+        @when(first & (step % 2 == 0) & (step // 2 + 1 < tasks // 2))
         def _():
             line.bring_start(step // 2 + 1)
 
-        @when(valid(r))
-        def _():
-            reduce_first(moves, r, mine, core_in, load_sem.at[1])
+        @when(first & (step < tasks))
+        def _():
+            line.bring_wait(step)
+
+        for k in range(2):
+            late = 2 * (step - 1) + k
+
+            @when(jnp.logical_not(first) & (late >= 0) & (late < early_count))
+            def _(late=late):
+                early.hand_on(opposite(late))
+
+        for k in range(2):
+            fresh = 2 * step + k
+
+            @when(jnp.logical_not(first) & (fresh < early_count))
+            def _(fresh=fresh):
+                line.bring_wait(opposite(fresh))
+                early.start(opposite(fresh))
+
+        @when(valid(g) & first)
+        def _():
+            load_rows(g, xin).start()
 
         @when(valid(c))
         def _():
             gather_wait(moves, c)
-            load = pltpu.make_async_copy(land.at[c], std, load_sem.at[2])
-            load.start()
 
             @when(c >= 1)
             def _():
-                for k in range(5):
+                for k in range(6):
                     store(k, c - 1).wait()
 
-            load.wait()
+            store(5, c).start()
             project(c)
             store(0, c).start()
 
+        @when(valid(g) & jnp.logical_not(first))
+        def _():
+            moves.hand(g).wait_recv()
+            load_rows(g, arrive).start()
+
+        @when(valid(c))
+        def _():
             @when(c % 2 == 0)
             def _():
                 attend(c, False)
@@ -502,29 +590,15 @@
             store(3, c).start()
             store(4, c).start()
 
-        @when(step < tasks)
-        def _():
-            line.bring_wait(step)
-
         @when(valid(g))
         def _():
-            @when(first)
-            def _():
-                load_rows(g, xin).start()
-
-            @when(jnp.logical_not(first))
-            def _():
-                moves.hand(g).wait_recv()
-                load_rows(g, arrive).start()
-
             load_rows(g, xin).wait()
 
             @when(g >= 1)
             def _():
                 gather_free(moves, g - 1)
 
-            own[...] = standardize(kept[g % 4])[0].astype(bf16)
-            gather_start(moves, g, keep_sem)
+            gather_start(moves, g, standardize(kept[g % 3])[0].astype(bf16))
 
         @when(step == 0)
         def _():
@@ -537,29 +611,29 @@
 
         @when(valid(c))
         def _():
-            expand()
+            expand(c)
             store(1, c).start()
             store(2, c).start()
 
         @when(valid(r))
         def _():
-            value = reduce_second(moves, r, mine, chip_in, load_sem.at[1])
-
-            @when(r >= 1)
-            def _():
-                line.home_each(r - 1, False)
+            value = reduce_second(moves, r, mine)
+
+            @when(r >= 2)
+            def _():
+                keep_state(r - 2).wait()
 
                 @when(first)
                 def _():
-                    moves.hand(r - 1).wait_send()
-
-            handed[...] = (kept[r % 4].astype(f32) + value + out_bias[...]).astype(bf16)
+                    moves.hand(r - 2).wait_send()
+
+            handed[r % 2] = (kept[r % 3].astype(f32) + value + out_bias[...]).astype(bf16)
 
             @when(first)
             def _():
                 moves.hand(r).start()
 
-            line.home_each(r, True)
+            keep_state(r).start()
 
         @when(valid(c))
         def _():
@@ -569,22 +643,35 @@
 
             branch_rows(1 - moves.core, theirs)
             moves.give_theirs(c).start()
+
+        @when(valid(g))
+        def _():
+            gather_pass(moves, g)
+
+        @when(valid(c))
+        def _():
             branch_rows(moves.core, mine)
-
-        @when(valid(g))
-        def _():
-            gather_pass(moves, g, keep_sem)
-
+            reduce_first(moves, c, mine)
+
+    gather_free(moves, tasks - 1)
     drain(moves, tasks - 1)
-    for k in range(5):
+    for k in range(6):
         store(k, tasks - 1).wait()
-    line.home_each(tasks - 1, False)
-    line.home_wait(tasks)
+
+    @when(jnp.logical_not(first))
+    def _():
+        for task in range(early_count):
+            early.finish(opposite(task))
+        for task in range(early_count, tasks):
+            line.bring_wait(opposite(task))
+
     line.bring_done(tasks // 2)
-
-    @when(first)
-    def _():
-        moves.hand(tasks - 1).wait_send()
+    for task in range(tasks - 2, tasks):
+        keep_state(task).wait()
+
+        @when(first)
+        def _(task=task):
+            moves.hand(task).wait_send()
 
 
 def move_semaphores(tasks, chips):
@@ -599,14 +686,14 @@
         dma((chips,)),
         dma,
         dma((chips - 1,)),
-        dma,
+        dma((2,)),
     ]
 
 
 def forward_pass(chosen, wq, wi, wo, wd, bq, bi, norms, out_bias, tables, pq, pk, chips, heads):
     per_device, count, part_rows, width = chosen.shape
     tasks, rows = 2 * per_device, count // 2 * part_rows
-    in_sems, home_sems = line_semaphores(tasks, count)
+    in_sems = line_semaphores(tasks, count)[0]
     block = pq.shape[0]
     units, inner = wd.shape[0], wo.shape[0]
     anywhere = pl.BlockSpec(memory_space=pl.ANY)
@@ -622,13 +709,12 @@
             shape((tasks, block, inner), bf16),
             shape((tasks, block, heads * LANES), f32),
             shape((tasks, rows, width), bf16),
-            shape((per_device * count, part_rows, width), bf16),
             shape((tasks, rows, width), bf16),
-            shape((tasks, chips * rows, width), bf16),
-            shape((tasks, chips - 1, rows, width), bf16),
+            shape((tasks, rows, width), bf16),
+            shape((tasks, block, width), bf16),
         ],
         in_specs=[anywhere] * 5 + [vmem] * 9,
-        out_specs=[anywhere] * 11,
+        out_specs=[anywhere] * 10,
         scratch_shapes=[
             pltpu.VMEM(wq.shape, bf16),
             pltpu.VMEM(wi.shape, bf16),
@@ -636,27 +722,26 @@
             pltpu.VMEM(wd.shape, bf16),
             pltpu.VMEM(bq.shape, f32),
             pltpu.VMEM(bi.shape, f32),
-            pltpu.VMEM((block, width), bf16),
+            pltpu.VMEM((3, block, width), bf16),
             pltpu.VMEM((2, block, 3 * inner), bf16),
             pltpu.VMEM((block, units), bf16),
             pltpu.VMEM((block, units), bf16),
             pltpu.VMEM((block, inner), bf16),
             pltpu.VMEM((block, heads * LANES), f32),
-            pltpu.VMEM((4, rows, width), bf16),
-            pltpu.VMEM((rows, width), bf16),
+            pltpu.VMEM((3, rows, width), bf16),
             pltpu.VMEM((chips * rows, width), bf16),
             pltpu.VMEM((chips * rows, width), f32),
+            pltpu.VMEM((2, chips * rows, width), bf16),
             pltpu.VMEM((chips * rows, width), bf16),
-            pltpu.VMEM((chips * rows, width), bf16),
-            pltpu.VMEM((chips - 1, rows, width), bf16),
-            pltpu.VMEM((rows, width), bf16),
+            pltpu.VMEM((2, chips - 1, rows, width), bf16),
+            pltpu.VMEM((2, rows, width), bf16),
             pltpu.SemaphoreType.DMA((4,)),
-            pltpu.SemaphoreType.DMA((3,)),
-            pltpu.SemaphoreType.DMA((5,)),
             pltpu.SemaphoreType.DMA,
+            pltpu.SemaphoreType.DMA((6,)),
+            pltpu.SemaphoreType.DMA((2,)),
         ]
         + in_sems
-        + home_sems
+        + early_semaphores(tasks, chips)
         + move_semaphores(tasks, chips),
         compiler_params=pltpu.CompilerParams(
             collective_id=3, has_side_effects=True, vmem_limit_bytes=PASS_VMEM
@@ -671,28 +756,33 @@
 
 
 def backward_kernel(
-    plan, gin, xin, xarrive, qkv_all, dg_all, ctx_all, lse_all, std_all, wq_all, wi_all, wo_all, wd_all,
+    plan, gin, xin, xarrive, states, early_all, qkv_all, dg_all, ctx_all, lse_all, std_all, wq_all, wi_all, wo_all, wd_all,
     gains, cosine, ahead, behind, pq, pk,
-    land, dproj_all, dh_all, home, arrive, core_land, chip_land, vectors, side_q, side_h,
-    wq, wi, wo, wd, gy, dg, dh, qkv, before, ctx, lse, std, dctx, dproj, dk_held, dv_held,
-    kept, xrows, own, theirs, mine, core_in, low, chip_in, handed,
-    weight_sem, load_sem, store_sem, keep_sem, put_home, got_home, kept_home, *sems,
+    gy_all, dproj_all, dh_all, home, state_home, arrive, vectors, side_q, side_h,
+    wq, wi, wo, wd, land, dg, dh, qkv, before, ctx, lse, std, dctx, dproj, dk_held, dv_held,
+    kept, theirs, mine, core_land, low, chip_land, handed, xrows,
+    weight_sem, load_sem, store_sem,
+    put_home, got_home, kept_home, put_state, got_state, kept_state, *sems,
 ):
     tasks, chips, rows, heads = plan
     line = Line(home.shape[1])
-    line.set_home(handed, home, put_home, got_home, kept_home)
+    grads_home = Home(line, lambda task: handed.at[place(task) % 2], home, put_home, got_home, kept_home)
+    states_home = Home(line, lambda task: states.at[task], state_home, put_state, got_state, kept_state)
     size = wq.shape[1] // (3 * heads)
     scale = size**-0.5
 
-    def place(task):
-        return task + 1 - 2 * (task % 2)
-
-    moves = Moves(
-        (tasks, chips, rows), place, land, arrive, core_land, chip_land, own, theirs, low, handed, sems
-    )
+    place = opposite
+    moves = Moves((tasks, chips, rows), land, arrive, core_land, chip_land, theirs, low, handed, sems)
     first = moves.section == 0
     source = moves.section == 1
     base = jnp.where(source, 0, LAG)
+    early_count = min(tasks, 2 * (LAG - 1))
+
+    def gathers(task):
+        return first | (task >= early_count)
+
+    def load_early(task):
+        return pltpu.make_async_copy(early_all.at[place(task)], land.at[task % 3], load_sem.at[8])
 
     weights = [
         pltpu.make_async_copy(a, b, weight_sem.at[k])
@@ -709,24 +799,26 @@
 
     def store(k, task):
         return pltpu.make_async_copy(
-            (dproj, dh)[k], (dproj_all, dh_all)[k].at[place(task)], store_sem.at[k]
+            (dproj, dh, land.at[task % 3])[k],
+            (dproj_all, dh_all, gy_all)[k].at[place(task)],
+            store_sem.at[k],
         )
 
     def load(k, task):
         return pltpu.make_async_copy(
-            (land, dg_all, qkv_all, ctx_all, lse_all, std_all)[k].at[place(task)],
-            (gy, dg, qkv, ctx, lse, std)[k],
+            (dg_all, qkv_all, ctx_all, lse_all, std_all)[k].at[place(task)],
+            (dg, qkv, ctx, lse, std)[k],
             load_sem.at[k],
         )
 
     def load_before(task):
-        return pltpu.make_async_copy(qkv_all.at[place(task) - 1], before, load_sem.at[6])
-
-    def spread():
-        dctx[...] = dot(gy[...], wo[...], NT).astype(bf16)
+        return pltpu.make_async_copy(qkv_all.at[place(task) - 1], before, load_sem.at[5])
+
+    def spread(task):
+        dctx[...] = dot(land[task % 3], wo[...], NT).astype(bf16)
         for at in range(0, wd.shape[0], 256):
             part = slice(at, at + 256)
-            value = (dot(gy[...], wd[part, :], NT) * dg[:, part].astype(f32)).astype(bf16)
+            value = (dot(land[task % 3], wd[part, :], NT) * dg[:, part].astype(f32)).astype(bf16)
             dh[:, part] = value
             side_h[:, part] += jnp.sum(value.astype(f32), axis=0, keepdims=True)
 
@@ -785,10 +877,14 @@
         r = g - 2
 
         def load_rows(task, held, number):
-            return pltpu.make_async_copy(held.at[number], kept.at[task % 4], load_sem.at[7])
+            return pltpu.make_async_copy(held.at[number], kept.at[task % 3], load_sem.at[6])
 
         def load_x(task, held):
-            return pltpu.make_async_copy(held.at[place(task)], xrows, load_sem.at[8])
+            return pltpu.make_async_copy(held.at[place(task)], xrows, load_sem.at[7])
+
+        @when(step < tasks)
+        def _():
+            states_home.each(step, True)
 
         @when(valid(g) & source)
         def _():
@@ -804,17 +900,18 @@
             def _():
                 load_x(r, xarrive).start()
 
-            reduce_first(moves, r, mine, core_in, load_sem.at[9])
 
         @when(valid(c))
         def _():
-            gather_wait(moves, c)
-            for k in range(6):
-                load(k, c).start()
-
-            @when(c % 2 == 0)
-            def _():
-                load_before(c).start()
+            @when(gathers(c))
+            def _():
+                gather_wait(moves, c)
+
+            @when(jnp.logical_not(gathers(c)))
+            def _():
+                load_early(c).wait()
+
+            store(2, c).start()
 
             @when(c == 0)
             def _():
@@ -827,11 +924,11 @@
                     store(k, c - 1).wait()
 
             load(0, c).wait()
-            load(1, c).wait()
-            spread()
+            spread(c)
             store(1, c).start()
-            for k in range(2, 6):
+            for k in range(1, 5):
                 load(k, c).wait()
+            store(2, c).wait()
 
         @when(valid(g))
         def _():
@@ -842,13 +939,19 @@
 
             load_rows(g, gin, g).wait()
 
-            @when(g >= 1)
+            @when((g >= 1) & gathers(g - 1))
             def _():
                 gather_free(moves, g - 1)
 
-            own[...] = kept[g % 4]
-            gather_start(moves, g, keep_sem)
-            vectors[4:5, :] += jnp.sum(kept[g % 4].astype(f32), axis=0, keepdims=True)
+            @when(gathers(g))
+            def _():
+                gather_start(moves, g, kept[g % 3])
+
+            @when(jnp.logical_not(gathers(g)))
+            def _():
+                load_early(g).start()
+
+            vectors[4:5, :] += jnp.sum(kept[g % 3].astype(f32), axis=0, keepdims=True)
 
         @when(valid(c))
         def _():
@@ -865,30 +968,30 @@
 
         @when(valid(r))
         def _():
-            e = reduce_second(moves, r, mine, chip_in, load_sem.at[9])
+            e = reduce_second(moves, r, mine)
             load_x(r, xin).wait()
 
-            @when(r >= 1)
-            def _():
-                line.home_each(place(r - 1), False)
+            @when(r >= 2)
+            def _():
+                grads_home.each(place(r - 2), False)
 
                 @when(source)
                 def _():
-                    moves.hand(r - 1).wait_send()
+                    moves.hand(r - 2).wait_send()
 
             standard, inverse = standardize(xrows[...])
-            d_input = kept[r % 4].astype(f32) + inverse * (
+            d_input = kept[r % 3].astype(f32) + inverse * (
                 e
                 - jnp.mean(e, axis=-1, keepdims=True)
                 - standard * jnp.mean(e * standard, axis=-1, keepdims=True)
             )
-            handed[...] = d_input.astype(bf16)
+            handed[r % 2] = d_input.astype(bf16)
 
             @when(source)
             def _():
                 moves.hand(r).start()
 
-            line.home_each(place(r), True)
+            grads_home.each(place(r), True)
 
         @when(valid(c))
         def _():
@@ -903,11 +1006,28 @@
 
             merge_rows(1 - moves.core, theirs)
             moves.give_theirs(c).start()
+
+        @when(valid(g) & gathers(g))
+        def _():
+            gather_pass(moves, g)
+
+        @when(valid(c))
+        def _():
             merge_rows(moves.core, mine)
-
-        @when(valid(g))
-        def _():
-            gather_pass(moves, g, keep_sem)
+            reduce_first(moves, c, mine)
+
+        @when(valid(c + 1))
+        def _():
+            for k in range(5):
+                load(k, c + 1).start()
+
+            @when((c + 1) % 2 == 0)
+            def _():
+                load_before(c + 1).start()
+
+    @when(gathers(tasks - 1))
+    def _():
+        gather_free(moves, tasks - 1)
 
     drain(moves, tasks - 1)
     for k in range(2):
@@ -918,15 +1038,20 @@
         rest = (value - high.astype(f32)).astype(bf16)
         pair = jnp.concatenate([high, rest, jnp.zeros((14, value.shape[1]), bf16)])
         vectors[2 * k + 1 : 2 * k + 2, :] = jnp.sum(dot(pair, weight[...], NT), axis=0, keepdims=True)
-    line.home_each(place(tasks - 1), False)
-    line.home_wait(tasks)
-
-    @when(source)
-    def _():
-        moves.hand(tasks - 1).wait_send()
-
-
-def backward_pass(gin, xin, xarrive, qkv, dg, ctx, lse, std, wq, wi, wo, wd, gains, tables, pq, pk, chips, heads):
+    for task in range(tasks - 2, tasks):
+        grads_home.each(place(task), False)
+
+        @when(source)
+        def _(task=task):
+            moves.hand(task).wait_send()
+
+    grads_home.wait(tasks)
+    for task in range(tasks):
+        states_home.each(task, False)
+    states_home.wait(tasks)
+
+
+def backward_pass(gin, xin, xarrive, states, early, qkv, dg, ctx, lse, std, wq, wi, wo, wd, gains, tables, pq, pk, chips, heads):
     tasks, rows, width = xin.shape
     count = lax.axis_size("ctx")
     home_sems = line_semaphores(tasks, count)[1]
@@ -942,21 +1067,20 @@
             shape((tasks, block, 3 * inner), bf16),
             shape((tasks, block, units), bf16),
             shape((tasks // 2 * count, 2 * rows // count, width), bf16),
+            shape((tasks // 2 * count, 2 * rows // count, width), bf16),
             shape((tasks, rows, width), bf16),
-            shape((tasks, chips * rows, width), bf16),
-            shape((tasks, chips - 1, rows, width), bf16),
             shape((8, width), f32),
             shape((1, 3 * inner), f32),
             shape((1, units), f32),
         ],
-        in_specs=[anywhere] * 12 + [vmem] * 6,
-        out_specs=[anywhere] * 7 + [vmem] * 3,
+        in_specs=[anywhere] * 14 + [vmem] * 6,
+        out_specs=[anywhere] * 6 + [vmem] * 3,
         scratch_shapes=[
             pltpu.VMEM(wq.shape, bf16),
             pltpu.VMEM(wi.shape, bf16),
             pltpu.VMEM(wo.shape, bf16),
             pltpu.VMEM(wd.shape, bf16),
-            pltpu.VMEM((block, width), bf16),
+            pltpu.VMEM((3, block, width), bf16),
             pltpu.VMEM((block, units), bf16),
             pltpu.VMEM((block, units), bf16),
             pltpu.VMEM((block, 3 * inner), bf16),
@@ -968,20 +1092,19 @@
             pltpu.VMEM((block, 3 * inner), bf16),
             pltpu.VMEM((block, inner), f32),
             pltpu.VMEM((block, inner), f32),
-            pltpu.VMEM((4, rows, width), bf16),
-            pltpu.VMEM((rows, width), bf16),
-            pltpu.VMEM((rows, width), bf16),
+            pltpu.VMEM((3, rows, width), bf16),
             pltpu.VMEM((chips * rows, width), bf16),
             pltpu.VMEM((chips * rows, width), f32),
+            pltpu.VMEM((2, chips * rows, width), bf16),
             pltpu.VMEM((chips * rows, width), bf16),
-            pltpu.VMEM((chips * rows, width), bf16),
-            pltpu.VMEM((chips - 1, rows, width), bf16),
+            pltpu.VMEM((2, chips - 1, rows, width), bf16),
+            pltpu.VMEM((2, rows, width), bf16),
             pltpu.VMEM((rows, width), bf16),
             pltpu.SemaphoreType.DMA((4,)),
-            pltpu.SemaphoreType.DMA((10,)),
-            pltpu.SemaphoreType.DMA((2,)),
-            pltpu.SemaphoreType.DMA,
+            pltpu.SemaphoreType.DMA((9,)),
+            pltpu.SemaphoreType.DMA((3,)),
         ]
+        + home_sems
         + home_sems
         + move_semaphores(tasks, chips),
         compiler_params=pltpu.CompilerParams(
@@ -993,7 +1116,7 @@
             transcendentals=0,
         ),
         name="backward_pass",
-    )(gin, xin, xarrive, qkv, dg, ctx, lse, std, wq, wi, wo, wd, gains, *tables, pq, pk)
+    )(gin, xin, xarrive, states, early, qkv, dg, ctx, lse, std, wq, wi, wo, wd, gains, *tables, pq, pk)
 
 
 CHUNK = 256
@@ -1392,7 +1515,7 @@
 
     chips = tensor // 2
     stacked_tables = [jnp.stack(pair) for pair in zip(*tables)]
-    std_all, qkv, act_all, dg_all, ctx_all, lse_all, chosen_rows, states, arrive, _, _ = forward_pass(
+    std_all, qkv, act_all, dg_all, ctx_all, lse_all, chosen_rows, states, arrive, early = forward_pass(
         chosen,
         wq,
         wi,
@@ -1409,10 +1532,12 @@
         heads,
     )
     gains = jnp.stack([gain_one, gain_two])[:, None]
-    gy_all, dproj_all, dh_all, dx_home, _, _, _, vectors, side_q, side_h = backward_pass(
+    gy_all, dproj_all, dh_all, dx_home, states_home, _, vectors, side_q, side_h = backward_pass(
         chosen_rows,
         chosen_rows,
         arrive,
+        states,
+        early,
         qkv,
         dg_all,
         ctx_all,
@@ -1463,7 +1588,7 @@
     def homeward(pieces):
         return pieces.reshape(micro, seqs, rows, width).transpose(0, 2, 1, 3)[None, :, None]
 
-    states = homeward(states)
+    states = homeward(states_home)
     input_grads = homeward(dx_home).astype(f32)
     return (
         states,

time: 1390 us -> 1350 us (0.971)
  Pallas kernels: 1300 us -> 1260 us
    pallas_call x1, Pallas kernels: 429 us -> 395 us  [backward_pass(): pl.pallas_call(partial(backward_kernel, (tasks, chips, rows, heads)), out...]
where the time goes in v5:
time: 1350 us; the launch traced here: 1340 us
  Pallas kernels  1260 us (93%)
  local copies, waits for them, and re-layouts  39.6 us (3%)
  other arithmetic  34.7 us (3%)
    pallas_call x1, Pallas kernels, reduce_gradients(): pl.pallas_call(partial(reduce_kernel, plan), out_shape=[result, jax.Shape...  584 us
    pallas_call x1, Pallas kernels, backward_pass(): pl.pallas_call(partial(backward_kernel, (tasks, chips, rows, heads)), out...  395 us
    pallas_call x1, Pallas kernels, forward_pass(): pl.pallas_call(partial(forward_kernel, (tasks, chips, rows, heads)), out_...  262 us
  transfers between devices with their start and end apart: 2, of which 0 were waited for; matrix products, arithmetic and copies ran while one was open for 2% of the time, Pallas kernels for 0%

profile of v5, /device:TPU:0, one launch (start us, length us, event | category | flops | bytes accessed | tf_op | source)
XLA Modules:
  0.0 1338.3 jit_solution(4781195156458178811)
XLA Ops:
  0.7 0.1 iota_add_fusion
  0.8 0.7 add.213.pk
  1.4 0.9 add.217.pq
  2.3 0.1 pad.46.clone
  2.4 0.1 pad.38.clone
  2.5 1.3 copy.52
  3.8 0.1 reshape.268
  3.9 0.1 reshape.261
  3.9 0.7 pad_maximum_fusion.9
  4.7 0.6 broadcast_in_dim.141.gains
  5.3 0.8 pad_maximum_fusion.7
  6.1 1.3 copy.45.norms
  7.4 6.9 copy.51
  14.3 0.0 copy-done.8
  14.3 0.0 copy-done.9
  14.3 0.6 add.205.out_bias
  14.9 1.9 multiply_sine_fusion.1
  16.8 0.3 fusion.2
  17.1 0.8 pad_maximum_fusion.2.behind
  18.0 0.2 maximum_bitcast_fusion
  18.2 0.8 pad_maximum_fusion.cosine
  19.0 0.8 pad_maximum_fusion.1.ahead
  19.8 0.0 copy-done
  19.8 0.0 copy-done.1
  19.8 10.2 fusion.chosen
  30.1 262.4 %forward_pass.1 = (bf16[8,512,2048]{2,1,0:T(8,128)(2,1)}, bf16[8,512,1536]{2,1,0:T(8,128)(2,1)}, bf16[8,512,2048]{2,1,0:T(8,128)(2,1)}, bf16[8,512,2048]{2,1,0:T...) custom-call(bf16[4,4,64,2048]{3,2,1,0:T(8,128)(2,1)} %fusion.chosen,, ...), custom_call_target="tpu_custom_call" | custom-call | flops 103079215104 | bytes 134217728 | tf_op jit(solution)/shard_map/forward_pass/pallas_call | solution.py:702
  292.5 0.0 copy-start.6
  292.5 0.0 copy-start.7
  292.5 0.0 copy-start.2
  292.5 0.0 copy-start.3
  292.6 394.7 %backward_pass.1 = (bf16[8,512,2048]{2,1,0:T(8,128)(2,1)}, bf16[8,512,1536]{2,1,0:T(8,128)(2,1)}, bf16[8,512,2048]{2,1,0:T(8,128)(2,1)}, bf16[16,64,2048]{2,1,0:...) custom-call(bf16[8,128,2048]{2,1,0:T(8,128)(2,1)} %get-tuple-element, ...), custom_call_target="tpu_custom_call" | custom-call | flops 103079215104 | bytes 167772160 | tf_op jit(solution)/shard_map/backward_pass/pallas_call | solution.py:1063
  687.3 0.1 collective-permute-start
  687.4 0.1 pad.20.clone
  687.4 0.1 pad.17.clone
  687.5 0.0 copy-done.6
  687.5 0.1 maximum_maximum_fusion.1
  687.6 0.0 copy-done.2
  687.6 0.1 maximum_maximum_fusion
  687.7 0.7 reduce.4
  688.4 0.7 pad_maximum_fusion.8
  689.1 0.0 collective-permute-done
  689.1 0.8 slice_add_fusion
  690.0 0.1 collective-permute-start.1
  690.0 0.7 select_maximum_fusion
  690.7 0.6 broadcast_in_dim.144.biases
  691.4 0.6 broadcast_in_dim.143.gains
  692.0 7.5 copy.61
  699.5 2.2 copy.50.sums
  701.7 9.5 copy.60
  711.1 0.0 collective-permute-done.1
  711.2 0.3 scatter.9.small
  711.5 0.0 copy-start.4
  711.5 0.6 copy-done.4
  712.1 584.1 %reduce_gradients.1 = (bf16[6144,2048]{1,0:T(8,128)(2,1)}, f32[8,2048]{1,0:T(8,128)}, bf16[6144,2048]{1,0:T(8,128)(2,1)}, bf16[6144,2048]{1,0:T(8,128)(2,1)}) custom-call(bf16[8,512,2048]{2,1,0:T(8,128)(2,1)} %get-tuple-element.69.act, bf16[8,512,512]{2,1,0:T(8,128)(2,1)} %get-tuple-element.64.ctx_all.ctx, bf16[8,512,1536]{2,1,0:T(8,128)(2,1)} %get-tuple-element.70.dproj, ...), custom_call_target="tpu_custom_call" | custom-call | flops 103079215104 | bytes 100663296 | tf_op jit(solution)/shard_map/reduce_gradients/pallas_call | solution.py:1400
  1296.3 0.8 slice_bitcast_fusion
  1297.1 1.7 fusion.12
  1298.8 0.6 slice.87
  1299.4 1.7 slice.82
  1301.1 10.3 turned_heads.1
  1311.4 11.7 bitcast_convert_fusion
  1323.1 11.1 turned.1
  1334.2 0.6 reshape.258
  1334.8 2.5 convert.6
  1337.3 0.6 copy.64
  (19 shorter events, 0.1 us)
Async XLA Ops:
  7.4 6.9 copy-start.8
  7.4 6.9 copy-start.9
  14.3 5.5 copy-start
  14.3 5.5 copy-start.1
  292.5 395.0 %copy-start.6 = (f32[1,2048]{1,0:T(1,128)S(1)}, f32[1,2048]{1,0:T(1,128)}, u32[]{:S(2)}) copy-start(f32[1,2048]{1,0:T(1,128)} %param.23) | copy-start | bytes 24580
  292.5 395.0 %copy-start.7 = (f32[1,2048]{1,0:T(1,128)S(1)}, f32[1,2048]{1,0:T(1,128)}, u32[]{:S(2)}) copy-start(f32[1,2048]{1,0:T(1,128)} %param.21) | copy-start | bytes 24580
  292.5 395.1 %copy-start.2 = (f32[1,2048]{1,0:T(1,128)S(1)}, f32[1,2048]{1,0:T(1,128)}, u32[]{:S(2)}) copy-start(f32[1,2048]{1,0:T(1,128)} %param.22) | copy-start | bytes 24580
  292.5 395.1 %copy-start.3 = (f32[1,2048]{1,0:T(1,128)S(1)}, f32[1,2048]{1,0:T(1,128)}, u32[]{:S(2)}) copy-start(f32[1,2048]{1,0:T(1,128)} %param.20) | copy-start | bytes 24580
  687.3 1.8 collective-permute-start
  690.0 21.2 %collective-permute-start.1 = (f32[5,2048]{1,0:T(8,128)S(1)}, f32[5,2048]{1,0:T(8,128)S(1)}, u32[]{:S(2)}, u32[]{:S(2)}) collective-permute-start(f32[5,2048]{1,0:T(8,128)S(1)} %slice_add_fusion), channel_id=1, source_target_pairs={{0,8},{4,12},{8,0},{12,4},{1,9},{5,13},{9,1},{13,5},{2,10},{6,14},... | collective-permute-start | bytes 122888 | tf_op jit(solution)/shard_map/ppermute | solution.py:1566
  711.5 0.6 copy-start.4
  1298.8 38.5 %copy-start.5 = (f32[1,2048]{1,0:T(1,128)}, f32[1,2048]{1,0:T(1,128)S(1)}, u32[]{:S(2)}) copy-start(f32[1,2048]{1,0:T(1,128)S(1)} %get-tuple-element.130) | copy-start | bytes 24580

commit v6 on v5

--- a/solution.py
+++ b/solution.py
@@ -523,6 +523,13 @@
             value = dot(ctx[at, :], wo[:, columns]) + dot(act[at, :], wd[:, columns])
             result[:, columns] = value.astype(result.dtype)
 
+    weights[0].wait()
+    fold(wq, bq_in, bq, 0)
+    weights[1].wait()
+    fold(wi, bi_in, bi, 2)
+    weights[2].wait()
+    weights[3].wait()
+
     @pl.loop(0, tasks + LAG + 2)
     def _(step):
         g = step - base
@@ -600,15 +607,6 @@
 
             gather_start(moves, g, standardize(kept[g % 3])[0].astype(bf16))
 
-        @when(step == 0)
-        def _():
-            weights[0].wait()
-            fold(wq, bq_in, bq, 0)
-            weights[1].wait()
-            fold(wi, bi_in, bi, 2)
-            weights[2].wait()
-            weights[3].wait()
-
         @when(valid(c))
         def _():
             expand(c)
@@ -644,14 +642,12 @@
             branch_rows(1 - moves.core, theirs)
             moves.give_theirs(c).start()
 
-        @when(valid(g))
-        def _():
-            gather_pass(moves, g)
-
-        @when(valid(c))
-        def _():
             branch_rows(moves.core, mine)
             reduce_first(moves, c, mine)
+
+        @when(valid(g))
+        def _():
+            gather_pass(moves, g)
 
     gather_free(moves, tasks - 1)
     drain(moves, tasks - 1)
@@ -758,10 +754,10 @@
 def backward_kernel(
     plan, gin, xin, xarrive, states, early_all, qkv_all, dg_all, ctx_all, lse_all, std_all, wq_all, wi_all, wo_all, wd_all,
     gains, cosine, ahead, behind, pq, pk,
-    gy_all, dproj_all, dh_all, home, state_home, arrive, vectors, side_q, side_h,
+    gy_all, dproj_all, dh_all, home, state_home, last_rows, arrive, vectors, side_q, side_h,
     wq, wi, wo, wd, land, dg, dh, qkv, before, ctx, lse, std, dctx, dproj, dk_held, dv_held,
     kept, theirs, mine, core_land, low, chip_land, handed, xrows,
-    weight_sem, load_sem, store_sem,
+    weight_sem, load_sem, store_sem, last_sem,
     put_home, got_home, kept_home, put_state, got_state, kept_state, *sems,
 ):
     tasks, chips, rows, heads = plan
@@ -870,6 +866,17 @@
             value = one * gains[0, :, columns] + two * gains[1, :, columns]
             result[:, columns] = value.astype(result.dtype)
 
+    def keep_last():
+        return pltpu.make_async_copy(handed.at[(tasks - 1) % 2], last_rows, last_sem)
+
+    def side_products():
+        for k, (side, weight) in enumerate(((side_q, wq), (side_h, wi))):
+            value = side[...]
+            high = value.astype(bf16)
+            rest = (value - high.astype(f32)).astype(bf16)
+            pair = jnp.concatenate([high, rest, jnp.zeros((14, value.shape[1]), bf16)])
+            vectors[2 * k + 1 : 2 * k + 2, :] = jnp.sum(dot(pair, weight[...], NT), axis=0, keepdims=True)
+
     @pl.loop(0, tasks + LAG + 2)
     def _(step):
         g = step - base
@@ -968,6 +975,10 @@
 
         @when(valid(r))
         def _():
+            @when(r == tasks - 1)
+            def _():
+                side_products()
+
             e = reduce_second(moves, r, mine)
             load_x(r, xin).wait()
 
@@ -991,7 +1002,13 @@
             def _():
                 moves.hand(r).start()
 
-            grads_home.each(place(r), True)
+            @when(r < tasks - 1)
+            def _():
+                grads_home.each(place(r), True)
+
+            @when(r == tasks - 1)
+            def _():
+                keep_last().start()
 
         @when(valid(c))
         def _():
@@ -1007,14 +1024,12 @@
             merge_rows(1 - moves.core, theirs)
             moves.give_theirs(c).start()
 
-        @when(valid(g) & gathers(g))
-        def _():
-            gather_pass(moves, g)
-
-        @when(valid(c))
-        def _():
             merge_rows(moves.core, mine)
             reduce_first(moves, c, mine)
+
+        @when(valid(g) & gathers(g))
+        def _():
+            gather_pass(moves, g)
 
         @when(valid(c + 1))
         def _():
@@ -1032,20 +1047,21 @@
     drain(moves, tasks - 1)
     for k in range(2):
         store(k, tasks - 1).wait()
-    for k, (side, weight) in enumerate(((side_q, wq), (side_h, wi))):
-        value = side[...]
-        high = value.astype(bf16)
-        rest = (value - high.astype(f32)).astype(bf16)
-        pair = jnp.concatenate([high, rest, jnp.zeros((14, value.shape[1]), bf16)])
-        vectors[2 * k + 1 : 2 * k + 2, :] = jnp.sum(dot(pair, weight[...], NT), axis=0, keepdims=True)
+    grads_home.each(place(tasks - 2), False)
+    keep_last().wait()
     for task in range(tasks - 2, tasks):
-        grads_home.each(place(task), False)
 
         @when(source)
         def _(task=task):
             moves.hand(task).wait_send()
 
-    grads_home.wait(tasks)
+    grads_home.wait(tasks - 2)
+
+    @when(line.z >= line.blocks)
+    def _():
+        for other in line.others():
+            grads_home.take(tasks - 1, 0, other).wait_recv()
+
     for task in range(tasks):
         states_home.each(task, False)
     states_home.wait(tasks)
@@ -1068,13 +1084,14 @@
             shape((tasks, block, units), bf16),
             shape((tasks // 2 * count, 2 * rows // count, width), bf16),
             shape((tasks // 2 * count, 2 * rows // count, width), bf16),
+            shape((rows, width), bf16),
             shape((tasks, rows, width), bf16),
             shape((8, width), f32),
             shape((1, 3 * inner), f32),
             shape((1, units), f32),
         ],
         in_specs=[anywhere] * 14 + [vmem] * 6,
-        out_specs=[anywhere] * 6 + [vmem] * 3,
+        out_specs=[anywhere] * 7 + [vmem] * 3,
         scratch_shapes=[
             pltpu.VMEM(wq.shape, bf16),
             pltpu.VMEM(wi.shape, bf16),
@@ -1103,6 +1120,7 @@
             pltpu.SemaphoreType.DMA((4,)),
             pltpu.SemaphoreType.DMA((9,)),
             pltpu.SemaphoreType.DMA((3,)),
+            pltpu.SemaphoreType.DMA,
         ]
         + home_sems
         + home_sems
@@ -1125,10 +1143,11 @@
 
 
 def reduce_kernel(
-    plan, act, ctx, dproj, dhid, gy, std, gains, biases, sums, small, out, small_out, from_left, from_right,
+    plan, act, ctx, dproj, dhid, gy, std, late, gains, biases, sums, small,
+    out, small_out, late_home, from_left, from_right,
     rhs, raw, lhs, own, inbox, outbox, stage, small_in,
     rhs_sem, raw_sem, right_sem, left_sem, final_sem, load_sem, sent, stage_left, stage_right, out_sem,
-    small_sent, small_got,
+    small_sent, small_got, late_sent, late_got, late_kept,
 ):
     bounds, tasks, count, piece, skew, ring = plan
     sources = (dproj, dhid, act, ctx)
@@ -1163,6 +1182,24 @@
             device_id_type=pl.DeviceIdType.MESH,
         )
 
+    late_blocks = count // 2
+    late_rows = late.shape[0] // late_blocks
+
+    def late_copy(k, source):
+        return pltpu.make_async_remote_copy(
+            src_ref=late.at[pl.ds(k * late_rows, late_rows)],
+            dst_ref=late_home.at[source],
+            send_sem=late_sent.at[k],
+            recv_sem=late_got.at[source],
+            device_id={"ctx": k},
+            device_id_type=pl.DeviceIdType.MESH,
+        )
+
+    def late_keep(k):
+        return pltpu.make_async_copy(
+            late.at[pl.ds(k * late_rows, late_rows)], late_home.at[z], late_kept
+        )
+
     def rhs_copy(k):
         return pltpu.make_async_copy((std, gy)[k].at[pl.ds(0, tasks)], rhs.at[k], rhs_sem.at[k])
 
@@ -1340,6 +1377,15 @@
     small_in[z] = small[...]
     for shift in range(1, count):
         small_copy(z, lax.rem(z + shift, count)).start()
+    for k in range(late_blocks):
+
+        @pl.when(z != k)
+        def _(k=k):
+            late_copy(k, z).start()
+
+        @pl.when(z == k)
+        def _(k=k):
+            late_keep(k).start()
 
     @pl.loop(0, pieces + (turn_at + max(root, last - root)) * skew)
     def _(step):
@@ -1364,6 +1410,18 @@
         other = lax.rem(z + shift, count)
         small_copy(z, other).wait_send()
         small_copy(other, other).wait_recv()
+    for k in range(late_blocks):
+
+        @pl.when(z != k)
+        def _(k=k):
+            late_copy(k, z).wait_send()
+
+        @pl.when(z == k)
+        def _(k=k):
+            late_keep(k).wait()
+            for shift in range(1, count):
+                late_copy(k, lax.rem(z + shift, count)).wait_recv()
+
     value = small_in[0]
     for k in range(1, count):
         value = value + small_in[k]
@@ -1384,7 +1442,7 @@
             stage_done(pieces - back)
 
 
-def reduce_gradients(act, ctx, dproj, dhid, gy, std, gains, biases, sums, small, tasks):
+def reduce_gradients(act, ctx, dproj, dhid, gy, std, late, gains, biases, sums, small, tasks):
     count = lax.axis_size("ctx")
     block, width = gy.shape[1:]
     bounds = [0]
@@ -1397,11 +1455,12 @@
     anywhere = pl.BlockSpec(memory_space=pl.ANY)
     vmem = pl.BlockSpec(memory_space=pltpu.VMEM)
     result = jax.ShapeDtypeStruct((total, width), bf16)
-    out, small_out, _, _ = pl.pallas_call(
+    late_shape = jax.ShapeDtypeStruct((count, 2 * late.shape[0] // count, width), bf16)
+    out, small_out, late_home, _, _ = pl.pallas_call(
         partial(reduce_kernel, plan),
-        out_shape=[result, jax.ShapeDtypeStruct(small.shape, f32), result, result],
-        in_specs=[anywhere] * 6 + [vmem] * 4,
-        out_specs=[anywhere, vmem, anywhere, anywhere],
+        out_shape=[result, jax.ShapeDtypeStruct(small.shape, f32), late_shape, result, result],
+        in_specs=[anywhere] * 7 + [vmem] * 4,
+        out_specs=[anywhere, vmem, anywhere, anywhere, anywhere],
         scratch_shapes=[
             pltpu.VMEM((2, tasks, block, width), bf16),
             pltpu.VMEM((2, tasks, block, CHUNK), bf16),
@@ -1423,6 +1482,9 @@
             pltpu.SemaphoreType.DMA((2,)),
             pltpu.SemaphoreType.DMA((count,)),
             pltpu.SemaphoreType.DMA((count,)),
+            pltpu.SemaphoreType.DMA((count // 2,)),
+            pltpu.SemaphoreType.DMA((count,)),
+            pltpu.SemaphoreType.DMA,
         ],
         compiler_params=pltpu.CompilerParams(
             collective_id=7, has_side_effects=True, vmem_limit_bytes=60 * 1024 * 1024
@@ -1433,8 +1495,8 @@
             transcendentals=0,
         ),
         name="reduce_gradients",
-    )(act, ctx, dproj, dhid, gy, std, gains, biases, sums, small)
-    return out, small_out
+    )(act, ctx, dproj, dhid, gy, std, late, gains, biases, sums, small)
+    return out, small_out, late_home
 
 
 def turned_kernel(part, out):
@@ -1443,12 +1505,13 @@
 
 def turned(total, start, count):
     width = total.shape[1]
+    wide = 2 * CHUNK if start % (2 * CHUNK) == 0 and count % (2 * CHUNK) == 0 else CHUNK
     return pl.pallas_call(
         turned_kernel,
         out_shape=jax.ShapeDtypeStruct((width, count), f32),
-        grid=(count // CHUNK,),
-        in_specs=[pl.BlockSpec((CHUNK, width), lambda i: (start // CHUNK + i, 0))],
-        out_specs=pl.BlockSpec((width, CHUNK), lambda i: (0, i)),
+        grid=(count // wide,),
+        in_specs=[pl.BlockSpec((wide, width), lambda i: (start // wide + i, 0))],
+        out_specs=pl.BlockSpec((width, wide), lambda i: (0, i)),
         compiler_params=pltpu.CompilerParams(vmem_limit_bytes=32 * 1024 * 1024),
         name="turned",
     )(total)
@@ -1532,7 +1595,7 @@
         heads,
     )
     gains = jnp.stack([gain_one, gain_two])[:, None]
-    gy_all, dproj_all, dh_all, dx_home, states_home, _, vectors, side_q, side_h = backward_pass(
+    gy_all, dproj_all, dh_all, dx_home, states_home, last_rows, _, vectors, side_q, side_h = backward_pass(
         chosen_rows,
         chosen_rows,
         arrive,
@@ -1572,8 +1635,8 @@
     small = small.at[5 : 5 + side_rows].set(
         jnp.pad(sides, (0, side_rows * width - sides.shape[0])).reshape(side_rows, width)
     )
-    summed, small = reduce_gradients(
-        act_all, ctx_all, dproj_all, dh_all, gy_all, std_all, gains, biases, sums, small, tasks
+    summed, small, late_home = reduce_gradients(
+        act_all, ctx_all, dproj_all, dh_all, gy_all, std_all, last_rows, gains, biases, sums, small, tasks
     )
     columns = wq.shape[1]
     vectors = small[:5]
@@ -1589,7 +1652,8 @@
         return pieces.reshape(micro, seqs, rows, width).transpose(0, 2, 1, 3)[None, :, None]
 
     states = homeward(states_home)
-    input_grads = homeward(dx_home).astype(f32)
+    late_home = jnp.where(lax.axis_index("ctx") < blocks, late_home, dx_home[-ctx_count:])
+    input_grads = homeward(jnp.concatenate([dx_home[:-ctx_count], late_home])).astype(f32)
     return (
         states,
         input_grads,

time: 1350 us -> 1310 us (0.970)
  Pallas kernels: 1260 us -> 1210 us
    pallas_call x1, Pallas kernels: 395 us -> 356 us  [backward_pass(): pl.pallas_call(partial(backward_kernel, (tasks, chips, rows, heads)), out...]
    pallas_call x1, Pallas kernels: 262 us -> 240 us  [forward_pass(): pl.pallas_call(partial(forward_kernel, (tasks, chips, rows, heads)), out_...]
  transfers between devices with their start and end apart: 2 -> 2, of which waited for: 0 -> 0; matrix products, arithmetic and copies ran while one was open for 2% -> 1% of each run, Pallas kernels for 0% -> 0%
where the time goes in v6:
time: 1310 us; the launch traced here: 1290 us
  Pallas kernels  1210 us (92%)
  local copies, waits for them, and re-layouts  40.3 us (3%)
  other arithmetic  38 us (3%)
    pallas_call x1, Pallas kernels, reduce_gradients(): pl.pallas_call(partial(reduce_kernel, plan), out_shape=[result, jax.Shape...  597 us
    pallas_call x1, Pallas kernels, backward_pass(): pl.pallas_call(partial(backward_kernel, (tasks, chips, rows, heads)), out...  356 us
    pallas_call x1, Pallas kernels, forward_pass(): pl.pallas_call(partial(forward_kernel, (tasks, chips, rows, heads)), out_...  240 us
  transfers between devices with their start and end apart: 2, of which 0 were waited for; matrix products, arithmetic and copies ran while one was open for 1% of the time, Pallas kernels for 0%

profile of v6, /device:TPU:0, one launch (start us, length us, event | category | flops | bytes accessed | tf_op | source)
XLA Modules:
  0.0 1294.1 jit_solution(13863217612084751966)
XLA Ops:
  0.7 0.1 iota_add_fusion
  0.8 0.7 add.213.pk
  1.4 0.9 add.217.pq
  2.3 0.1 pad.48.clone
  2.4 0.1 pad.40.clone
  2.5 1.3 copy.52
  3.8 0.1 reshape.268
  3.9 0.1 reshape.261
  4.0 0.7 pad_maximum_fusion.10
  4.7 0.6 broadcast_in_dim.141.gains
  5.3 0.8 pad_maximum_fusion.8
  6.1 1.3 copy.45.norms
  7.4 6.9 copy.51
  14.3 0.6 add.205.out_bias
  14.9 1.9 multiply_sine_fusion.1
  16.9 0.3 fusion.2
  17.1 0.8 pad_maximum_fusion.3.behind
  18.0 0.2 maximum_bitcast_fusion
  18.2 0.8 pad_maximum_fusion.1.cosine
  19.0 0.8 pad_maximum_fusion.2.ahead
  19.8 10.2 fusion.chosen
  30.1 240.2 %forward_pass.1 = (bf16[8,512,2048]{2,1,0:T(8,128)(2,1)}, bf16[8,512,1536]{2,1,0:T(8,128)(2,1)}, bf16[8,512,2048]{2,1,0:T(8,128)(2,1)}, bf16[8,512,2048]{2,1,0:T...) custom-call(bf16[4,4,64,2048]{3,2,1,0:T(8,128)(2,1)} %fusion.chosen,, ...), custom_call_target="tpu_custom_call" | custom-call | flops 103079215104 | bytes 134217728 | tf_op jit(solution)/shard_map/forward_pass/pallas_call | solution.py:698
  270.2 0.0 copy-start.7
  270.3 0.0 copy-start.8
  270.3 0.0 copy-start.3
  270.3 0.0 copy-start.4
  270.3 356.4 %backward_pass.1 = (bf16[8,512,2048]{2,1,0:T(8,128)(2,1)}, bf16[8,512,1536]{2,1,0:T(8,128)(2,1)}, bf16[8,512,2048]{2,1,0:T(8,128)(2,1)}, bf16[16,64,2048]{2,1,0:...) custom-call(bf16[8,128,2048]{2,1,0:T(8,128)(2,1)} %get-tuple-element, ...), custom_call_target="tpu_custom_call" | custom-call | flops 103079215104 | bytes 167772160 | tf_op jit(solution)/shard_map/backward_pass/pallas_call | solution.py:1079
  626.7 0.1 collective-permute-start
  626.8 0.1 pad.22.clone
  626.9 0.1 pad.19.clone
  627.0 0.0 copy-done.8
  627.0 0.1 maximum_maximum_fusion.1
  627.1 0.1 maximum_maximum_fusion
  627.1 0.7 reduce.4
  627.9 0.7 pad_maximum_fusion.9
  628.6 0.0 collective-permute-done
  628.6 0.8 slice_add_fusion
  629.4 0.1 collective-permute-start.1
  629.5 0.7 select_maximum_fusion
  630.2 0.6 broadcast_in_dim.144.biases
  630.8 0.6 broadcast_in_dim.143.gains
  631.4 7.5 copy.61
  638.9 2.2 copy.49.sums
  641.1 2.1 slice.81
  643.2 0.0 collective-permute-done.1
  643.3 0.3 scatter.9.small
  643.6 0.0 copy-start.5
  643.6 0.6 copy-done.5
  644.2 597.2 %reduce_gradients.1 = (bf16[6144,2048]{1,0:T(8,128)(2,1)}, f32[8,2048]{1,0:T(8,128)}, bf16[4,64,2048]{2,1,0:T(8,128)(2,1)}, bf16[6144,2048]{1,0:T(8,128)(2,1)}, bf16[6144,2048]{1,0:T(8,128)(2,1)}) custom-call(bf16[8,512,2048]{2,1,0:T(8,128)(2,1)} %get-tuple-element.71.act, bf16[8,512,512]{2,1,0:T(8,128)(2,1)} %get-tuple-element.66.ctx_all.ctx, ...), custom_call_target="tpu_custom_call" | custom-call | flops 103079215104 | bytes 100663296 | tf_op jit(solution)/shard_map/reduce_gradients/pallas_call | solution.py:1459
  1241.4 0.8 slice_bitcast_fusion
  1242.3 1.7 fusion.12
  1243.9 0.6 slice.95
  1244.5 3.2 slice.90
  1247.7 10.3 turned_heads.1
  1258.0 11.7 bitcast_convert_fusion
  1269.6 10.6 turned.1
  1280.2 0.6 reshape.258
  1280.8 4.2 convert.6
  1285.0 0.0 copy-done.2
  1285.0 1.3 slice_select_fusion
  1286.3 0.4 pad_maximum_fusion
  1286.7 6.6 copy.60
  1293.4 0.0 copy-done.6
  1293.4 0.6 copy.64
  (24 shorter events, 0.1 us)
Async XLA Ops:
  7.4 6.9 copy-start.9
  7.4 6.9 copy-start.10
  14.9 4.9 copy-start
  14.9 4.9 copy-start.1
  270.2 356.7 %copy-start.7 = (f32[1,2048]{1,0:T(1,128)S(1)}, f32[1,2048]{1,0:T(1,128)}, u32[]{:S(2)}) copy-start(f32[1,2048]{1,0:T(1,128)} %param.23) | copy-start | bytes 24580
  270.3 356.7 %copy-start.8 = (f32[1,2048]{1,0:T(1,128)S(1)}, f32[1,2048]{1,0:T(1,128)}, u32[]{:S(2)}) copy-start(f32[1,2048]{1,0:T(1,128)} %param.21) | copy-start | bytes 24580
  270.3 356.8 %copy-start.3 = (f32[1,2048]{1,0:T(1,128)S(1)}, f32[1,2048]{1,0:T(1,128)}, u32[]{:S(2)}) copy-start(f32[1,2048]{1,0:T(1,128)} %param.22) | copy-start | bytes 24580
  270.3 356.8 %copy-start.4 = (f32[1,2048]{1,0:T(1,128)S(1)}, f32[1,2048]{1,0:T(1,128)}, u32[]{:S(2)}) copy-start(f32[1,2048]{1,0:T(1,128)} %param.20) | copy-start | bytes 24580
  626.7 1.8 collective-permute-start
  629.4 13.8 %collective-permute-start.1 = (f32[5,2048]{1,0:T(8,128)S(1)}, f32[5,2048]{1,0:T(8,128)S(1)}, u32[]{:S(2)}, u32[]{:S(2)}) collective-permute-start(f32[5,2048]{1,0:T(8,128)S(1)} %slice_add_fusion), channel_id=1, source_target_pairs={{0,8},{4,12},{8,0},{12,4},{1,9},{5,13},{9,1},{13,5},{2,10},{6,14},... | collective-permute-start | bytes 122888 | tf_op jit(solution)/shard_map/ppermute | solution.py:1629
  643.6 0.6 copy-start.5
  1243.9 49.4 %copy-start.6 = (f32[1,2048]{1,0:T(1,128)}, f32[1,2048]{1,0:T(1,128)S(1)}, u32[]{:S(2)}) copy-start(f32[1,2048]{1,0:T(1,128)S(1)} %get-tuple-element.134) | copy-start | bytes 24580
  1280.8 4.2 copy-start.2

commit v7 on v6

--- a/solution.py
+++ b/solution.py
@@ -2,6 +2,7 @@
 
 import jax
 import jax.numpy as jnp
+import numpy as np
 from jax import lax
 from jax.experimental import pallas as pl
 from jax.experimental.pallas import tpu as pltpu
@@ -32,28 +33,27 @@
     return centred * inverse, inverse
 
 
-def position_tables(section_rows, blocks, rows, tensor):
-    half = ROT // 2
-    frequency = 1.0 / 10000.0 ** (jnp.arange(0, ROT, 2, dtype=f32) / ROT)
-    core, chip, c, i = jnp.meshgrid(
-        jnp.arange(2), jnp.arange(tensor // 2), jnp.arange(blocks), jnp.arange(rows), indexing="ij"
+def position_tables(blocks, rows, tensor):
+    frequency = (1.0 / 10000.0 ** (np.arange(0, ROT, 2) / ROT)).astype(np.float32)
+    core, chip, c, i = np.meshgrid(
+        np.arange(2), np.arange(tensor // 2), np.arange(blocks), np.arange(rows), indexing="ij"
     )
-    relative = (c * (rows * tensor) + (chip * 2 + core) * rows + i).reshape(-1).astype(jnp.int32)
+    relative = (c * (rows * tensor) + (chip * 2 + core) * rows + i).reshape(-1).astype(np.int32)
     tables = []
     for part in range(2):
-        places = (relative + part * blocks * rows * tensor).astype(f32)
-        angles = places[:, None] * frequency[None, :]
-        cosine, sine = jnp.cos(angles), jnp.sin(angles)
-        none = jnp.zeros_like(sine)
-        rest = jnp.zeros((relative.shape[0], LANES - ROT), f32)
+        places = (relative + part * blocks * rows * tensor).astype(np.float32)
+        angles = (places[:, None] * frequency[None, :]).astype(np.float64)
+        cosine, sine = np.cos(angles), np.sin(angles)
+        none = np.zeros_like(sine)
+        rest = np.zeros((relative.shape[0], LANES - ROT))
         tables.append(
             (
-                jnp.concatenate([cosine, cosine, rest + 1.0], axis=-1),
-                jnp.concatenate([-sine, none, rest], axis=-1),
-                jnp.concatenate([none, sine, rest], axis=-1),
+                np.concatenate([cosine, cosine, rest + 1.0], axis=-1),
+                np.concatenate([-sine, none, rest], axis=-1),
+                np.concatenate([none, sine, rest], axis=-1),
             )
         )
-    return relative, tables
+    return relative, [jnp.asarray(np.stack(pair).astype(np.float32)) for pair in zip(*tables)]
 
 
 def turn(values, cosine, ahead, behind, sign):
@@ -784,7 +784,7 @@
         pltpu.make_async_copy(a, b, weight_sem.at[k])
         for k, (a, b) in enumerate(((wo_all, wo), (wd_all, wd), (wq_all, wq), (wi_all, wi)))
     ]
-    for copy in weights:
+    for copy in weights[:2]:
         copy.start()
     for total in (vectors, side_q, side_h):
         total[...] = jnp.zeros_like(total)
@@ -1002,11 +1002,11 @@
             def _():
                 moves.hand(r).start()
 
-            @when(r < tasks - 1)
+            @when((r < tasks - 1) | (line.z != line.blocks))
             def _():
                 grads_home.each(place(r), True)
 
-            @when(r == tasks - 1)
+            @when((r == tasks - 1) & (line.z == line.blocks))
             def _():
                 keep_last().start()
 
@@ -1039,6 +1039,11 @@
             @when((c + 1) % 2 == 0)
             def _():
                 load_before(c + 1).start()
+
+            @when(c + 1 == 0)
+            def _():
+                for copy in weights[2:]:
+                    copy.start()
 
     @when(gathers(tasks - 1))
     def _():
@@ -1048,7 +1053,15 @@
     for k in range(2):
         store(k, tasks - 1).wait()
     grads_home.each(place(tasks - 2), False)
-    keep_last().wait()
+
+    @when(line.z != line.blocks)
+    def _():
+        grads_home.each(place(tasks - 1), False)
+
+    @when(line.z == line.blocks)
+    def _():
+        keep_last().wait()
+
     for task in range(tasks - 2, tasks):
 
         @when(source)
@@ -1057,9 +1070,10 @@
 
     grads_home.wait(tasks - 2)
 
-    @when(line.z >= line.blocks)
-    def _():
-        for other in line.others():
+    for other in line.others():
+
+        @when((line.z >= line.blocks) | (other != line.blocks))
+        def _(other=other):
             grads_home.take(tasks - 1, 0, other).wait_recv()
 
     for task in range(tasks):
@@ -1147,7 +1161,7 @@
     out, small_out, late_home, from_left, from_right,
     rhs, raw, lhs, own, inbox, outbox, stage, small_in,
     rhs_sem, raw_sem, right_sem, left_sem, final_sem, load_sem, sent, stage_left, stage_right, out_sem,
-    small_sent, small_got, late_sent, late_got, late_kept,
+    small_sent, small_got, late_sent, late_got,
 ):
     bounds, tasks, count, piece, skew, ring = plan
     sources = (dproj, dhid, act, ctx)
@@ -1185,19 +1199,14 @@
     late_blocks = count // 2
     late_rows = late.shape[0] // late_blocks
 
-    def late_copy(k, source):
+    def late_copy(k):
         return pltpu.make_async_remote_copy(
             src_ref=late.at[pl.ds(k * late_rows, late_rows)],
-            dst_ref=late_home.at[source],
+            dst_ref=late_home,
             send_sem=late_sent.at[k],
-            recv_sem=late_got.at[source],
+            recv_sem=late_got,
             device_id={"ctx": k},
             device_id_type=pl.DeviceIdType.MESH,
-        )
-
-    def late_keep(k):
-        return pltpu.make_async_copy(
-            late.at[pl.ds(k * late_rows, late_rows)], late_home.at[z], late_kept
         )
 
     def rhs_copy(k):
@@ -1377,15 +1386,10 @@
     small_in[z] = small[...]
     for shift in range(1, count):
         small_copy(z, lax.rem(z + shift, count)).start()
-    for k in range(late_blocks):
-
-        @pl.when(z != k)
-        def _(k=k):
-            late_copy(k, z).start()
-
-        @pl.when(z == k)
-        def _(k=k):
-            late_keep(k).start()
+    @pl.when(middle)
+    def _():
+        for k in range(late_blocks):
+            late_copy(k).start()
 
     @pl.loop(0, pieces + (turn_at + max(root, last - root)) * skew)
     def _(step):
@@ -1410,17 +1414,14 @@
         other = lax.rem(z + shift, count)
         small_copy(z, other).wait_send()
         small_copy(other, other).wait_recv()
-    for k in range(late_blocks):
-
-        @pl.when(z != k)
-        def _(k=k):
-            late_copy(k, z).wait_send()
-
-        @pl.when(z == k)
-        def _(k=k):
-            late_keep(k).wait()
-            for shift in range(1, count):
-                late_copy(k, lax.rem(z + shift, count)).wait_recv()
+    @pl.when(middle)
+    def _():
+        for k in range(late_blocks):
+            late_copy(k).wait_send()
+
+    @pl.when(low)
+    def _():
+        late_copy(0).wait_recv()
 
     value = small_in[0]
     for k in range(1, count):
@@ -1455,7 +1456,7 @@
     anywhere = pl.BlockSpec(memory_space=pl.ANY)
     vmem = pl.BlockSpec(memory_space=pltpu.VMEM)
     result = jax.ShapeDtypeStruct((total, width), bf16)
-    late_shape = jax.ShapeDtypeStruct((count, 2 * late.shape[0] // count, width), bf16)
+    late_shape = jax.ShapeDtypeStruct((2 * late.shape[0] // count, width), bf16)
     out, small_out, late_home, _, _ = pl.pallas_call(
         partial(reduce_kernel, plan),
         out_shape=[result, jax.ShapeDtypeStruct(small.shape, f32), late_shape, result, result],
@@ -1483,7 +1484,6 @@
             pltpu.SemaphoreType.DMA((count,)),
             pltpu.SemaphoreType.DMA((count,)),
             pltpu.SemaphoreType.DMA((count // 2,)),
-            pltpu.SemaphoreType.DMA((count,)),
             pltpu.SemaphoreType.DMA,
         ],
         compiler_params=pltpu.CompilerParams(
@@ -1562,8 +1562,12 @@
     blocks = ctx_count // 2
     tasks = 2 * per_device
 
-    chosen = jnp.where(first, inputs[:, 0], out_grads[:, 0])
-    chosen = chosen.transpose(0, 2, 1, 3).reshape(per_device, ctx_count, rows, width)
+    chosen = lax.cond(
+        first,
+        lambda: inputs[:, 0].transpose(0, 2, 1, 3),
+        lambda: out_grads[:, 0].transpose(0, 2, 1, 3),
+    )
+    chosen = chosen.reshape(per_device, ctx_count, rows, width)
 
     wq = w_qkv[0].reshape(width, heads * head_cols)
     wi = input_projection[0]
@@ -1573,11 +1577,10 @@
     norms = jnp.stack([gain_one, bias_one, gain_two, bias_two], axis=1)
     out_bias = (b_out[0] + b_down[0])[None]
 
-    relative, tables = position_tables(None, blocks, rows, tensor)
-    places_q, places_k = relative[:, None], relative[None, :]
+    relative, tables = position_tables(blocks, rows, tensor)
+    places_q, places_k = jnp.asarray(relative[:, None]), jnp.asarray(relative[None, :])
 
     chips = tensor // 2
-    stacked_tables = [jnp.stack(pair) for pair in zip(*tables)]
     std_all, qkv, act_all, dg_all, ctx_all, lse_all, chosen_rows, states, arrive, early = forward_pass(
         chosen,
         wq,
@@ -1588,7 +1591,7 @@
         input_bias_vector,
         norms,
         out_bias,
-        stacked_tables,
+        tables,
         places_q,
         places_k,
         chips,
@@ -1611,7 +1614,7 @@
         wo,
         wd,
         gains,
-        stacked_tables,
+        tables,
         places_q,
         places_k,
         chips,
@@ -1652,8 +1655,9 @@
         return pieces.reshape(micro, seqs, rows, width).transpose(0, 2, 1, 3)[None, :, None]
 
     states = homeward(states_home)
-    late_home = jnp.where(lax.axis_index("ctx") < blocks, late_home, dx_home[-ctx_count:])
-    input_grads = homeward(jnp.concatenate([dx_home[:-ctx_count], late_home])).astype(f32)
+    at = (per_device - 1) * ctx_count + blocks
+    late_home = jnp.where(lax.axis_index("ctx") < blocks, late_home, dx_home[at])
+    input_grads = homeward(lax.dynamic_update_index_in_dim(dx_home, late_home, at, 0)).astype(f32)
     return (
         states,
         input_grads,

time: 1310 us -> 1290 us (0.985)
  other arithmetic: 38 us -> 18.9 us
    pallas_call x1, Pallas kernels: 597 us -> 584 us  [reduce_gradients(): pl.pallas_call(partial(reduce_kernel, plan), out_shape=[result, jax.Shape...]
where the time goes in v7:
time: 1290 us; the launch traced here: 1280 us
  Pallas kernels  1210 us (94%)
  local copies, waits for them, and re-layouts  44.5 us (3%)
  other arithmetic  18.9 us (1%)
    pallas_call x1, Pallas kernels, reduce_gradients(): pl.pallas_call(partial(reduce_kernel, plan), out_shape=[result, jax.Shape...  584 us
    pallas_call x1, Pallas kernels, backward_pass(): pl.pallas_call(partial(backward_kernel, (tasks, chips, rows, heads)), out...  368 us
    pallas_call x1, Pallas kernels, forward_pass(): pl.pallas_call(partial(forward_kernel, (tasks, chips, rows, heads)), out_...  240 us
  transfers between devices with their start and end apart: 2, of which 0 were waited for; matrix products, arithmetic and copies ran while one was open for 1% of the time, Pallas kernels for 0%

profile of v7, /device:TPU:0, one launch (start us, length us, event | category | flops | bytes accessed | tf_op | source)
XLA Modules:
  0.0 1278.5 jit_solution(7200303128406754603)
XLA Ops:
  0.7 0.0 copy-start.13
  0.7 0.0 copy-start.1
  0.7 0.0 copy-start.3
  0.7 0.0 copy-start.7
  0.7 0.0 copy-start.9
  0.7 0.0 copy-start.11
  0.7 0.0 copy-start.12
  0.7 6.9 copy.53
  7.6 0.0 copy-done.13
  7.6 0.6 copy.54
  8.2 0.0 copy-done.1
  8.2 0.0 copy-done.3
  8.2 0.0 copy-done.7
  8.2 0.0 copy-done.9
  8.3 1.3 copy.47.norms
  9.6 0.6 broadcast_in_dim.37.gains
  10.3 0.0 copy-done.11
  10.3 0.0 copy-done.12
  10.3 0.6 add.20.out_bias
  10.9 6.5 conditional.1
  10.9 6.5 copy.52
  17.4 240.2 %forward_pass.1 = (bf16[8,512,2048]{2,1,0:T(8,128)(2,1)}, bf16[8,512,1536]{2,1,0:T(8,128)(2,1)}, bf16[8,512,2048]{2,1,0:T(8,128)(2,1)}, bf16[8,512,2048]{2,1,0:T...) custom-call(bf16[4,4,64,2048]{3,2,1,0:T(8,128)(2,1)} %get-tuple-elem, ...), custom_call_target="tpu_custom_call" | custom-call | flops 103079215104 | bytes 134217728 | tf_op jit(solution)/shard_map/forward_pass/pallas_call | solution.py:698
  257.6 0.0 copy-start.2
  257.6 0.0 copy-start.4
  257.6 0.0 copy-start.8
  257.6 0.0 copy-start.10
  257.6 368.3 %backward_pass.1 = (bf16[8,512,2048]{2,1,0:T(8,128)(2,1)}, bf16[8,512,1536]{2,1,0:T(8,128)(2,1)}, bf16[8,512,2048]{2,1,0:T(8,128)(2,1)}, bf16[16,64,2048]{2,1,0:...) custom-call(bf16[8,128,2048]{2,1,0:T(8,128)(2,1)} %get-tuple-element, ...), custom_call_target="tpu_custom_call" | custom-call | flops 103079215104 | bytes 167772160 | tf_op jit(solution)/shard_map/backward_pass/pallas_call | solution.py:1093
  625.9 0.1 collective-permute-start
  626.0 0.1 pad.20.clone
  626.0 0.0 copy-done.2
  626.0 0.0 copy-done.4
  626.0 0.1 maximum_maximum_fusion
  626.1 0.1 pad.17.clone
  626.2 0.0 copy-done.10
  626.2 0.1 maximum_maximum_fusion.1
  626.3 0.7 reduce.4
  627.0 0.7 pad_maximum_fusion.1
  627.7 0.0 collective-permute-done
  627.7 0.8 slice_add_fusion
  628.5 0.7 collective-permute-start.1
  629.3 0.7 select_maximum_fusion
  630.0 7.5 copy.59
  637.4 0.6 broadcast_in_dim.39.gains
  638.1 0.6 broadcast_in_dim.40.biases
  638.7 2.2 copy.49.sums
  640.9 1.0 slice.79
  641.8 0.0 collective-permute-done.1
  641.9 0.3 scatter.9.small
  642.2 0.0 copy-start.5
  642.2 0.6 copy-done.5
  642.8 583.7 %reduce_gradients.1 = (bf16[6144,2048]{1,0:T(8,128)(2,1)}, f32[8,2048]{1,0:T(8,128)}, bf16[64,2048]{1,0:T(8,128)(2,1)}, bf16[6144,2048]{1,0:T(8,128)(2,1)}, bf16[6144,2048]{1,0:T(8,128)(2,1)}) custom-call(bf16[8,512,2048]{2,1,0:T(8,128)(2,1)} %get-tuple-element.76.act, bf16[8,512,512]{2,1,0:T(8,128)(2,1)} %get-tuple-element.71.ctx_all.ctx, ...), custom_call_target="tpu_custom_call" | custom-call | flops 103079215104 | bytes 100663296 | tf_op jit(solution)/shard_map/reduce_gradients/pallas_call | solution.py:1460
  1226.5 1.7 fusion
  1228.2 0.9 slice_bitcast_fusion
  1229.0 10.3 turned_heads.1
  1239.3 1.7 slice.86
  1241.1 10.6 turned.1
  1251.7 0.6 slice.91
  1252.3 11.7 bitcast_convert_fusion
  1264.0 0.8 bitcast_dynamic-update-slice_fusion
  1264.9 9.5 copy.58
  1274.3 0.6 reshape.107
  1274.9 2.5 convert.6
  1277.5 0.0 copy-done.6
  1277.5 0.6 copy.65
  (12 shorter events, 0.1 us)
Async XLA Ops:
  0.7 7.0 copy-start.13
  0.7 7.5 copy-start.1
  0.7 7.5 copy-start.3
  0.7 7.6 copy-start.7
  0.7 7.5 copy-start.9
  0.7 9.5 copy-start.11
  0.7 9.5 copy-start.12
  257.6 368.5 %copy-start.2 = (f32[1,2048]{1,0:T(1,128)S(1)}, f32[1,2048]{1,0:T(1,128)}, u32[]{:S(2)}) copy-start(f32[1,2048]{1,0:T(1,128)} %param.29) | copy-start | bytes 24580
  257.6 368.5 %copy-start.4 = (f32[1,2048]{1,0:T(1,128)S(1)}, f32[1,2048]{1,0:T(1,128)}, u32[]{:S(2)}) copy-start(f32[1,2048]{1,0:T(1,128)} %param.27) | copy-start | bytes 24580
  257.6 368.6 %copy-start.8 = (f32[1,2048]{1,0:T(1,128)S(1)}, f32[1,2048]{1,0:T(1,128)}, u32[]{:S(2)}) copy-start(f32[1,2048]{1,0:T(1,128)} %param.30) | copy-start | bytes 24580
  257.6 368.6 %copy-start.10 = (f32[1,2048]{1,0:T(1,128)S(1)}, f32[1,2048]{1,0:T(1,128)}, u32[]{:S(2)}) copy-start(f32[1,2048]{1,0:T(1,128)} %param.28) | copy-start | bytes 24580
  625.9 1.8 collective-permute-start
  628.5 13.3 %collective-permute-start.1 = (f32[5,2048]{1,0:T(8,128)S(1)}, f32[5,2048]{1,0:T(8,128)S(1)}, u32[]{:S(2)}, u32[]{:S(2)}) collective-permute-start(f32[5,2048]{1,0:T(8,128)S(1)} %slice_add_fusion), channel_id=1, source_target_pairs={{0,8},{4,12},{8,0},{12,4},{1,9},{5,13},{9,1},{13,5},{2,10},{6,14},... | collective-permute-start | bytes 122888 | tf_op jit(solution)/shard_map/ppermute | solution.py:1632
  642.2 0.6 copy-start.5
  1228.2 49.3 %copy-start.6 = (f32[1,2048]{1,0:T(1,128)}, f32[1,2048]{1,0:T(1,128)S(1)}, u32[]{:S(2)}) copy-start(f32[1,2048]{1,0:T(1,128)S(1)} %get-tuple-element.126) | copy-start | bytes 24580
  1252.3 11.7 copy-start

commit v8 on v7

--- a/solution.py
+++ b/solution.py
@@ -1372,11 +1372,11 @@
                 announce(index, True).start()
             out_copy(index).start()
 
+    each_source(0, lambda copy: copy.start())
     rhs_copy(0).start()
-    each_source(0, lambda copy: copy.start())
-    rhs_copy(1).start()
     take(0)
     rhs_copy(0).wait()
+    rhs_copy(1).start()
 
     @pl.loop(0, per_chunk)
     def _(part):

time: 1290 us -> 1290 us (level)
  no operation moved by 1% of the time
where the time goes in v8:
time: 1290 us; the launch traced here: 1280 us
  Pallas kernels  1210 us (94%)
  local copies, waits for them, and re-layouts  44.5 us (3%)
  other arithmetic  18.9 us (1%)
    pallas_call x1, Pallas kernels, reduce_gradients(): pl.pallas_call(partial(reduce_kernel, plan), out_shape=[result, jax.Shape...  583 us
    pallas_call x1, Pallas kernels, backward_pass(): pl.pallas_call(partial(backward_kernel, (tasks, chips, rows, heads)), out...  368 us
    pallas_call x1, Pallas kernels, forward_pass(): pl.pallas_call(partial(forward_kernel, (tasks, chips, rows, heads)), out_...  240 us
  transfers between devices with their start and end apart: 2, of which 0 were waited for; matrix products, arithmetic and copies ran while one was open for 1% of the time, Pallas kernels for 0%

profile of v8, /device:TPU:0, one launch (start us, length us, event | category | flops | bytes accessed | tf_op | source)
XLA Modules:
  0.0 1277.9 jit_solution(7112570735054052003)
XLA Ops:
  0.7 0.0 copy-start.13
  0.7 0.0 copy-start.1
  0.7 0.0 copy-start.3
  0.7 0.0 copy-start.7
  0.7 0.0 copy-start.9
  0.7 0.0 copy-start.11
  0.7 0.0 copy-start.12
  0.7 6.9 copy.53
  7.6 0.0 copy-done.13
  7.6 0.6 copy.54
  8.2 0.0 copy-done.1
  8.2 0.0 copy-done.3
  8.2 0.0 copy-done.7
  8.2 0.0 copy-done.9
  8.3 1.3 copy.47.norms
  9.6 0.6 broadcast_in_dim.37.gains
  10.3 0.0 copy-done.11
  10.3 0.0 copy-done.12
  10.3 0.6 add.20.out_bias
  10.9 6.5 conditional.1
  10.9 6.5 copy.52
  17.4 240.2 %forward_pass.1 = (bf16[8,512,2048]{2,1,0:T(8,128)(2,1)}, bf16[8,512,1536]{2,1,0:T(8,128)(2,1)}, bf16[8,512,2048]{2,1,0:T(8,128)(2,1)}, bf16[8,512,2048]{2,1,0:T...) custom-call(bf16[4,4,64,2048]{3,2,1,0:T(8,128)(2,1)} %get-tuple-elem, ...), custom_call_target="tpu_custom_call" | custom-call | flops 103079215104 | bytes 134217728 | tf_op jit(solution)/shard_map/forward_pass/pallas_call | solution.py:698
  257.6 0.0 copy-start.2
  257.6 0.0 copy-start.4
  257.6 0.0 copy-start.8
  257.6 0.0 copy-start.10
  257.6 368.3 %backward_pass.1 = (bf16[8,512,2048]{2,1,0:T(8,128)(2,1)}, bf16[8,512,1536]{2,1,0:T(8,128)(2,1)}, bf16[8,512,2048]{2,1,0:T(8,128)(2,1)}, bf16[16,64,2048]{2,1,0:...) custom-call(bf16[8,128,2048]{2,1,0:T(8,128)(2,1)} %get-tuple-element, ...), custom_call_target="tpu_custom_call" | custom-call | flops 103079215104 | bytes 167772160 | tf_op jit(solution)/shard_map/backward_pass/pallas_call | solution.py:1093
  625.9 0.1 collective-permute-start
  626.0 0.1 pad.20.clone
  626.0 0.0 copy-done.4
  626.0 0.1 maximum_maximum_fusion
  626.1 0.1 pad.17.clone
  626.2 0.0 copy-done.10
  626.2 0.1 maximum_maximum_fusion.1
  626.3 0.7 reduce.4
  627.0 0.7 pad_maximum_fusion.1
  627.7 0.0 collective-permute-done
  627.7 0.8 slice_add_fusion
  628.5 0.7 collective-permute-start.1
  629.3 0.7 select_maximum_fusion
  630.0 7.5 copy.59
  637.4 0.6 broadcast_in_dim.39.gains
  638.1 0.6 broadcast_in_dim.40.biases
  638.7 2.2 copy.49.sums
  640.9 1.0 slice.79
  641.8 0.0 collective-permute-done.1
  641.9 0.3 scatter.9.small
  642.2 0.0 copy-start.5
  642.2 0.6 copy-done.5
  642.8 583.1 %reduce_gradients.1 = (bf16[6144,2048]{1,0:T(8,128)(2,1)}, f32[8,2048]{1,0:T(8,128)}, bf16[64,2048]{1,0:T(8,128)(2,1)}, bf16[6144,2048]{1,0:T(8,128)(2,1)}, bf16[6144,2048]{1,0:T(8,128)(2,1)}) custom-call(bf16[8,512,2048]{2,1,0:T(8,128)(2,1)} %get-tuple-element.76.act, bf16[8,512,512]{2,1,0:T(8,128)(2,1)} %get-tuple-element.71.ctx_all.ctx, ...), custom_call_target="tpu_custom_call" | custom-call | flops 103079215104 | bytes 100663296 | tf_op jit(solution)/shard_map/reduce_gradients/pallas_call | solution.py:1460
  1226.0 1.7 fusion
  1227.6 0.9 slice_bitcast_fusion
  1228.5 10.3 turned_heads.1
  1238.7 1.7 slice.86
  1240.5 10.6 turned.1
  1251.2 0.6 slice.91
  1251.8 11.7 bitcast_convert_fusion
  1263.5 0.0 copy-done
  1263.5 0.8 bitcast_dynamic-update-slice_fusion
  1264.3 9.5 copy.58
  1273.8 0.6 reshape.107
  1274.4 2.5 convert.6
  1276.9 0.0 copy-done.6
  1276.9 0.6 copy.65
  (12 shorter events, 0.1 us)
Async XLA Ops:
  0.7 7.0 copy-start.13
  0.7 7.5 copy-start.1
  0.7 7.5 copy-start.3
  0.7 7.6 copy-start.7
  0.7 7.5 copy-start.9
  0.7 9.5 copy-start.11
  0.7 9.5 copy-start.12
  257.6 368.5 %copy-start.2 = (f32[1,2048]{1,0:T(1,128)S(1)}, f32[1,2048]{1,0:T(1,128)}, u32[]{:S(2)}) copy-start(f32[1,2048]{1,0:T(1,128)} %param.29) | copy-start | bytes 24580
  257.6 368.5 %copy-start.4 = (f32[1,2048]{1,0:T(1,128)S(1)}, f32[1,2048]{1,0:T(1,128)}, u32[]{:S(2)}) copy-start(f32[1,2048]{1,0:T(1,128)} %param.27) | copy-start | bytes 24580
  257.6 368.6 %copy-start.8 = (f32[1,2048]{1,0:T(1,128)S(1)}, f32[1,2048]{1,0:T(1,128)}, u32[]{:S(2)}) copy-start(f32[1,2048]{1,0:T(1,128)} %param.30) | copy-start | bytes 24580
  257.6 368.6 %copy-start.10 = (f32[1,2048]{1,0:T(1,128)S(1)}, f32[1,2048]{1,0:T(1,128)}, u32[]{:S(2)}) copy-start(f32[1,2048]{1,0:T(1,128)} %param.28) | copy-start | bytes 24580
  625.9 1.8 collective-permute-start
  628.5 13.3 %collective-permute-start.1 = (f32[5,2048]{1,0:T(8,128)S(1)}, f32[5,2048]{1,0:T(8,128)S(1)}, u32[]{:S(2)}, u32[]{:S(2)}) collective-permute-start(f32[5,2048]{1,0:T(8,128)S(1)} %slice_add_fusion), channel_id=1, source_target_pairs={{0,8},{4,12},{8,0},{12,4},{1,9},{5,13},{9,1},{13,5},{2,10},{6,14},... | collective-permute-start | bytes 122888 | tf_op jit(solution)/shard_map/ppermute | solution.py:1632
  642.2 0.6 copy-start.5
  1227.6 49.3 %copy-start.6 = (f32[1,2048]{1,0:T(1,128)}, f32[1,2048]{1,0:T(1,128)S(1)}, u32[]{:S(2)}) copy-start(f32[1,2048]{1,0:T(1,128)S(1)} %get-tuple-element.126) | copy-start | bytes 24580
  1251.8 11.7 copy-start
